TPU v7x, 32 devices: a whole 2x2x4 slice. The times are simulated.
32 devices in a mesh: seq: 8 (over z, x), head: 4 (over y, core).
Axes of the slice: x: 2, y: 2, z: 4, core: 2. Of those that a mesh axis runs over, the one named last changes fastest.
Arguments:
- latent: float32 [2048, 128], P('seq'), may hold values from -6 to 6
- w_in: bfloat16 [128, 3072], replicated, may hold values from -0.5 to 0.5
- w_query: bfloat16 [3072, 3072], P(None, 'head'), may hold values from -0.109375 to 0.109375
- w_key: bfloat16 [3072, 3072], P(None, 'head'), may hold values from -0.109375 to 0.109375
- w_value: bfloat16 [3072, 3072], P(None, 'head'), may hold values from -0.109375 to 0.109375
- w_attn_out: bfloat16 [3072, 3072], P('head'), may hold values from -0.109375 to 0.109375
- w_up: bfloat16 [3072, 12288], P('seq', 'head'), may hold values from -0.109375 to 0.109375
- w_down: bfloat16 [12288, 3072], P('head', 'seq'), may hold values from -0.0546875 to 0.0546875
- w_final: bfloat16 [3072, 256], replicated, may hold values from -0.109375 to 0.109375
- gain_attn: float32 [3072], replicated, may hold values from 0.5 to 1.5
- gain_mlp: float32 [3072], replicated, may hold values from 0.5 to 1.5
- gain_final: float32 [3072], replicated, may hold values from 0.5 to 1.5
Outputs:
- restored: float32 [2048, 128], P('seq')
All inputs are finite; a program needn't handle non-finite values.
Results may differ from a plain program's by a relative error of at most 0.013.
Values may be sent and summed in bfloat16 or wider, within the bound.
No kernel may reach another device: no remote copies, remote signals or barrier semaphores. Data moves between devices by JAX's collectives and lax.ppermute only.
A program may use at most 192 MiB of HBM per device.

v0:
```python
import jax
import jax.numpy as jnp
from jax import lax
from jax.sharding import PartitionSpec as P

D = 3072
HEAD_DIM = 128
C = 128
ITERS = 2


EPSILON = 1e-05


def passed_along(value, axis, steps):
    count = lax.axis_size(axis)
    leading, last = (max(0, -steps), min(count, count - steps))
    return lax.ppermute(value, axis, [(source, source + steps) for source in range(leading, last)])


def swapped(block, axis, bit):
    count = lax.axis_size(axis)
    route = []
    for low in range(count):
        high = low | 1 << bit
        if high != low and high < count:
            route += [(low, high), (high, low)]
    return lax.ppermute(block, axis, route)


def layer_norm(stream, gain):
    center = stream - jnp.mean(stream, axis=-1, keepdims=True)
    spread = jnp.mean(center * center, axis=-1, keepdims=True)
    return center * lax.rsqrt(spread + EPSILON) * gain


def sinusoid(positions, model_width):
    pair_count = model_width // 2
    frequency = jnp.exp(
        -jnp.log(10000.0) * 2.0 * jnp.arange(pair_count).astype(jnp.float32) / model_width
    )
    angles = positions[:, None] * frequency[None, :]
    return jnp.concatenate([jnp.sin(angles), jnp.cos(angles)], axis=1)


def per_device(
    latent,
    w_in,
    w_query,
    w_key,
    w_value,
    w_attn_out,
    w_up,
    w_down,
    w_final,
    gain_attn,
    gain_mlp,
    gain_final,
):
    seq_count = lax.axis_size("seq")
    my_index = lax.axis_index("seq")
    row_count = latent.shape[0]
    local_heads = w_query.shape[1] // HEAD_DIM
    up_full, down_full = (
        lax.all_gather(w_up, "seq", axis=0, tiled=True),
        lax.all_gather(w_down, "seq", axis=1, tiled=True),
    )
    positions_int = my_index * row_count + jnp.arange(row_count, dtype=jnp.int32)
    embedding = sinusoid(positions_int.astype(jnp.float32), D)
    query_last = jnp.max(positions_int)
    current = latent
    for step_index in range(ITERS):
        stream_in = (
            jnp.dot(current.astype(jnp.bfloat16), w_in, preferred_element_type=jnp.float32)
            + embedding
        )
        normed = layer_norm(stream_in, gain_attn).astype(jnp.bfloat16)
        queries = (
            jnp.dot(normed, w_query, preferred_element_type=jnp.float32) * HEAD_DIM ** (-0.5)
        ).astype(jnp.bfloat16)
        queries = queries.reshape(row_count, local_heads, HEAD_DIM)
        key_rows = jnp.dot(normed, w_key, preferred_element_type=jnp.float32).astype(jnp.bfloat16)
        value_rows = jnp.dot(normed, w_value, preferred_element_type=jnp.float32).astype(
            jnp.bfloat16
        )
        initial = (
            jnp.zeros((local_heads, row_count), jnp.float32),
            jnp.zeros((local_heads, row_count, HEAD_DIM), jnp.float32),
        )
        block_keys = lax.all_gather(key_rows, "seq", axis=0, tiled=True)
        block_values = lax.all_gather(value_rows, "seq", axis=0, tiled=True)
        attend_span_rows = block_keys.shape[0]
        key_positions = jnp.arange(attend_span_rows, dtype=jnp.int32)
        attend_key_positions = key_positions

        def update(state_in):
            scores = jnp.einsum(
                "qhd,khd->hqk",
                queries,
                block_keys.reshape(attend_span_rows, local_heads, HEAD_DIM),
                preferred_element_type=jnp.float32,
            )
            visible = attend_key_positions[None, None, :] <= positions_int[None, :, None]
            weights_now = jnp.where(visible, jnp.exp(jnp.where(visible, scores, 0.0)), 0.0)
            totals_new = jnp.sum(weights_now, axis=-1)
            weighted_new = jnp.einsum(
                "hqk,khd->hqd",
                weights_now.astype(jnp.bfloat16),
                block_values.reshape(attend_span_rows, local_heads, HEAD_DIM),
                preferred_element_type=jnp.float32,
            )
            return (totals_new, weighted_new)

        totals, weighted = lax.cond(
            jnp.min(attend_key_positions) <= query_last, update, lambda state_in: state_in, initial
        )
        attended = (
            (weighted / totals[..., None])
            .transpose(1, 0, 2)
            .reshape(row_count, local_heads * HEAD_DIM)
            .astype(jnp.bfloat16)
        )
        stream_attn = stream_in + lax.psum(
            jnp.dot(attended, w_attn_out, preferred_element_type=jnp.float32).astype(jnp.bfloat16),
            "head",
        ).astype(jnp.float32)
        normed_mlp = layer_norm(stream_attn, gain_mlp).astype(jnp.bfloat16)
        hidden = jax.nn.gelu(
            jnp.dot(normed_mlp, up_full, preferred_element_type=jnp.float32), approximate=True
        ).astype(jnp.bfloat16)
        stream_mlp = stream_attn + lax.psum(
            jnp.dot(hidden, down_full, preferred_element_type=jnp.float32).astype(jnp.bfloat16),
            "head",
        ).astype(jnp.float32)
        final_normed = layer_norm(stream_mlp, gain_final).astype(jnp.bfloat16)
        params_out = jnp.dot(final_normed, w_final, preferred_element_type=jnp.float32)
        from_before = passed_along(params_out[row_count - 1 :], "seq", 1)
        shifted = jnp.concatenate([from_before, params_out[: row_count - 1]], axis=0)
        current = latent * jnp.exp(jnp.tanh(shifted[:, C:])) + shifted[:, :C]
    result = current[::-1]
    for bit_number in range(seq_count.bit_length() - 1):
        result = swapped(result.astype(jnp.bfloat16), "seq", bit_number).astype(result.dtype)
    return result


def solution(mesh):
    in_specs = (
        P("seq", None),
        P(),
        P(None, "head"),
        P(None, "head"),
        P(None, "head"),
        P("head", None),
        P("seq", "head"),
        P("head", "seq"),
        P(),
        P(),
        P(),
        P(),
    )
    out_specs = P("seq", None)
    return jax.shard_map(
        per_device, mesh=mesh, in_specs=in_specs, out_specs=out_specs, check_vma=False
    )
```

profile of v0, /device:TPU:0, one launch (start us, length us, event | category | flops | bytes accessed | tf_op | source)
XLA Modules:
  0.0 1315.7 jit_solution(8858396239224865665)
XLA Ops:
  7.2 5.5 multiply_sine_fusion
  14.4 2.0 copy-done.15
  18.2 2.2 convolution_convert_fusion.7
  20.5 5.0 convolution_convert_fusion.6
  26.2 5.0 fusion.46
  31.2 52.6 %all-gather.7.cloned.1.call-done = bf16[2048,768]{1,0:T(8,128)(2,1)} async-done(((bf16[256,768]{1,0:T(8,128)(2,1)}), bf16[2048,768]{1,0:T(8,128)(2,1)}) %all-gather.7.cloned.1.call-update) | async-done | bytes 3145744 | tf_op jit(solution)/shard_map/all_gather | solution.py:90
  83.8 61.3 %all-gather.9.cloned.1.call-done = bf16[2048,768]{1,0:T(8,128)(2,1)} async-done(((bf16[256,768]{1,0:T(8,128)(2,1)}), bf16[2048,768]{1,0:T(8,128)(2,1)}) %all-gather.9.cloned.1.call-update) | async-done | bytes 3145744 | tf_op jit(solution)/shard_map/all_gather | solution.py:91
  145.1 31.9 %conditional.2 = (f32[6,256]{1,0:T(8,128)S(1)}, f32[6,256,128]{1,2,0:T(8,128)}) conditional(s32[]{:T(128)} %convert_element_type.127, () %tuple.21, (s32[2048]{0:T(1024)S(1)}, s32[256]{0:T(256)S(1)}, bf16[256,768]{1,0:T(8,128)(2,1)}, bf16[2048,768]{1,0:T(8,128)(2,1)}, bf16[2048,768]{1,0:T(8,128)(2,1)}) %tuple.22), branch_computations={%region_3.0_spmd, %region_4.6_spmd} | conditional | flops 1630009856 | bytes 47594512 | solution.py:114
  146.5 1.9 copy.25
  148.4 4.7 copy.26
  153.1 10.0 fusion.1
  163.1 4.7 copy.27
  167.8 9.2 fusion.2
  178.2 4.9 convolution_convert_fusion.3
  184.7 40.0 %all-reduce.5.cloned.1.call-done = bf16[256,3072]{1,0:T(8,128)(2,1)} async-done(((bf16[256,3072]{1,0:T(8,128)(2,1)}), bf16[256,3072]{1,0:T(8,128)(2,1)}) %all-reduce.5.cloned.1.call-update) | async-done | bytes 1572880 | tf_op jit(solution)/shard_map/psum | solution.py:123
  224.7 2.7 fusion.67
  227.5 1.6 copy-done.1
  229.6 359.1 %all-gather.11.cloned.1.call-done = bf16[3072,3072]{1,0:T(8,128)(2,1)} async-done(((bf16[384,3072]{1,0:T(8,128)(2,1)}), bf16[3072,3072]{1,0:T(8,128)(2,1)}) %all-gather.11.cloned.1.call-update) | async-done | bytes 18874384 | tf_op jit(solution)/shard_map/all_gather | solution.py:65
  588.7 11.2 fusion.21
  599.9 352.6 %all-gather.13.cloned.1.call-done = bf16[3072,3072]{1,0:T(8,128)(2,1)} async-done(((bf16[3072,384]{1,0:T(8,128)(2,1)}), bf16[3072,3072]{1,0:T(8,128)(2,1)}) %all-gather.13.cloned.1.call-update) | async-done | bytes 18874384 | tf_op jit(solution)/shard_map/all_gather | solution.py:66
  952.5 10.4 convolution_convert_fusion.2
  963.0 42.9 %all-reduce.7.cloned.1.call-done = bf16[256,3072]{1,0:T(8,128)(2,1)} async-done(((bf16[256,3072]{1,0:T(8,128)(2,1)}), bf16[256,3072]{1,0:T(8,128)(2,1)}) %all-reduce.7.cloned.1.call-update) | async-done | bytes 1572880 | tf_op jit(solution)/shard_map/psum | solution.py:131
  1005.9 2.9 fusion.48
  1011.2 3.4 collective-permute-start
  1019.3 2.2 convolution_convert_fusion.5
  1021.6 4.5 convolution_convert_fusion.4
  1026.2 4.5 fusion.47
  1030.7 52.4 %all-gather.15.cloned.1.call-done = bf16[2048,768]{1,0:T(8,128)(2,1)} async-done(((bf16[256,768]{1,0:T(8,128)(2,1)}), bf16[2048,768]{1,0:T(8,128)(2,1)}) %all-gather.15.cloned.1.call-update) | async-done | bytes 3145744 | tf_op jit(solution)/shard_map/all_gather | solution.py:90
  1083.0 61.3 %all-gather.17.cloned.1.call-done = bf16[2048,768]{1,0:T(8,128)(2,1)} async-done(((bf16[256,768]{1,0:T(8,128)(2,1)}), bf16[2048,768]{1,0:T(8,128)(2,1)}) %all-gather.17.cloned.1.call-update) | async-done | bytes 3145744 | tf_op jit(solution)/shard_map/all_gather | solution.py:91
  1144.3 26.7 %conditional.3 = (f32[6,256]{1,0:T(8,128)S(1)}, f32[6,256,128]{1,2,0:T(8,128)S(1)}) conditional(s32[]{:T(128)} %convert_element_type.127, () %tuple.23, (s32[2048]{0:T(1024)S(1)}, s32[256]{0:T(256)S(1)}, bf16[256,768]{1,0:T(8,128)(2,1)}, bf16[2048,768]{1,0:T(8,128)(2,1)}, bf16[2048,768]{1,0:T(8,128)(2,1)}) %tuple.24), branch_computations={%region_14.15_spmd, %region_15.0_spmd} | conditional | flops 1630009856 | bytes 47594512 | solution.py:114
  1146.0 4.7 copy.30
  1150.8 8.7 fusion.8
  1159.4 4.7 copy.31
  1164.1 6.9 fusion.9
  1171.2 4.9 convolution_convert_fusion.1
  1176.1 41.6 %all-reduce.9.cloned.1.call-done = bf16[256,3072]{1,0:T(8,128)(2,1)} async-done(((bf16[256,3072]{1,0:T(8,128)(2,1)}), bf16[256,3072]{1,0:T(8,128)(2,1)}) %all-reduce.9.cloned.1.call-update) | async-done | bytes 1572880 | tf_op jit(solution)/shard_map/psum | solution.py:123
  1217.7 2.7 fusion.66
  1221.0 10.8 fusion.29
  1233.4 6.2 convolution_convert_fusion
  1239.7 43.1 %all-reduce.11.cloned.1.call-done = bf16[256,3072]{1,0:T(8,128)(2,1)} async-done(((bf16[256,3072]{1,0:T(8,128)(2,1)}), bf16[256,3072]{1,0:T(8,128)(2,1)}) %all-reduce.11.cloned.1.call-update) | async-done | bytes 1572880 | tf_op jit(solution)/shard_map/psum | solution.py:131
  1282.8 2.9 fusion.49
  1288.0 3.4 collective-permute-start.1
  1292.9 2.3 collective-permute-start.2
  1295.2 2.2 collective-permute-done.2
  1297.4 2.9 collective-permute-start.3
  1300.4 2.2 collective-permute-done.3
  1302.6 3.2 collective-permute-start.4
  1305.8 2.2 collective-permute-done.4
  (116 shorter events, 24.0 us)
Async XLA Ops:
  6.5 1003.8 %copy-start = (bf16[3072,256]{1,0:T(8,128)(2,1)S(1)}, bf16[3072,256]{1,0:T(8,128)(2,1)}, u32[]{:S(2)}) copy-start(bf16[3072,256]{1,0:T(8,128)(2,1)} %param.24) | copy-start | bytes 4718596
  6.5 6.2 copy-start.14
  6.5 77.3 %all-gather.7.cloned.1.call-start = ((), (), s32[]{:S(2)}) async-start(), calls=%async_computation | async-start | bytes 3538944 | tf_op jit(solution)/shard_map/all_gather | solution.py:90
  6.6 6.2 copy-start.11
  12.7 1.2 copy-start.9
  12.8 5.5 slice-start.5
  13.9 3.1 copy-start.5
  13.9 2.5 copy-start.15
  13.9 4.3 slice-start.6
  17.0 1.2 copy-start.13
  20.5 124.6 %all-gather.9.cloned.1.call-start = ((), (), s32[]{:S(2)}) async-start(), calls=%async_computation.1 | async-start | bytes 3538944 | tf_op jit(solution)/shard_map/all_gather | solution.py:91
  25.5 199.2 %all-reduce.5.cloned.1.call-start = ((), (), s32[]{:S(2)}) async-start(), calls=%async_computation.2 | async-start | bytes 3145728 | tf_op jit(solution)/shard_map/psum | solution.py:123
  183.1 405.6 %all-gather.11.cloned.1.call-start = ((), (), s32[]{:S(2)}) async-start(), calls=%async_computation.3 | async-start | bytes 21233664 | tf_op jit(solution)/shard_map/all_gather | solution.py:65
  183.7 768.9 %all-gather.13.cloned.1.call-start = ((), (), s32[]{:S(2)}) async-start(), calls=%async_computation.4 | async-start | bytes 21233664 | tf_op jit(solution)/shard_map/all_gather | solution.py:66
  184.3 821.7 %all-reduce.7.cloned.1.call-start = ((), (), s32[]{:S(2)}) async-start(), calls=%async_computation.5 | async-start | bytes 3145728 | tf_op jit(solution)/shard_map/psum | solution.py:131
  227.5 1.6 copy-start.1
  227.5 361.2 %copy-start.17 = (f32[3072]{0:T(1024)S(1)}, f32[3072]{0:T(1024)}, u32[]{:S(2)}) copy-start(f32[3072]{0:T(1024)} %param.26) | copy-start | bytes 36868
  963.0 120.1 %all-gather.15.cloned.1.call-start = ((), (), s32[]{:S(2)}) async-start(), calls=%async_computation.6 | async-start | bytes 3538944 | tf_op jit(solution)/shard_map/all_gather | solution.py:90
  1005.9 3.3 copy-start.2
  1005.9 3.8 copy-start.7
  1008.8 1.5 copy-start.16
  1010.4 5.5 copy-start.10
  1010.4 5.5 copy-start.12
  1011.2 4.7 collective-permute-start
  1015.9 3.3 slice-start.7
  1016.6 1.6 copy-start.6
  1016.6 2.7 slice-start.8
  1021.6 122.8 %all-gather.17.cloned.1.call-start = ((), (), s32[]{:S(2)}) async-start(), calls=%async_computation.7 | async-start | bytes 3538944 | tf_op jit(solution)/shard_map/all_gather | solution.py:91
  1026.1 191.6 %all-reduce.9.cloned.1.call-start = ((), (), s32[]{:S(2)}) async-start(), calls=%async_computation.8 | async-start | bytes 3145728 | tf_op jit(solution)/shard_map/psum | solution.py:123
  1176.1 106.7 %all-reduce.11.cloned.1.call-start = ((), (), s32[]{:S(2)}) async-start(), calls=%async_computation.9 | async-start | bytes 3145728 | tf_op jit(solution)/shard_map/psum | solution.py:131
  1220.5 11.4 copy-start.3
  1220.5 11.4 slice-start
  1221.0 10.9 slice-start.1
  1221.0 10.9 slice-start.2
  1221.0 11.8 slice-start.3
  1221.0 12.4 slice-start.4
  1282.8 3.3 copy-start.4
  1282.8 3.8 copy-start.8
  1288.0 4.7 collective-permute-start.1
  1292.9 4.6 collective-permute-start.2
  1297.4 5.2 collective-permute-start.3
  1302.6 5.4 collective-permute-start.4
Sparse Core Ops, SparseCore 0:
  20.6 63.1 all-gather.6
  86.0 59.0 all-gather.8
  183.2 41.4 all-reduce.4
  226.1 362.4 all-gather.10
  590.1 362.4 all-gather.12
  963.1 42.8 all-reduce.6
  1021.7 61.2 all-gather.14
  1085.2 59.0 all-gather.16
  1176.2 41.4 all-reduce.8
  1239.8 42.8 all-reduce.10
where the time goes:
time: 1320 us
  waiting for transfers between devices  1120 us (85%)
  matrix products  110 us (8%)
  local copies, waits for them, and re-layouts  32.3 us (2%)
  other arithmetic  25.4 us (2%)
  starting transfers between devices  16 us (1%)
  between operations  14.8 us (1%)
    all_gather x1, waiting for transfers between devices, per_device(): lax.all_gather(w_up, 'seq', axis=0, tiled=True)  359 us
    all_gather x1, waiting for transfers between devices, per_device(): lax.all_gather(w_down, 'seq', axis=1, tiled=True)  353 us
    all_gather x2, waiting for transfers between devices, per_device(): block_values = lax.all_gather(value_rows, 'seq', axis=0, tiled=True)  123 us
    all_gather x2, waiting for transfers between devices, per_device(): block_keys = lax.all_gather(key_rows, 'seq', axis=0, tiled=True)  105 us
    psum x2, waiting for transfers between devices, per_device(): lax.psum(jnp.dot(hidden, down_full, preferred_element_type=jnp.float32).a...  86 us
    psum x2, waiting for transfers between devices, per_device(): lax.psum(jnp.dot(attended, w_attn_out, preferred_element_type=jnp.float32...  81.6 us
  transfers between devices with their start and end apart: 15, of which 15 were waited for; matrix products, arithmetic and copies ran while one was open for 3% of the time, Pallas kernels for 0%

commit v1 on v0

v1 whole, which is shorter than its diff:
```python
import functools

import jax
import jax.numpy as jnp
from jax import lax
from jax.experimental import pallas as pl
from jax.experimental.pallas import tpu as pltpu
from jax.sharding import PartitionSpec as P

HEAD_DIM = 128
ITERS = 2
EPSILON = 1e-05
FINE = 64
BF16, F32 = jnp.bfloat16, jnp.float32


def layer_norm(stream, gain):
    center = stream - jnp.mean(stream, axis=-1, keepdims=True)
    spread = jnp.mean(center * center, axis=-1, keepdims=True)
    return center * lax.rsqrt(spread + EPSILON) * gain


class Grid:
    def __init__(self):
        self.ns, self.nh = lax.axis_size("seq"), lax.axis_size("head")
        self.s, self.h = lax.axis_index("seq"), lax.axis_index("head")
        self.outer, self.groups = self.ns // 2, self.nh // 2
        self.z, self.x = self.s // 2, self.s % 2
        self.y, self.c = self.h // 2, self.h % 2
        self.ring = []
        for y in range(self.groups):
            line = [(z, y) for z in range(self.outer)]
            self.ring += line if y % 2 == 0 else line[::-1]
        self.place = {zy: i for i, zy in enumerate(self.ring)}

    def move(self, value, target):
        route = []
        for s in range(self.ns):
            for h in range(self.nh):
                there = target(s, h)
                if there is not None:
                    route.append((s * self.nh + h, there[0] * self.nh + there[1]))
        return lax.ppermute(value, ("seq", "head"), route)

    def ring_step(self, value, step):
        def target(s, h):
            i = self.place[(s // 2, h // 2)]
            z, y = self.ring[(i + step) % len(self.ring)]
            return z * 2 + s % 2, y * 2 + h % 2

        return self.move(value, target)

    def seq_shift(self, value, step):
        return self.move(value, lambda s, h: ((s + step) % self.ns, h))

    def outer_shift(self, value, step):
        return self.move(value, lambda s, h: ((s + 2 * step) % self.ns, h))

    def pair_swap(self, value):
        return self.move(value, lambda s, h: (s ^ 1, h))

    def group_shift(self, value, step):
        return self.move(value, lambda s, h: (s, (h + 2 * step) % self.nh))

    def core_swap(self, value):
        return self.move(value, lambda s, h: (s, h ^ 1))


def in_order(parts, mine):
    count = len(parts)
    twice = jnp.stack(parts + parts[:-1])
    return lax.dynamic_slice_in_dim(twice, (count - mine) % count, count, axis=0)


def gather_rows(grid, own):
    over_seq = [own] + [grid.seq_shift(own, -j) for j in range(1, grid.ns)]
    by_seq = in_order(over_seq, grid.s)
    over_group = [by_seq] + [grid.group_shift(by_seq, -j) for j in range(1, grid.groups)]
    by_group = in_order(over_group, grid.y)
    other = grid.core_swap(by_group)
    by_core = jnp.where(grid.c == 0, jnp.stack([by_group, other]), jnp.stack([other, by_group]))
    return by_core.transpose(2, 1, 0, 3, 4).reshape(-1, own.shape[-1])


def gather_ring(grid, own):
    size = len(grid.ring)
    half, cut = size // 2, own.shape[0] // 2
    pieces = {0: own}
    ahead = back = own
    for j in range(1, half):
        ahead, back = grid.ring_step(ahead, 1), grid.ring_step(back, -1)
        pieces[-j], pieces[j] = ahead, back
    pieces[half] = jnp.concatenate(
        [grid.ring_step(ahead[:cut], 1), grid.ring_step(back[cut:], -1)], axis=0
    )
    return pieces


def reduce_ring(grid, terms):
    size = len(grid.ring)
    half, cut = size // 2, terms[0].shape[0] // 2
    ahead = grid.ring_step(terms[half][:cut], 1)
    back = grid.ring_step(terms[half][cut:], -1)
    for j in range(half - 1, 0, -1):
        if j == half - 1:
            up, down = terms[j].astype(F32), terms[-j].astype(F32)
            up = jnp.concatenate([up[:cut] + ahead.astype(F32), up[cut:]], axis=0)
            down = jnp.concatenate([down[:cut], down[cut:] + back.astype(F32)], axis=0)
        else:
            up = terms[j].astype(F32) + ahead.astype(F32)
            down = terms[-j].astype(F32) + back.astype(F32)
        ahead, back = grid.ring_step(up.astype(BF16), 1), grid.ring_step(down.astype(BF16), -1)
    return terms[0].astype(F32) + ahead.astype(F32) + back.astype(F32)


def reduce_head(grid, term):
    rows, width = term.shape
    blocks = term.reshape(grid.groups, 2, rows // grid.nh, width)
    keep = lax.dynamic_index_in_dim(blocks, grid.c, 1, keepdims=False)
    give = lax.dynamic_index_in_dim(blocks, 1 - grid.c, 1, keepdims=False)
    both = keep.astype(F32) + grid.core_swap(give).astype(F32)
    total = lax.dynamic_index_in_dim(both, grid.y, 0, keepdims=False)
    rounded = both.astype(BF16)
    for j in range(1, grid.groups):
        send = lax.dynamic_index_in_dim(rounded, (grid.y + j) % grid.groups, 0, keepdims=False)
        total = total + grid.group_shift(send, j).astype(F32)
    return total


def spread_weights(grid, w_up, w_down):
    rows, hidden = w_up.shape
    chunk = hidden // grid.outer
    outer, ns = grid.outer, grid.ns
    up_parts, down_parts = [], []
    for kind in range(2):
        for j in range(outer):
            to = (grid.z + j) % outer
            if kind == 0:
                part = lax.dynamic_slice_in_dim(w_up, to * chunk, chunk, axis=1)
            else:
                part = lax.dynamic_slice_in_dim(w_down, to * chunk, chunk, axis=0)
            if j:
                part = grid.outer_shift(part, j)
            other = grid.pair_swap(part)
            source = (grid.z - j) % outer
            (up_parts, down_parts)[kind].append((source * 2 + grid.x, part))
            (up_parts, down_parts)[kind].append((source * 2 + 1 - grid.x, other))
    up = jnp.zeros((rows * ns, chunk), w_up.dtype)
    down = jnp.zeros((chunk, rows * ns), w_down.dtype)
    for place, part in up_parts:
        up = lax.dynamic_update_slice_in_dim(up, part, place * rows, axis=0)
    for place, part in down_parts:
        down = lax.dynamic_update_slice_in_dim(down, part, place * rows, axis=1)
    return up, down


def angle_tables(tokens, width):
    pairs = width // 2
    frequency = jnp.exp(-jnp.log(10000.0) * 2.0 * jnp.arange(pairs).astype(F32) / width)
    coarse = (jnp.arange(tokens // FINE) * FINE).astype(F32)[:, None] * frequency[None, :]
    fine = jnp.arange(FINE).astype(F32)[:, None] * frequency[None, :]
    return jnp.sin(coarse), jnp.cos(coarse), jnp.sin(fine), jnp.cos(fine)


def embed(sin_a, cos_a, sin_b, cos_b):
    return jnp.concatenate([sin_a * cos_b + cos_a * sin_b, cos_a * cos_b - sin_a * sin_b], axis=-1)


def project_kernel(
    scales, cur_ref, w_in_ref, sin_a, cos_a, sin_b, cos_b, gain_ref, *rest
):
    count = len(scales)
    weights, outs, normed = rest[:count], rest[count : 2 * count], rest[2 * count]
    for part in range(cur_ref.shape[0] // FINE):
        rows = pl.ds(part * FINE, FINE)
        stream = jnp.dot(cur_ref[rows, :], w_in_ref[...], preferred_element_type=F32)
        stream = stream + embed(
            sin_a[pl.ds(part, 1), :], cos_a[pl.ds(part, 1), :], sin_b[...], cos_b[...]
        )
        normed[rows, :] = layer_norm(stream, gain_ref[...]).astype(BF16)
    for scale, weight, out in zip(scales, weights, outs):
        value = jnp.dot(normed[...], weight[...], preferred_element_type=F32)
        out[...] = (value * scale if scale != 1.0 else value).astype(BF16)


def project(current, w_in, tables, gain, weights, scales, block):
    tokens, channels = current.shape
    width = w_in.shape[1]
    sin_a, cos_a, sin_b, cos_b = tables
    coarse = block // FINE
    sin_a, cos_a = (t.reshape(tokens // block, coarse, width // 2) for t in (sin_a, cos_a))
    whole = lambda shape: pl.BlockSpec(shape, lambda i: (0,) * len(shape))
    in_specs = [
        pl.BlockSpec((block, channels), lambda i: (i, 0)),
        whole(w_in.shape),
        pl.BlockSpec((None, coarse, width // 2), lambda i: (i, 0, 0)),
        pl.BlockSpec((None, coarse, width // 2), lambda i: (i, 0, 0)),
        whole(sin_b.shape),
        whole(cos_b.shape),
        whole((1, width)),
    ] + [whole(w.shape) for w in weights]
    macs = tokens * width * (channels + sum(w.shape[1] for w in weights))
    return pl.pallas_call(
        functools.partial(project_kernel, scales),
        grid=(tokens // block,),
        in_specs=in_specs,
        out_specs=[pl.BlockSpec((block, w.shape[1]), lambda i: (i, 0)) for w in weights],
        out_shape=[jax.ShapeDtypeStruct((tokens, w.shape[1]), BF16) for w in weights],
        scratch_shapes=[pltpu.VMEM((block, width), BF16)],
        compiler_params=pltpu.CompilerParams(vmem_limit_bytes=56 * 2**20),
        cost_estimate=pl.CostEstimate(
            flops=2 * macs, bytes_accessed=2 * sum(w.size for w in weights), transcendentals=0
        ),
        name="project",
    )(current, w_in, sin_a, cos_a, sin_b, cos_b, gain.reshape(1, width), *weights)


def attend_kernel(block, index_ref, q_ref, k_ref, v_ref, out_ref):
    own = index_ref[0]
    queries = q_ref[...]
    rows = queries.shape[0]

    def visit(j, state, masked):
        totals, weighted = state
        here = pl.ds(pl.multiple_of(j * block, block), block)
        scores = lax.dot_general(
            queries, k_ref[here, :], (((1,), (1,)), ((), ())), preferred_element_type=F32
        )
        if masked:
            query = lax.broadcasted_iota(jnp.int32, scores.shape, 0)
            key = lax.broadcasted_iota(jnp.int32, scores.shape, 1)
            seen = key <= query
            weights = jnp.where(seen, jnp.exp(jnp.where(seen, scores, 0.0)), 0.0)
        else:
            weights = jnp.exp(scores)
        totals = totals + jnp.sum(weights, axis=-1, keepdims=True)
        weighted = weighted + jnp.dot(
            weights.astype(BF16), v_ref[here, :], preferred_element_type=F32
        )
        return totals, weighted

    state = (jnp.zeros((rows, 1), F32), jnp.zeros((rows, v_ref.shape[1]), F32))
    state = lax.fori_loop(0, own, lambda j, st: visit(j, st, False), state)
    totals, weighted = visit(own, state, True)
    out_ref[...] = (weighted / totals).astype(BF16)


def attend(index, queries, keys, values):
    rows, columns = queries.shape
    tokens = keys.shape[0]
    whole = pl.BlockSpec((tokens, HEAD_DIM), lambda i, n: (0, i))
    own = pl.BlockSpec((rows, HEAD_DIM), lambda i, n: (0, i))
    return pl.pallas_call(
        functools.partial(attend_kernel, rows),
        grid_spec=pltpu.PrefetchScalarGridSpec(
            num_scalar_prefetch=1,
            grid=(columns // HEAD_DIM,),
            in_specs=[own, whole, whole],
            out_specs=own,
        ),
        out_shape=jax.ShapeDtypeStruct((rows, columns), BF16),
        compiler_params=pltpu.CompilerParams(vmem_limit_bytes=32 * 2**20),
        cost_estimate=pl.CostEstimate(
            flops=4 * rows * tokens * columns,
            bytes_accessed=4 * tokens * columns,
            transcendentals=rows * tokens * columns // HEAD_DIM,
        ),
        name="attend",
    )(index.reshape(1).astype(jnp.int32), queries, keys, values)


def per_device(
    latent, w_in, w_query, w_key, w_value, w_attn_out, w_up, w_down, w_final,
    gain_attn, gain_mlp, gain_final,
):
    grid = Grid()
    rows, channels = latent.shape
    width = w_in.shape[1]
    sub = rows // grid.nh
    tokens = rows * grid.ns
    tables = angle_tables(tokens, width)
    start = grid.s * rows + grid.h * sub

    latent_own = lax.dynamic_slice_in_dim(latent, grid.h * sub, sub)
    next_row = grid.seq_shift(latent[:1], -1)
    latent_next = lax.dynamic_slice_in_dim(
        jnp.concatenate([latent, next_row]), grid.h * sub + 1, sub
    )
    latent_all = gather_rows(grid, latent_own.astype(BF16))
    up, down = spread_weights(grid, w_up, w_down)

    current = latent_all
    for step_index in range(ITERS):
        keys, values = project(
            current, w_in, tables, gain_attn, (w_key, w_value), (1.0, 1.0), min(256, rows)
        )
        block_rows = lax.dynamic_slice_in_dim(current, grid.s * rows, rows)
        coarse = rows // FINE
        own_tables = tuple(
            lax.dynamic_slice_in_dim(t, grid.s * coarse, coarse) for t in tables[:2]
        ) + tables[2:]
        (queries,) = project(
            block_rows, w_in, own_tables, gain_attn, (w_query,), (HEAD_DIM**-0.5,), rows
        )
        attended = attend(grid.s, queries, keys, values)
        own_rows = lax.dynamic_slice_in_dim(current, start, sub)
        position = (start + jnp.arange(sub)) // FINE
        offset = (start + jnp.arange(sub)) % FINE
        stream_in = jnp.dot(own_rows, w_in, preferred_element_type=F32) + embed(
            *(jnp.take(t, position, axis=0) for t in tables[:2]),
            *(jnp.take(t, offset, axis=0) for t in tables[2:]),
        )
        stream_attn = stream_in + reduce_head(
            grid, jnp.dot(attended, w_attn_out, preferred_element_type=F32).astype(BF16)
        )
        pieces = gather_ring(grid, layer_norm(stream_attn, gain_mlp).astype(BF16))
        order = sorted(pieces)
        mine = jnp.concatenate([pieces[k] for k in order])
        others = jnp.concatenate([grid.core_swap(pieces[k]) for k in order])
        both = jnp.concatenate([mine, others])
        hidden = jax.nn.gelu(
            jnp.dot(both, up, preferred_element_type=F32), approximate=True
        ).astype(BF16)
        terms = jnp.dot(hidden, down, preferred_element_type=F32).astype(BF16)
        from_core = grid.core_swap(terms[mine.shape[0] :])
        summed = (terms[: mine.shape[0]].astype(F32) + from_core.astype(F32)).astype(BF16)
        by_offset = {k: summed[i * sub : (i + 1) * sub] for i, k in enumerate(order)}
        stream_mlp = stream_attn + reduce_ring(grid, by_offset)
        final = layer_norm(stream_mlp, gain_final).astype(BF16)
        params = jnp.dot(final, w_final, preferred_element_type=F32)
        moved = latent_next * jnp.exp(jnp.tanh(params[:, channels:])) + params[:, :channels]
        if step_index < ITERS - 1:
            gathered = gather_rows(grid, moved.astype(BF16))
            current = jnp.concatenate([latent_all[:1], gathered[:-1]])

    mirrored = grid.move(moved, lambda s, h: (grid.ns - 1 - s, h))

    def after(s, h):
        place = s * grid.nh + h + 1
        if place == grid.ns * grid.nh:
            return None
        return grid.ns - 1 - place // grid.nh, place % grid.nh

    first = grid.move(moved[-1:], after)
    is_start = (grid.s == grid.ns - 1) & (grid.h == 0)
    first = jnp.where(is_start, latent_all[:1].astype(F32), first)
    block = jnp.concatenate([first, mirrored[:-1]])
    over_group = [block] + [grid.group_shift(block, -j) for j in range(1, grid.groups)]
    by_group = in_order(over_group, grid.y)
    other = grid.core_swap(by_group)
    by_core = jnp.where(
        grid.c == 0, jnp.stack([by_group, other], 1), jnp.stack([other, by_group], 1)
    )
    return by_core.reshape(rows, channels)[::-1]


def solution(mesh):
    in_specs = (
        P("seq", None),
        P(),
        P(None, "head"),
        P(None, "head"),
        P(None, "head"),
        P("head", None),
        P("seq", "head"),
        P("head", "seq"),
        P(),
        P(),
        P(),
        P(),
    )
    return jax.shard_map(
        per_device, mesh=mesh, in_specs=in_specs, out_specs=P("seq", None), check_vma=False
    )
```

time: 1320 us -> 575 us (0.44)
  waiting for transfers between devices: 1120 us -> 177 us
  starting transfers between devices: 16 us -> 162 us
  Pallas kernels: 0 us -> 95.5 us
  matrix products: 110 us -> 48.6 us
  local copies, waits for them, and re-layouts: 32.3 us -> 64.5 us
  between operations: 14.8 us -> 1.47 us
    all_gather x6 -> x0, waiting for transfers between devices: 939 us -> none  [the longest x1 359 us: per_device(): lax.all_gather(w_up, 'seq', axis=0, tiled=True)]
    ppermute x5 -> x91, waiting for transfers between devices: 9.29 us -> 177 us  [move(): return lax.ppermute(value, ('seq', 'head'), route)]
    psum x4 -> x0, waiting for transfers between devices: 168 us -> none  [the longest x2 86 us: per_device(): lax.psum(jnp.dot(hidden, down_full, preferred_element_type=jnp.float32).a...]
    ppermute x5 -> x91, starting transfers between devices: 15.2 us -> 162 us  [move(): return lax.ppermute(value, ('seq', 'head'), route)]
    pallas_call x0 -> x6, Pallas kernels: none -> 95.5 us  [the longest x4 88.5 us: project(): pl.pallas_call(functools.partial(project_kernel, scales), grid=(tokens //...]
    dot_general x18 -> x8, matrix products: 93.5 us -> 48.6 us  [the longest x2 38.9 us: per_device(): terms = jnp.dot(hidden, down, preferred_element_type=F32).astype(BF16)]
    unnamed x54 -> x103, local copies, waits for them, and re-layouts: 10.2 us -> 33 us
    another operation x6 -> x4, local copies, waits for them, and re-layouts: 21.9 us -> 0.05 us  [in_order(): twice = jnp.stack(parts + parts[:-1])]
  transfers between devices with their start and end apart: 15 -> 91, of which waited for: 15 -> 44; matrix products, arithmetic and copies ran while one was open for 3% -> 12% of each run, Pallas kernels for 0% -> 8%
where the time goes in v1:
time: 575 us; the launch traced here: 572 us
  waiting for transfers between devices  177 us (31%)
  starting transfers between devices  162 us (28%)
  Pallas kernels  95.5 us (17%)
  local copies, waits for them, and re-layouts  64.5 us (11%)
  matrix products  48.6 us (8%)
  other arithmetic  22.1 us (4%)
    ppermute x91, waiting for transfers between devices, move(): return lax.ppermute(value, ('seq', 'head'), route)  177 us
    ppermute x91, starting transfers between devices, move(): return lax.ppermute(value, ('seq', 'head'), route)  162 us
    pallas_call x4, Pallas kernels, project(): pl.pallas_call(functools.partial(project_kernel, scales), grid=(tokens //...  88.5 us
    dot_general x2, matrix products, per_device(): terms = jnp.dot(hidden, down, preferred_element_type=F32).astype(BF16)  38.9 us
    unnamed x103, local copies, waits for them, and re-layouts  33 us
  transfers between devices with their start and end apart: 91, of which 44 were waited for; matrix products, arithmetic and copies ran while one was open for 12% of the time, Pallas kernels for 8%

profile of v1, /device:TPU:0, one launch (start us, length us, event | category | flops | bytes accessed | tf_op | source)
XLA Modules:
  0.0 571.6 jit_solution(3595463551303148996)
XLA Ops:
  0.9 6.0 %collective-permute-start = (bf16[64,128]{1,0:T(8,128)(2,1)S(1)}, bf16[64,128]{1,0:T(8,128)(2,1)S(1)}, u32[]{:S(2)}, u32[]{:S(2)}) collective-permute-start(bf16[64,128]{1,0:T(8,128)(2,1)S(1)} %get-tuple-element.28), channel_id=1, source_target_pairs={{0,28},{1,29},{2,30},{3,31},{4,0},{5,1},{6,2},{7,3},{8,4},{9,5},{1... | collective-permute-start | bytes 49160 | tf_op jit(solution)/shard_map/ppermute | solution.py:43
  37.6 6.5 %project.4.q_ref = bf16[256,768]{1,0:T(8,128)(2,1)} custom-call(bf16[256,128]{1,0:T(8,128)(2,1)} %constant_dynamic-slice_fusion.9.cur_ref, bf16[128,3072]{1,0:T(8,128)(2,1)} %w_in_ref.7, f32[1,4,1536]{2,1,0:T(4,128)} %get-tuple-element.70.sin_a, f32[1,4,1536]{2,1,0:T(4,128)} %get-tuple-element.69.cos_a, f32[64,1536]{1,0:T(8,128)} %get-tuple-element.62.sin_b, ...), custom_call_target="tpu_custom_call" | custom-call | flops 1409286144 | bytes 4718592 | tf_op jit(solution)/shard_map/project/pallas_call | solution.py:203
  44.1 37.8 %project.5 = (bf16[2048,768]{1,0:T(8,128)(2,1)}, bf16[2048,768]{1,0:T(8,128)(2,1)}) custom-call(bf16[2048,128]{1,0:T(8,128)(2,1)} %bitcast.146, bf16[128,3072]{1,0:T(8,128)(2,1)} %w_in_ref.7, f32[8,4,1536]{2,1,0:T(4,128)} %get-tuple-element.58.sin_a, f32[8,4,1536]{2,1,0:T(4,128)} %get-tuple-element.57.cos_a, f32[64,1536]{1,0:T(8,128)} %get-tuple-element.62.sin_b, ...), custom_call_target="tpu_custom_call" | custom-call | flops 20937965568 | bytes 9437184 | tf_op jit(solution)/shard_map/project/pallas_call | solution.py:203
  85.7 3.5 attend.2
  89.2 3.8 convolution_convert_fusion.3
  110.4 3.9 collective-permute-start.29
  116.4 10.6 %collective-permute-start.31 = (bf16[384,768]{1,0:T(8,128)(2,1)S(1)}, bf16[384,768]{1,0:T(8,128)(2,1)S(1)}, u32[]{:S(2)}, u32[]{:S(2)}) collective-permute-start(bf16[384,768]{1,0:T(8,128)(2,1)S(1)} %get-tuple-element.49), channel_id=1, source_target_pairs={{0,16},{1,17},{2,18},{3,19},{4,20},{5,21},{6,22},{7,23},{8,24},{9,... | collective-permute-start | bytes 1769480 | tf_op jit(solution)/shard_map/ppermute | solution.py:43
  128.6 10.1 %collective-permute-done.29 = bf16[384,768]{1,0:T(8,128)(2,1)S(1)} collective-permute-done((bf16[384,768]{1,0:T(8,128)(2,1)S(1)}, bf16[384,768]{1,0:T(8,128)(2,1)S(1)}, u32[]{:S(2)}, u32[]{:S(2)}) %collective-permute-start.29) | collective-permute-done | bytes 589856 | tf_op jit(solution)/shard_map/ppermute | solution.py:43
  140.2 19.1 %collective-permute-start.12 = (bf16[64,3072]{1,0:T(8,128)(2,1)S(1)}, bf16[64,3072]{1,0:T(8,128)(2,1)S(1)}, u32[]{:S(2)}, u32[]{:S(2)}) collective-permute-start(bf16[64,3072]{1,0:T(8,128)(2,1)S(1)} %multiply_convert_fusion.3), channel_id=1, source_target_pairs={{0,8},{1,9},{2,0},{3,1},{4,12},{5,13},{6,4},{7,5},{8,16},{9,17},{1... | collective-permute-start | bytes 1179656 | tf_op jit(solution)/shard_map/ppermute | solution.py:43
  166.2 12.7 %collective-permute-start.13 = (bf16[64,3072]{1,0:T(8,128)(2,1)S(1)}, bf16[64,3072]{1,0:T(8,128)(2,1)S(1)}, u32[]{:S(2)}, u32[]{:S(2)}) collective-permute-start(bf16[64,3072]{1,0:T(8,128)(2,1)S(1)} %collective-permute-done.12), channel_id=1, source_target_pairs={{0,8},{1,9},{2,0},{3,1},{4,12},{5,13},{6,4},{7,5},{8,16},{9,17},{1... | collective-permute-start | bytes 1179656 | tf_op jit(solution)/shard_map/ppermute | solution.py:43
  184.1 5.8 %collective-permute-start.16 = (bf16[64,3072]{1,0:T(8,128)(2,1)S(1)}, bf16[64,3072]{1,0:T(8,128)(2,1)S(1)}, u32[]{:S(2)}, u32[]{:S(2)}) collective-permute-start(bf16[64,3072]{1,0:T(8,128)(2,1)S(1)} %collective-permute-done.15), channel_id=1, source_target_pairs={{0,2},{1,3},{2,10},{3,11},{4,6},{5,7},{6,14},{7,15},{8,0},{9,1},{1... | collective-permute-start | bytes 1179656 | tf_op jit(solution)/shard_map/ppermute | solution.py:43
  189.9 4.1 collective-permute-done.13
  194.1 7.1 %collective-permute-done.41 = bf16[768,384]{1,0:T(8,128)(2,1)S(1)} collective-permute-done((bf16[768,384]{1,0:T(8,128)(2,1)}, bf16[768,384]{1,0:T(8,128)(2,1)S(1)}, u32[]{:S(2)}, u32[]{:S(2)}) %collective-permute-start.41) | collective-permute-done | bytes 589856 | tf_op jit(solution)/shard_map/ppermute | solution.py:43
  202.1 8.5 %collective-permute-done.34 = bf16[384,768]{1,0:T(8,128)(2,1)S(1)} collective-permute-done((bf16[384,768]{1,0:T(8,128)(2,1)S(1)}, bf16[384,768]{1,0:T(8,128)(2,1)S(1)}, u32[]{:S(2)}, u32[]{:S(2)}) %collective-permute-start.34) | collective-permute-done | bytes 589856 | tf_op jit(solution)/shard_map/ppermute | solution.py:43
  213.6 9.6 %collective-permute-start.18 = (bf16[32,3072]{1,0:T(8,128)(2,1)S(1)}, bf16[32,3072]{1,0:T(8,128)(2,1)S(1)}, u32[]{:S(2)}, u32[]{:S(2)}) collective-permute-start(bf16[32,3072]{1,0:T(8,128)(2,1)S(1)} %slice.204), channel_id=1, source_target_pairs={{0,8},{1,9},{2,0},{3,1},{4,12},{5,13},{6,4},{7,5},{8,16},{9,17},{1... | collective-permute-start | bytes 589832 | tf_op jit(solution)/shard_map/ppermute | solution.py:43
  226.5 6.4 %collective-permute-done.17 = bf16[64,3072]{1,0:T(8,128)(2,1)S(1)} collective-permute-done((bf16[64,3072]{1,0:T(8,128)(2,1)S(1)}, bf16[64,3072]{1,0:T(8,128)(2,1)S(1)}, u32[]{:S(2)}, u32[]{:S(2)}) %collective-permute-start.17) | collective-permute-done | bytes 393248 | tf_op jit(solution)/shard_map/ppermute | solution.py:43
  235.3 5.0 collective-permute-done.19
  249.1 19.5 %convolution_convert_fusion.1 = bf16[1024,3072]{1,0:T(8,128)(2,1)} fusion(bf16[768,3072]{1,0:T(8,128)(2,1)} %constant_dynamic-update-slice_fusion.64, bf16[1024,3072]{1,0:T(8,128)(2,1)} %constant_dynamic-update-slice_fusion.15, bf16[3072,768]{1,0:T(8,128)(2,1)} %copy-done.14), kind=kOutput, calls=%fused_computation.7 | convolution fusion | flops 9673900032 | bytes 22020096 | tf_op jit(solution)/shard_map/dot_general | solution.py:324
  271.2 5.4 collective-permute-done.42
  279.9 5.1 collective-permute-done.43
  288.8 8.1 %collective-permute-done.44 = bf16[64,3072]{1,0:T(8,128)(2,1)S(1)} collective-permute-done((bf16[64,3072]{1,0:T(8,128)(2,1)S(1)}, bf16[64,3072]{1,0:T(8,128)(2,1)S(1)}, u32[]{:S(2)}, u32[]{:S(2)}) %collective-permute-start.44) | collective-permute-done | bytes 393248 | tf_op jit(solution)/shard_map/ppermute | solution.py:43
  298.6 7.7 %collective-permute-done.45 = bf16[64,3072]{1,0:T(8,128)(2,1)S(1)} collective-permute-done((bf16[64,3072]{1,0:T(8,128)(2,1)S(1)}, bf16[64,3072]{1,0:T(8,128)(2,1)S(1)}, u32[]{:S(2)}, u32[]{:S(2)}) %collective-permute-start.45) | collective-permute-done | bytes 393248 | tf_op jit(solution)/shard_map/ppermute | solution.py:43
  309.2 6.3 %collective-permute-done.49 = bf16[64,3072]{1,0:T(8,128)(2,1)S(1)} collective-permute-done((bf16[64,3072]{1,0:T(8,128)(2,1)S(1)}, bf16[64,3072]{1,0:T(8,128)(2,1)S(1)}, u32[]{:S(2)}, u32[]{:S(2)}) %collective-permute-start.49) | collective-permute-done | bytes 393248 | tf_op jit(solution)/shard_map/ppermute | solution.py:43
  316.6 3.8 collective-permute-start.9
  320.4 4.0 collective-permute-done.50
  339.2 3.0 collective-permute-done.57
  343.9 3.4 collective-permute-done.58
  350.9 6.5 %project.6.q_ref = bf16[256,768]{1,0:T(8,128)(2,1)} custom-call(bf16[256,128]{1,0:T(8,128)(2,1)} %fusion.44.cur_ref, bf16[128,3072]{1,0:T(8,128)(2,1)} %w_in_ref.7, f32[1,4,1536]{2,1,0:T(4,128)} %get-tuple-element.70.sin_a, f32[1,4,1536]{2,1,0:T(4,128)} %get-tuple-element.69.cos_a, f32[64,1536]{1,0:T(8,128)} %get-tuple-element.62.sin_b, ...), custom_call_target="tpu_custom_call" | custom-call | flops 1409286144 | bytes 4718592 | tf_op jit(solution)/shard_map/project/pallas_call | solution.py:203
  357.4 37.7 %project.7 = (bf16[2048,768]{1,0:T(8,128)(2,1)}, bf16[2048,768]{1,0:T(8,128)(2,1)}) custom-call(bf16[2048,128]{1,0:T(8,128)(2,1)} %pad_maximum_fusion.cur_ref, bf16[128,3072]{1,0:T(8,128)(2,1)} %w_in_ref.7, f32[8,4,1536]{2,1,0:T(4,128)} %get-tuple-element.58.sin_a, f32[8,4,1536]{2,1,0:T(4,128)} %get-tuple-element.57.cos_a, ...), custom_call_target="tpu_custom_call" | custom-call | flops 20937965568 | bytes 9437184 | tf_op jit(solution)/shard_map/project/pallas_call | solution.py:203
  398.9 3.5 attend.3
  402.4 3.7 convolution_convert_fusion.2
  410.7 9.4 %collective-permute-done.61 = bf16[64,3072]{1,0:T(8,128)(2,1)S(1)} collective-permute-done((bf16[64,3072]{1,0:T(8,128)(2,1)S(1)}, bf16[64,3072]{1,0:T(8,128)(2,1)S(1)}, u32[]{:S(2)}, u32[]{:S(2)}) %collective-permute-start.61) | collective-permute-done | bytes 393248 | tf_op jit(solution)/shard_map/ppermute | solution.py:43
  420.7 3.9 collective-permute-start.62
  424.6 7.9 %collective-permute-done.62 = bf16[64,3072]{1,0:T(8,128)(2,1)S(1)} collective-permute-done((bf16[64,3072]{1,0:T(8,128)(2,1)S(1)}, bf16[64,3072]{1,0:T(8,128)(2,1)S(1)}, u32[]{:S(2)}, u32[]{:S(2)}) %collective-permute-start.62) | collective-permute-done | bytes 393248 | tf_op jit(solution)/shard_map/ppermute | solution.py:43
  432.5 5.4 collective-permute-start.63
  438.3 6.5 %collective-permute-done.63 = bf16[64,3072]{1,0:T(8,128)(2,1)S(1)} collective-permute-done((bf16[64,3072]{1,0:T(8,128)(2,1)S(1)}, bf16[64,3072]{1,0:T(8,128)(2,1)S(1)}, u32[]{:S(2)}, u32[]{:S(2)}) %collective-permute-start.63) | collective-permute-done | bytes 393248 | tf_op jit(solution)/shard_map/ppermute | solution.py:43
  444.8 4.4 collective-permute-start.64
  450.4 5.3 collective-permute-done.64
  465.4 4.1 collective-permute-done.69
  478.2 19.4 %convolution_convert_fusion = bf16[1024,3072]{1,0:T(8,128)(2,1)} fusion(bf16[768,3072]{1,0:T(8,128)(2,1)} %constant_dynamic-update-slice_fusion.64, bf16[1024,3072]{1,0:T(8,128)(2,1)} %constant_dynamic-update-slice_fusion.47, bf16[3072,768]{1,0:T(8,128)(2,1)} %copy-done.14), kind=kOutput, calls=%fused_computation.6 | convolution fusion | flops 9673900032 | bytes 22020096 | tf_op jit(solution)/shard_map/dot_general | solution.py:324
  500.2 5.4 collective-permute-done.78
  508.9 5.1 collective-permute-done.79
  517.7 8.1 %collective-permute-done.80 = bf16[64,3072]{1,0:T(8,128)(2,1)S(1)} collective-permute-done((bf16[64,3072]{1,0:T(8,128)(2,1)S(1)}, bf16[64,3072]{1,0:T(8,128)(2,1)S(1)}, u32[]{:S(2)}, u32[]{:S(2)}) %collective-permute-start.80) | collective-permute-done | bytes 393248 | tf_op jit(solution)/shard_map/ppermute | solution.py:43
  527.5 7.7 %collective-permute-done.81 = bf16[64,3072]{1,0:T(8,128)(2,1)S(1)} collective-permute-done((bf16[64,3072]{1,0:T(8,128)(2,1)S(1)}, bf16[64,3072]{1,0:T(8,128)(2,1)S(1)}, u32[]{:S(2)}, u32[]{:S(2)}) %collective-permute-start.81) | collective-permute-done | bytes 393248 | tf_op jit(solution)/shard_map/ppermute | solution.py:43
  537.5 7.1 %collective-permute-done.85 = bf16[64,3072]{1,0:T(8,128)(2,1)S(1)} collective-permute-done((bf16[64,3072]{1,0:T(8,128)(2,1)S(1)}, bf16[64,3072]{1,0:T(8,128)(2,1)S(1)}, u32[]{:S(2)}, u32[]{:S(2)}) %collective-permute-start.85) | collective-permute-done | bytes 393248 | tf_op jit(solution)/shard_map/ppermute | solution.py:43
  545.1 7.5 %collective-permute-done.86 = bf16[64,3072]{1,0:T(8,128)(2,1)S(1)} collective-permute-done((bf16[64,3072]{1,0:T(8,128)(2,1)S(1)}, bf16[64,3072]{1,0:T(8,128)(2,1)S(1)}, u32[]{:S(2)}, u32[]{:S(2)}) %collective-permute-start.86) | collective-permute-done | bytes 393248 | tf_op jit(solution)/shard_map/ppermute | solution.py:43
  555.7 4.5 collective-permute-start.88
  566.4 3.2 collective-permute-start.90
  (367 shorter events, 177.5 us)
Async XLA Ops:
  0.9 18.6 %collective-permute-start = (bf16[64,128]{1,0:T(8,128)(2,1)S(1)}, bf16[64,128]{1,0:T(8,128)(2,1)S(1)}, u32[]{:S(2)}, u32[]{:S(2)}) collective-permute-start(bf16[64,128]{1,0:T(8,128)(2,1)S(1)} %get-tuple-element.28), channel_id=1, source_target_pairs={{0,28},{1,29},{2,30},{3,31},{4,0},{5,1},{6,2},{7,3},{8,4},{9,5},{1... | collective-permute-start | bytes 49160 | tf_op jit(solution)/shard_map/ppermute | solution.py:43
  6.9 14.5 %collective-permute-start.1 = (bf16[64,128]{1,0:T(8,128)(2,1)S(1)}, bf16[64,128]{1,0:T(8,128)(2,1)S(1)}, u32[]{:S(2)}, u32[]{:S(2)}) collective-permute-start(bf16[64,128]{1,0:T(8,128)(2,1)S(1)} %get-tuple-element.28), channel_id=1, source_target_pairs={{0,24},{1,25},{2,26},{3,27},{4,28},{5,29},{6,30},{7,31},{8,0},{9,1... | collective-permute-start | bytes 49160 | tf_op jit(solution)/shard_map/ppermute | solution.py:43
  7.3 15.2 %collective-permute-start.2 = (bf16[64,128]{1,0:T(8,128)(2,1)S(1)}, bf16[64,128]{1,0:T(8,128)(2,1)S(1)}, u32[]{:S(2)}, u32[]{:S(2)}) collective-permute-start(bf16[64,128]{1,0:T(8,128)(2,1)S(1)} %get-tuple-element.28), channel_id=1, source_target_pairs={{0,20},{1,21},{2,22},{3,23},{4,24},{5,25},{6,26},{7,27},{8,28},{9,... | collective-permute-start | bytes 49160 | tf_op jit(solution)/shard_map/ppermute | solution.py:43
  7.3 17.1 %collective-permute-start.3 = (bf16[64,128]{1,0:T(8,128)(2,1)S(1)}, bf16[64,128]{1,0:T(8,128)(2,1)S(1)}, u32[]{:S(2)}, u32[]{:S(2)}) collective-permute-start(bf16[64,128]{1,0:T(8,128)(2,1)S(1)} %get-tuple-element.28), channel_id=1, source_target_pairs={{0,16},{1,17},{2,18},{3,19},{4,20},{5,21},{6,22},{7,23},{8,24},{9,... | collective-permute-start | bytes 49160 | tf_op jit(solution)/shard_map/ppermute | solution.py:43
  10.3 16.6 %collective-permute-start.4 = (bf16[64,128]{1,0:T(8,128)(2,1)S(1)}, bf16[64,128]{1,0:T(8,128)(2,1)S(1)}, u32[]{:S(2)}, u32[]{:S(2)}) collective-permute-start(bf16[64,128]{1,0:T(8,128)(2,1)S(1)} %get-tuple-element.28), channel_id=1, source_target_pairs={{0,12},{1,13},{2,14},{3,15},{4,16},{5,17},{6,18},{7,19},{8,20},{9,... | collective-permute-start | bytes 49160 | tf_op jit(solution)/shard_map/ppermute | solution.py:43
  22.5 83.1 %collective-permute-start.35 = (bf16[768,384]{1,0:T(8,128)(2,1)}, bf16[768,384]{1,0:T(8,128)(2,1)}, u32[]{:S(2)}, u32[]{:S(2)}) collective-permute-start(bf16[768,384]{1,0:T(8,128)(2,1)} %get-tuple-element.53), channel_id=1, source_target_pairs={{0,4},{1,5},{2,6},{3,7},{4,0},{5,1},{6,2},{7,3},{8,12},{9,13},{10,... | collective-permute-start | bytes 1769480 | tf_op jit(solution)/shard_map/ppermute | solution.py:43
  24.4 86.0 %collective-permute-start.36 = (bf16[768,384]{1,0:T(8,128)(2,1)}, bf16[768,384]{1,0:T(8,128)(2,1)}, u32[]{:S(2)}, u32[]{:S(2)}) collective-permute-start(bf16[768,384]{1,0:T(8,128)(2,1)} %get-tuple-element.51), channel_id=1, source_target_pairs={{0,8},{1,9},{2,10},{3,11},{4,12},{5,13},{6,14},{7,15},{8,16},{9,17... | collective-permute-start | bytes 1769480 | tf_op jit(solution)/shard_map/ppermute | solution.py:43
  26.9 101.5 %collective-permute-start.38 = (bf16[768,384]{1,0:T(8,128)(2,1)}, bf16[768,384]{1,0:T(8,128)(2,1)}, u32[]{:S(2)}, u32[]{:S(2)}) collective-permute-start(bf16[768,384]{1,0:T(8,128)(2,1)} %get-tuple-element.54), channel_id=1, source_target_pairs={{0,16},{1,17},{2,18},{3,19},{4,20},{5,21},{6,22},{7,23},{8,24},{9,... | collective-permute-start | bytes 1769480 | tf_op jit(solution)/shard_map/ppermute | solution.py:43
  27.2 111.8 %collective-permute-start.40 = (bf16[768,384]{1,0:T(8,128)(2,1)}, bf16[768,384]{1,0:T(8,128)(2,1)}, u32[]{:S(2)}, u32[]{:S(2)}) collective-permute-start(bf16[768,384]{1,0:T(8,128)(2,1)} %get-tuple-element.50), channel_id=1, source_target_pairs={{0,24},{1,25},{2,26},{3,27},{4,28},{5,29},{6,30},{7,31},{8,0},{9,1... | collective-permute-start | bytes 1769480 | tf_op jit(solution)/shard_map/ppermute | solution.py:43
  103.4 13.0 %collective-permute-start.11 = (bf16[64,3072]{1,0:T(8,128)(2,1)S(1)}, bf16[64,3072]{1,0:T(8,128)(2,1)S(1)}, u32[]{:S(2)}, u32[]{:S(2)}) collective-permute-start(bf16[64,3072]{1,0:T(8,128)(2,1)S(1)} %fusion.32), channel_id=1, source_target_pairs={{0,2},{1,3},{2,0},{3,1},{4,6},{5,7},{6,4},{7,5},{8,10},{9,11},{10,... | collective-permute-start | bytes 1179656 | tf_op jit(solution)/shard_map/ppermute | solution.py:43
  105.6 34.6 %collective-permute-start.28 = (bf16[384,768]{1,0:T(8,128)(2,1)S(1)}, bf16[384,768]{1,0:T(8,128)(2,1)S(1)}, u32[]{:S(2)}, u32[]{:S(2)}) collective-permute-start(bf16[384,768]{1,0:T(8,128)(2,1)S(1)} %get-tuple-element.48), channel_id=1, source_target_pairs={{0,4},{1,5},{2,6},{3,7},{4,0},{5,1},{6,2},{7,3},{8,12},{9,13},{10,... | collective-permute-start | bytes 1769480 | tf_op jit(solution)/shard_map/ppermute | solution.py:43
  110.4 28.3 %collective-permute-start.29 = (bf16[384,768]{1,0:T(8,128)(2,1)S(1)}, bf16[384,768]{1,0:T(8,128)(2,1)S(1)}, u32[]{:S(2)}, u32[]{:S(2)}) collective-permute-start(bf16[384,768]{1,0:T(8,128)(2,1)S(1)} %get-tuple-element.46), channel_id=1, source_target_pairs={{0,8},{1,9},{2,10},{3,11},{4,12},{5,13},{6,14},{7,15},{8,16},{9,17... | collective-permute-start | bytes 1769480 | tf_op jit(solution)/shard_map/ppermute | solution.py:43
  116.4 46.8 %collective-permute-start.31 = (bf16[384,768]{1,0:T(8,128)(2,1)S(1)}, bf16[384,768]{1,0:T(8,128)(2,1)S(1)}, u32[]{:S(2)}, u32[]{:S(2)}) collective-permute-start(bf16[384,768]{1,0:T(8,128)(2,1)S(1)} %get-tuple-element.49), channel_id=1, source_target_pairs={{0,16},{1,17},{2,18},{3,19},{4,20},{5,21},{6,22},{7,23},{8,24},{9,... | collective-permute-start | bytes 1769480 | tf_op jit(solution)/shard_map/ppermute | solution.py:43
  128.4 30.9 %collective-permute-start.37 = (bf16[768,384]{1,0:T(8,128)(2,1)}, bf16[768,384]{1,0:T(8,128)(2,1)S(1)}, u32[]{:S(2)}, u32[]{:S(2)}) collective-permute-start(bf16[768,384]{1,0:T(8,128)(2,1)} %collective-permute-done.36), channel_id=1, source_target_pairs={{0,4},{1,5},{2,6},{3,7},{4,0},{5,1},{6,2},{7,3},{8,12},{9,13},{10,... | collective-permute-start | bytes 1769480 | tf_op jit(solution)/shard_map/ppermute | solution.py:43
  138.7 26.9 %collective-permute-start.30 = (bf16[384,768]{1,0:T(8,128)(2,1)S(1)}, bf16[384,768]{1,0:T(8,128)(2,1)S(1)}, u32[]{:S(2)}, u32[]{:S(2)}) collective-permute-start(bf16[384,768]{1,0:T(8,128)(2,1)S(1)} %collective-permute-done.29), channel_id=1, source_target_pairs={{0,4},{1,5},{2,6},{3,7},{4,0},{5,1},{6,2},{7,3},{8,12},{9,13},{10,... | collective-permute-start | bytes 1769480 | tf_op jit(solution)/shard_map/ppermute | solution.py:43
  139.0 39.9 %collective-permute-start.33 = (bf16[384,768]{1,0:T(8,128)(2,1)S(1)}, bf16[384,768]{1,0:T(8,128)(2,1)S(1)}, u32[]{:S(2)}, u32[]{:S(2)}) collective-permute-start(bf16[384,768]{1,0:T(8,128)(2,1)S(1)} %get-tuple-element.45), channel_id=1, source_target_pairs={{0,24},{1,25},{2,26},{3,27},{4,28},{5,29},{6,30},{7,31},{8,0},{9,1... | collective-permute-start | bytes 1769480 | tf_op jit(solution)/shard_map/ppermute | solution.py:43
  140.2 26.0 %collective-permute-start.12 = (bf16[64,3072]{1,0:T(8,128)(2,1)S(1)}, bf16[64,3072]{1,0:T(8,128)(2,1)S(1)}, u32[]{:S(2)}, u32[]{:S(2)}) collective-permute-start(bf16[64,3072]{1,0:T(8,128)(2,1)S(1)} %multiply_convert_fusion.3), channel_id=1, source_target_pairs={{0,8},{1,9},{2,0},{3,1},{4,12},{5,13},{6,4},{7,5},{8,16},{9,17},{1... | collective-permute-start | bytes 1179656 | tf_op jit(solution)/shard_map/ppermute | solution.py:43
  159.3 20.0 %collective-permute-start.39 = (bf16[768,384]{1,0:T(8,128)(2,1)}, bf16[768,384]{1,0:T(8,128)(2,1)S(1)}, u32[]{:S(2)}, u32[]{:S(2)}) collective-permute-start(bf16[768,384]{1,0:T(8,128)(2,1)} %collective-permute-done.38), channel_id=1, source_target_pairs={{0,4},{1,5},{2,6},{3,7},{4,0},{5,1},{6,2},{7,3},{8,12},{9,13},{10,... | collective-permute-start | bytes 1769480 | tf_op jit(solution)/shard_map/ppermute | solution.py:43
  163.2 30.8 %collective-permute-start.32 = (bf16[384,768]{1,0:T(8,128)(2,1)S(1)}, bf16[384,768]{1,0:T(8,128)(2,1)S(1)}, u32[]{:S(2)}, u32[]{:S(2)}) collective-permute-start(bf16[384,768]{1,0:T(8,128)(2,1)S(1)} %collective-permute-done.31), channel_id=1, source_target_pairs={{0,4},{1,5},{2,6},{3,7},{4,0},{5,1},{6,2},{7,3},{8,12},{9,13},{10,... | collective-permute-start | bytes 1769480 | tf_op jit(solution)/shard_map/ppermute | solution.py:43
  165.6 18.5 %collective-permute-start.15 = (bf16[64,3072]{1,0:T(8,128)(2,1)S(1)}, bf16[64,3072]{1,0:T(8,128)(2,1)S(1)}, u32[]{:S(2)}, u32[]{:S(2)}) collective-permute-start(bf16[64,3072]{1,0:T(8,128)(2,1)S(1)} %multiply_convert_fusion.3), channel_id=1, source_target_pairs={{0,2},{1,3},{2,10},{3,11},{4,6},{5,7},{6,14},{7,15},{8,0},{9,1},{1... | collective-permute-start | bytes 1179656 | tf_op jit(solution)/shard_map/ppermute | solution.py:43
  166.2 27.8 %collective-permute-start.13 = (bf16[64,3072]{1,0:T(8,128)(2,1)S(1)}, bf16[64,3072]{1,0:T(8,128)(2,1)S(1)}, u32[]{:S(2)}, u32[]{:S(2)}) collective-permute-start(bf16[64,3072]{1,0:T(8,128)(2,1)S(1)} %collective-permute-done.12), channel_id=1, source_target_pairs={{0,8},{1,9},{2,0},{3,1},{4,12},{5,13},{6,4},{7,5},{8,16},{9,17},{1... | collective-permute-start | bytes 1179656 | tf_op jit(solution)/shard_map/ppermute | solution.py:43
  178.9 22.2 %collective-permute-start.41 = (bf16[768,384]{1,0:T(8,128)(2,1)}, bf16[768,384]{1,0:T(8,128)(2,1)S(1)}, u32[]{:S(2)}, u32[]{:S(2)}) collective-permute-start(bf16[768,384]{1,0:T(8,128)(2,1)} %collective-permute-done.40), channel_id=1, source_target_pairs={{0,4},{1,5},{2,6},{3,7},{4,0},{5,1},{6,2},{7,3},{8,12},{9,13},{10,... | collective-permute-start | bytes 1769480 | tf_op jit(solution)/shard_map/ppermute | solution.py:43
  179.3 31.2 %collective-permute-start.34 = (bf16[384,768]{1,0:T(8,128)(2,1)S(1)}, bf16[384,768]{1,0:T(8,128)(2,1)S(1)}, u32[]{:S(2)}, u32[]{:S(2)}) collective-permute-start(bf16[384,768]{1,0:T(8,128)(2,1)S(1)} %collective-permute-done.33), channel_id=1, source_target_pairs={{0,4},{1,5},{2,6},{3,7},{4,0},{5,1},{6,2},{7,3},{8,12},{9,13},{10,... | collective-permute-start | bytes 1769480 | tf_op jit(solution)/shard_map/ppermute | solution.py:43
  184.1 27.1 %collective-permute-start.16 = (bf16[64,3072]{1,0:T(8,128)(2,1)S(1)}, bf16[64,3072]{1,0:T(8,128)(2,1)S(1)}, u32[]{:S(2)}, u32[]{:S(2)}) collective-permute-start(bf16[64,3072]{1,0:T(8,128)(2,1)S(1)} %collective-permute-done.15), channel_id=1, source_target_pairs={{0,2},{1,3},{2,10},{3,11},{4,6},{5,7},{6,14},{7,15},{8,0},{9,1},{1... | collective-permute-start | bytes 1179656 | tf_op jit(solution)/shard_map/ppermute | solution.py:43
  194.0 19.7 %collective-permute-start.14 = (bf16[64,3072]{1,0:T(8,128)(2,1)S(1)}, bf16[64,3072]{1,0:T(8,128)(2,1)S(1)}, u32[]{:S(2)}, u32[]{:S(2)}) collective-permute-start(bf16[64,3072]{1,0:T(8,128)(2,1)S(1)} %collective-permute-done.13), channel_id=1, source_target_pairs={{0,8},{1,9},{2,0},{3,1},{4,12},{5,13},{6,4},{7,5},{8,16},{9,17},{1... | collective-permute-start | bytes 1179656 | tf_op jit(solution)/shard_map/ppermute | solution.py:43
  210.6 34.6 %collective-permute-start.23 = (bf16[64,3072]{1,0:T(8,128)(2,1)S(1)}, bf16[64,3072]{1,0:T(8,128)(2,1)S(1)}, u32[]{:S(2)}, u32[]{:S(2)}) collective-permute-start(bf16[64,3072]{1,0:T(8,128)(2,1)S(1)} %multiply_convert_fusion.3), channel_id=1, source_target_pairs={{0,1},{1,0},{2,3},{3,2},{4,5},{5,4},{6,7},{7,6},{8,9},{9,8},{10,11... | collective-permute-start | bytes 1179656 | tf_op jit(solution)/shard_map/ppermute | solution.py:43
  210.7 33.5 %collective-permute-start.22 = (bf16[64,3072]{1,0:T(8,128)(2,1)S(1)}, bf16[64,3072]{1,0:T(8,128)(2,1)S(1)}, u32[]{:S(2)}, u32[]{:S(2)}) collective-permute-start(bf16[64,3072]{1,0:T(8,128)(2,1)S(1)} %collective-permute-done.12), channel_id=1, source_target_pairs={{0,1},{1,0},{2,3},{3,2},{4,5},{5,4},{6,7},{7,6},{8,9},{9,8},{10,11... | collective-permute-start | bytes 1179656 | tf_op jit(solution)/shard_map/ppermute | solution.py:43
  211.2 34.8 %collective-permute-start.24 = (bf16[64,3072]{1,0:T(8,128)(2,1)S(1)}, bf16[64,3072]{1,0:T(8,128)(2,1)S(1)}, u32[]{:S(2)}, u32[]{:S(2)}) collective-permute-start(bf16[64,3072]{1,0:T(8,128)(2,1)S(1)} %collective-permute-done.15), channel_id=1, source_target_pairs={{0,1},{1,0},{2,3},{3,2},{4,5},{5,4},{6,7},{7,6},{8,9},{9,8},{10,11... | collective-permute-start | bytes 1179656 | tf_op jit(solution)/shard_map/ppermute | solution.py:43
  211.2 21.6 %collective-permute-start.17 = (bf16[64,3072]{1,0:T(8,128)(2,1)S(1)}, bf16[64,3072]{1,0:T(8,128)(2,1)S(1)}, u32[]{:S(2)}, u32[]{:S(2)}) collective-permute-start(bf16[64,3072]{1,0:T(8,128)(2,1)S(1)} %collective-permute-done.16), channel_id=1, source_target_pairs={{0,2},{1,3},{2,10},{3,11},{4,6},{5,7},{6,14},{7,15},{8,0},{9,1},{1... | collective-permute-start | bytes 1179656 | tf_op jit(solution)/shard_map/ppermute | solution.py:43
  213.6 21.7 %collective-permute-start.18 = (bf16[32,3072]{1,0:T(8,128)(2,1)S(1)}, bf16[32,3072]{1,0:T(8,128)(2,1)S(1)}, u32[]{:S(2)}, u32[]{:S(2)}) collective-permute-start(bf16[32,3072]{1,0:T(8,128)(2,1)S(1)} %slice.204), channel_id=1, source_target_pairs={{0,8},{1,9},{2,0},{3,1},{4,12},{5,13},{6,4},{7,5},{8,16},{9,17},{1... | collective-permute-start | bytes 589832 | tf_op jit(solution)/shard_map/ppermute | solution.py:43
  286.6 10.2 %collective-permute-start.44 = (bf16[64,3072]{1,0:T(8,128)(2,1)S(1)}, bf16[64,3072]{1,0:T(8,128)(2,1)S(1)}, u32[]{:S(2)}, u32[]{:S(2)}) collective-permute-start(bf16[64,3072]{1,0:T(8,128)(2,1)S(1)} %pad_maximum_fusion.3), channel_id=1, source_target_pairs={{0,8},{1,9},{2,0},{3,1},{4,12},{5,13},{6,4},{7,5},{8,16},{9,17},{1... | collective-permute-start | bytes 1179656 | tf_op jit(solution)/shard_map/ppermute | solution.py:43
  288.3 10.3 %collective-permute-start.48 = (bf16[64,3072]{1,0:T(8,128)(2,1)S(1)}, bf16[64,3072]{1,0:T(8,128)(2,1)S(1)}, u32[]{:S(2)}, u32[]{:S(2)}) collective-permute-start(bf16[64,3072]{1,0:T(8,128)(2,1)S(1)} %pad_maximum_fusion.4), channel_id=1, source_target_pairs={{0,2},{1,3},{2,10},{3,11},{4,6},{5,7},{6,14},{7,15},{8,0},{9,1},{1... | collective-permute-start | bytes 1179656 | tf_op jit(solution)/shard_map/ppermute | solution.py:43
  307.5 13.0 %collective-permute-start.46 = (bf16[64,3072]{1,0:T(8,128)(2,1)}, bf16[64,3072]{1,0:T(8,128)(2,1)}, u32[]{:S(2)}, u32[]{:S(2)}) collective-permute-start(bf16[64,3072]{1,0:T(8,128)(2,1)} %get-tuple-element.37), channel_id=1, source_target_pairs={{0,8},{1,9},{2,0},{3,1},{4,12},{5,13},{6,4},{7,5},{8,16},{9,17},{1... | collective-permute-start | bytes 1179656 | tf_op jit(solution)/shard_map/ppermute | solution.py:43
  316.6 10.1 %collective-permute-start.9 = (f32[1,128]{1,0:T(1,128)S(1)}, f32[1,128]{1,0:T(1,128)S(1)}, u32[]{:S(2)}, u32[]{:S(2)}) collective-permute-start(f32[1,128]{1,0:T(1,128)S(1)} %slice.153), channel_id=1, source_target_pairs={{0,28},{1,29},{2,30},{3,31},{4,0},{5,1},{6,2},{7,3},{8,4},{9,5},{1... | collective-permute-start | bytes 1544 | tf_op jit(solution)/shard_map/ppermute | solution.py:43
  408.8 11.2 %collective-permute-start.61 = (bf16[64,3072]{1,0:T(8,128)(2,1)S(1)}, bf16[64,3072]{1,0:T(8,128)(2,1)S(1)}, u32[]{:S(2)}, u32[]{:S(2)}) collective-permute-start(bf16[64,3072]{1,0:T(8,128)(2,1)S(1)} %fusion.33), channel_id=1, source_target_pairs={{0,2},{1,3},{2,0},{3,1},{4,6},{5,7},{6,4},{7,5},{8,10},{9,11},{10,... | collective-permute-start | bytes 1179656 | tf_op jit(solution)/shard_map/ppermute | solution.py:43
  420.7 11.8 %collective-permute-start.62 = (bf16[64,3072]{1,0:T(8,128)(2,1)S(1)}, bf16[64,3072]{1,0:T(8,128)(2,1)S(1)}, u32[]{:S(2)}, u32[]{:S(2)}) collective-permute-start(bf16[64,3072]{1,0:T(8,128)(2,1)S(1)} %multiply_convert_fusion.1), channel_id=1, source_target_pairs={{0,8},{1,9},{2,0},{3,1},{4,12},{5,13},{6,4},{7,5},{8,16},{9,17},{1... | collective-permute-start | bytes 1179656 | tf_op jit(solution)/shard_map/ppermute | solution.py:43
  424.6 13.7 %collective-permute-start.65 = (bf16[64,3072]{1,0:T(8,128)(2,1)S(1)}, bf16[64,3072]{1,0:T(8,128)(2,1)S(1)}, u32[]{:S(2)}, u32[]{:S(2)}) collective-permute-start(bf16[64,3072]{1,0:T(8,128)(2,1)S(1)} %multiply_convert_fusion.1), channel_id=1, source_target_pairs={{0,2},{1,3},{2,10},{3,11},{4,6},{5,7},{6,14},{7,15},{8,0},{9,1},{1... | collective-permute-start | bytes 1179656 | tf_op jit(solution)/shard_map/ppermute | solution.py:43
  432.5 12.3 %collective-permute-start.63 = (bf16[64,3072]{1,0:T(8,128)(2,1)S(1)}, bf16[64,3072]{1,0:T(8,128)(2,1)S(1)}, u32[]{:S(2)}, u32[]{:S(2)}) collective-permute-start(bf16[64,3072]{1,0:T(8,128)(2,1)S(1)} %collective-permute-done.62), channel_id=1, source_target_pairs={{0,8},{1,9},{2,0},{3,1},{4,12},{5,13},{6,4},{7,5},{8,16},{9,17},{1... | collective-permute-start | bytes 1179656 | tf_op jit(solution)/shard_map/ppermute | solution.py:43
  438.3 12.1 %collective-permute-start.66 = (bf16[64,3072]{1,0:T(8,128)(2,1)S(1)}, bf16[64,3072]{1,0:T(8,128)(2,1)S(1)}, u32[]{:S(2)}, u32[]{:S(2)}) collective-permute-start(bf16[64,3072]{1,0:T(8,128)(2,1)S(1)} %collective-permute-done.65), channel_id=1, source_target_pairs={{0,2},{1,3},{2,10},{3,11},{4,6},{5,7},{6,14},{7,15},{8,0},{9,1},{1... | collective-permute-start | bytes 1179656 | tf_op jit(solution)/shard_map/ppermute | solution.py:43
  444.8 10.9 %collective-permute-start.64 = (bf16[64,3072]{1,0:T(8,128)(2,1)S(1)}, bf16[64,3072]{1,0:T(8,128)(2,1)S(1)}, u32[]{:S(2)}, u32[]{:S(2)}) collective-permute-start(bf16[64,3072]{1,0:T(8,128)(2,1)S(1)} %collective-permute-done.63), channel_id=1, source_target_pairs={{0,8},{1,9},{2,0},{3,1},{4,12},{5,13},{6,4},{7,5},{8,16},{9,17},{1... | collective-permute-start | bytes 1179656 | tf_op jit(solution)/shard_map/ppermute | solution.py:43
  449.2 25.1 %collective-permute-start.73 = (bf16[64,3072]{1,0:T(8,128)(2,1)S(1)}, bf16[64,3072]{1,0:T(8,128)(2,1)S(1)}, u32[]{:S(2)}, u32[]{:S(2)}) collective-permute-start(bf16[64,3072]{1,0:T(8,128)(2,1)S(1)} %multiply_convert_fusion.1), channel_id=1, source_target_pairs={{0,1},{1,0},{2,3},{3,2},{4,5},{5,4},{6,7},{7,6},{8,9},{9,8},{10,11... | collective-permute-start | bytes 1179656 | tf_op jit(solution)/shard_map/ppermute | solution.py:43
  449.2 24.1 %collective-permute-start.72 = (bf16[64,3072]{1,0:T(8,128)(2,1)S(1)}, bf16[64,3072]{1,0:T(8,128)(2,1)S(1)}, u32[]{:S(2)}, u32[]{:S(2)}) collective-permute-start(bf16[64,3072]{1,0:T(8,128)(2,1)S(1)} %collective-permute-done.62), channel_id=1, source_target_pairs={{0,1},{1,0},{2,3},{3,2},{4,5},{5,4},{6,7},{7,6},{8,9},{9,8},{10,11... | collective-permute-start | bytes 1179656 | tf_op jit(solution)/shard_map/ppermute | solution.py:43
  449.7 25.3 %collective-permute-start.74 = (bf16[64,3072]{1,0:T(8,128)(2,1)S(1)}, bf16[64,3072]{1,0:T(8,128)(2,1)S(1)}, u32[]{:S(2)}, u32[]{:S(2)}) collective-permute-start(bf16[64,3072]{1,0:T(8,128)(2,1)S(1)} %collective-permute-done.65), channel_id=1, source_target_pairs={{0,1},{1,0},{2,3},{3,2},{4,5},{5,4},{6,7},{7,6},{8,9},{9,8},{10,11... | collective-permute-start | bytes 1179656 | tf_op jit(solution)/shard_map/ppermute | solution.py:43
  450.4 11.6 %collective-permute-start.67 = (bf16[64,3072]{1,0:T(8,128)(2,1)S(1)}, bf16[64,3072]{1,0:T(8,128)(2,1)S(1)}, u32[]{:S(2)}, u32[]{:S(2)}) collective-permute-start(bf16[64,3072]{1,0:T(8,128)(2,1)S(1)} %collective-permute-done.66), channel_id=1, source_target_pairs={{0,2},{1,3},{2,10},{3,11},{4,6},{5,7},{6,14},{7,15},{8,0},{9,1},{1... | collective-permute-start | bytes 1179656 | tf_op jit(solution)/shard_map/ppermute | solution.py:43
  455.7 9.7 %collective-permute-start.68 = (bf16[32,3072]{1,0:T(8,128)(2,1)S(1)}, bf16[32,3072]{1,0:T(8,128)(2,1)S(1)}, u32[]{:S(2)}, u32[]{:S(2)}) collective-permute-start(bf16[32,3072]{1,0:T(8,128)(2,1)S(1)} %slice.222), channel_id=1, source_target_pairs={{0,8},{1,9},{2,0},{3,1},{4,12},{5,13},{6,4},{7,5},{8,16},{9,17},{1... | collective-permute-start | bytes 589832 | tf_op jit(solution)/shard_map/ppermute | solution.py:43
  515.6 10.2 %collective-permute-start.80 = (bf16[64,3072]{1,0:T(8,128)(2,1)S(1)}, bf16[64,3072]{1,0:T(8,128)(2,1)S(1)}, u32[]{:S(2)}, u32[]{:S(2)}) collective-permute-start(bf16[64,3072]{1,0:T(8,128)(2,1)S(1)} %pad_maximum_fusion.6), channel_id=1, source_target_pairs={{0,8},{1,9},{2,0},{3,1},{4,12},{5,13},{6,4},{7,5},{8,16},{9,17},{1... | collective-permute-start | bytes 1179656 | tf_op jit(solution)/shard_map/ppermute | solution.py:43
  517.2 10.3 %collective-permute-start.84 = (bf16[64,3072]{1,0:T(8,128)(2,1)S(1)}, bf16[64,3072]{1,0:T(8,128)(2,1)S(1)}, u32[]{:S(2)}, u32[]{:S(2)}) collective-permute-start(bf16[64,3072]{1,0:T(8,128)(2,1)S(1)} %pad_maximum_fusion.7), channel_id=1, source_target_pairs={{0,2},{1,3},{2,10},{3,11},{4,6},{5,7},{6,14},{7,15},{8,0},{9,1},{1... | collective-permute-start | bytes 1179656 | tf_op jit(solution)/shard_map/ppermute | solution.py:43
  525.9 9.3 %collective-permute-start.81 = (bf16[64,3072]{1,0:T(8,128)(2,1)S(1)}, bf16[64,3072]{1,0:T(8,128)(2,1)S(1)}, u32[]{:S(2)}, u32[]{:S(2)}) collective-permute-start(bf16[64,3072]{1,0:T(8,128)(2,1)S(1)} %add_convert_fusion.5), channel_id=1, source_target_pairs={{0,8},{1,9},{2,0},{3,1},{4,12},{5,13},{6,4},{7,5},{8,16},{9,17},{1... | collective-permute-start | bytes 1179656 | tf_op jit(solution)/shard_map/ppermute | solution.py:43
  (66 other events, 916.4 us)

commit v2 on v1

v2 whole, which is shorter than its diff:
```python
import functools

import jax
import jax.numpy as jnp
from jax import lax
from jax.experimental import pallas as pl
from jax.experimental.pallas import tpu as pltpu
from jax.sharding import PartitionSpec as P

HEAD_DIM = 128
ITERS = 2
EPSILON = 1e-05
FINE = 64
BLOCKS = 2
STRIP = 256
CHUNK = 1024
HEADS_A_STEP = 2
BF16, F32 = jnp.bfloat16, jnp.float32


def layer_norm(stream, gain):
    center = stream - jnp.mean(stream, axis=-1, keepdims=True)
    spread = jnp.mean(center * center, axis=-1, keepdims=True)
    return center * lax.rsqrt(spread + EPSILON) * gain


class Grid:
    def __init__(self):
        self.ns, self.nh = lax.axis_size("seq"), lax.axis_size("head")
        self.s, self.h = lax.axis_index("seq"), lax.axis_index("head")
        self.outer, self.groups = self.ns // 2, self.nh // 2
        self.z, self.x = self.s // 2, self.s % 2
        self.y, self.c = self.h // 2, self.h % 2
        self.ring = []
        for y in range(self.groups):
            line = [(z, y) for z in range(self.outer)]
            self.ring += line if y % 2 == 0 else line[::-1]
        self.place = {zy: i for i, zy in enumerate(self.ring)}

    def move(self, value, target):
        route = []
        for s in range(self.ns):
            for h in range(self.nh):
                there = target(s, h)
                if there is not None:
                    route.append((s * self.nh + h, there[0] * self.nh + there[1]))
        return lax.ppermute(value, ("seq", "head"), route)

    def ring_step(self, value, step):
        def target(s, h):
            i = self.place[(s // 2, h // 2)]
            z, y = self.ring[(i + step) % len(self.ring)]
            return z * 2 + s % 2, y * 2 + h % 2

        return self.move(value, target)

    def seq_shift(self, value, step):
        return self.move(value, lambda s, h: ((s + step) % self.ns, h))

    def outer_shift(self, value, step):
        return self.move(value, lambda s, h: ((s + 2 * step) % self.ns, h))

    def pair_swap(self, value):
        return self.move(value, lambda s, h: (s ^ 1, h))

    def group_shift(self, value, step):
        return self.move(value, lambda s, h: (s, (h + 2 * step) % self.nh))

    def core_swap(self, value):
        return self.move(value, lambda s, h: (s, h ^ 1))


def after_kernel(value_ref, *refs):
    refs[-1][0] = value_ref[0]


def after(value, arrays):
    smem = pl.BlockSpec(memory_space=pltpu.SMEM)
    made = pl.pallas_call(
        after_kernel,
        in_specs=[smem] + [pl.BlockSpec(memory_space=pl.ANY)] * len(arrays),
        out_specs=smem,
        out_shape=jax.ShapeDtypeStruct((1,), jnp.int32),
        name="after",
    )(value.reshape(1).astype(jnp.int32), *arrays)
    return made[0]


def place_kernel(count, sub, shifted, dest_ref, *refs):
    parts, out = refs[:count], refs[count + shifted]
    wide = refs[-1] if shifted else out
    n = 0
    for part in parts:
        for first in range(0, part.shape[0], sub):
            there = pl.ds(pl.multiple_of(dest_ref[n] * sub, sub), sub)
            wide[there, :] = part[pl.ds(first, sub), :].astype(wide.dtype)
            n += 1
    if shifted:
        moved = pltpu.roll(wide[...], 1, axis=0)
        top = lax.broadcasted_iota(jnp.int32, moved.shape, 0) == 0
        out[...] = jnp.where(top, refs[count][:1, :].astype(F32), moved).astype(out.dtype)


def place(parts, dests, sub, first=None):
    width, total = parts[0].shape[1], sum(p.shape[0] for p in parts)
    vmem = pl.BlockSpec(memory_space=pltpu.VMEM)
    extra = [] if first is None else [first]
    return pl.pallas_call(
        functools.partial(place_kernel, len(parts), sub, len(extra)),
        in_specs=[pl.BlockSpec(memory_space=pltpu.SMEM)] + [vmem] * (len(parts) + len(extra)),
        out_specs=vmem,
        out_shape=jax.ShapeDtypeStruct((total, width), parts[0].dtype),
        scratch_shapes=[pltpu.VMEM((total, width), F32)] if extra else [],
        name="place",
    )(jnp.stack(dests).astype(jnp.int32), *parts, *extra)


def gather_rows(grid, own, first=None, gates=(), late_gates=()):
    sub = own.shape[0]
    over_seq = [own] + [grid.seq_shift(own, -j) for j in range(1, grid.ns)]
    turn = after(grid.s, gates) if gates else grid.s
    line = place(over_seq, [(turn + j) % grid.ns for j in range(grid.ns)], sub)
    lines = [line] + [grid.group_shift(line, -j) for j in range(1, grid.groups)]
    heads = [((grid.y + j) % grid.groups) * 2 + grid.c for j in range(grid.groups)]
    lines += [grid.core_swap(line) for line in lines]
    heads += [head ^ 1 for head in heads]
    zero = after(grid.s, late_gates) - grid.s if late_gates else 0
    dests = [zero + seq * grid.nh + head for head in heads for seq in range(grid.ns)]
    return place(lines, dests, sub, first)


def gather_ring(grid, own, zero):
    size = len(grid.ring)
    half, cut = size // 2, own.shape[0] // 2
    pieces = {0: own}
    ahead = back = own
    for j in range(1, half):
        ahead, back = grid.ring_step(ahead, 1), grid.ring_step(back, -1)
        pieces[-j], pieces[j] = ahead, back
    pieces[half] = jnp.concatenate(
        [
            grid.ring_step(lax.dynamic_slice_in_dim(ahead, zero, cut), 1),
            grid.ring_step(lax.dynamic_slice_in_dim(back, zero + cut, cut), -1),
        ],
        axis=0,
    )
    return pieces


def reduce_ring(grid, terms):
    size = len(grid.ring)
    half, cut = size // 2, terms[0].shape[0] // 2
    ahead = grid.ring_step(terms[half][:cut].astype(BF16), 1)
    back = grid.ring_step(terms[half][cut:].astype(BF16), -1)
    for j in range(half - 1, 0, -1):
        up, down = terms[j], terms[-j]
        if j == half - 1:
            up = jnp.concatenate([up[:cut] + ahead.astype(F32), up[cut:]], axis=0)
            down = jnp.concatenate([down[:cut], down[cut:] + back.astype(F32)], axis=0)
        else:
            up, down = up + ahead.astype(F32), down + back.astype(F32)
        ahead, back = grid.ring_step(up.astype(BF16), 1), grid.ring_step(down.astype(BF16), -1)
    return terms[0] + ahead.astype(F32) + back.astype(F32)


def reduce_head(grid, term, zero):
    rows, width = term.shape
    blocks = term.reshape(grid.groups, 2, rows // grid.nh, width)
    keep = lax.dynamic_index_in_dim(blocks, grid.c + zero, 1, keepdims=False)
    give = lax.dynamic_index_in_dim(blocks, 1 - grid.c + zero, 1, keepdims=False)
    both = keep.astype(F32) + grid.core_swap(give).astype(F32)
    total = lax.dynamic_index_in_dim(both, grid.y, 0, keepdims=False)
    rounded = both.astype(BF16)
    for j in range(1, grid.groups):
        send = lax.dynamic_index_in_dim(rounded, (grid.y + j) % grid.groups, 0, keepdims=False)
        total = total + grid.group_shift(send, j).astype(F32)
    return total


class Weights:
    def __init__(self, grid, w_up, w_down):
        self.grid, self.sources = grid, (w_up, w_down)
        self.chunk, self.rows = w_up.shape[1] // grid.outer, w_up.shape[0]
        steps = [(kind, j) for kind in range(2) for j in range(1, grid.outer)]
        size, longer = divmod(len(steps), 4)
        self.phases = []
        for i in range(4):
            count = size + (i < longer)
            self.phases.append(steps[:count])
            steps = steps[count:]
        self.arrived, self.swapped = {}, {}
        for kind in range(2):
            self.arrived[kind, 0] = self.cut(kind, grid.z, 0)
            self.swapped[kind, 0] = grid.pair_swap(self.arrived[kind, 0])

    def partner(self, z, j):
        outer = self.grid.outer
        return z ^ j if outer & (outer - 1) == 0 else (2 * outer + j - z) % outer if j else z

    def cut(self, kind, to, zero):
        return lax.dynamic_slice_in_dim(
            self.sources[kind], to * self.chunk + zero, self.chunk, axis=1 - kind
        )

    def send(self, phase, zero):
        grid = self.grid
        for kind, j in self.phases[phase]:
            part = self.cut(kind, self.partner(grid.z, j), zero)
            self.arrived[kind, j] = grid.move(
                part, lambda s, h, j=j: (self.partner(s // 2, j) * 2 + s % 2, h)
            )
        return [self.arrived[step] for step in self.phases[phase]]

    def swap(self, phase):
        for step in self.phases[phase]:
            self.swapped[step] = self.grid.pair_swap(self.arrived[step])
        return [self.swapped[step] for step in self.phases[phase]]

    def parts(self):
        grid, places, made = self.grid, [], ([], [])
        for j in range(grid.outer):
            at = self.partner(grid.z, j) * 2
            places += [at + grid.x, at + 1 - grid.x]
            for kind in range(2):
                made[kind].extend([self.arrived[kind, j], self.swapped[kind, j]])
        if self.rows % 128:
            for kind in range(2):
                shape = [self.rows * grid.ns] * 2
                shape[1 - kind] = self.chunk
                full = jnp.zeros(shape, BF16)
                for at, part in zip(places, made[kind]):
                    full = lax.dynamic_update_slice_in_dim(full, part, at * self.rows, axis=kind)
                made[kind][:] = [full]
            places = [jnp.zeros_like(grid.s)]
        return jnp.stack(places).astype(jnp.int32), *made


def angle_tables(tokens, width):
    pairs = width // 2
    frequency = jnp.exp(-jnp.log(10000.0) * 2.0 * jnp.arange(pairs).astype(F32) / width)
    coarse = (jnp.arange(tokens // FINE) * FINE).astype(F32)[:, None] * frequency[None, :]
    fine = jnp.arange(FINE).astype(F32)[:, None] * frequency[None, :]
    return jnp.sin(coarse), jnp.cos(coarse), jnp.sin(fine), jnp.cos(fine)


def embedding_means(sin_a, cos_a, sin_b, cos_b):
    left = jnp.concatenate([sin_a, cos_a], axis=1)
    right = jnp.concatenate([cos_b - sin_b, cos_b + sin_b], axis=1)
    total = jnp.dot(left, right.T, precision=lax.Precision.HIGHEST)
    return (total / left.shape[1]).reshape(-1, 1)


def embed(sin_a, cos_a, sin_b, cos_b):
    return jnp.concatenate([sin_a * cos_b + cos_a * sin_b, cos_a * cos_b - sin_a * sin_b], axis=-1)


def embed_kernel(blocks, with_query, ids_ref, *refs):
    w_in_ref, gain_ref, mean_ref, sin_a, cos_a, sin_b, cos_b, wk_ref, wv_ref = refs[:9]
    refs = refs[9:]
    if with_query:
        wq_ref, ek_ref, ev_ref, cross_ref, eq_ref, aq_ref, scaled, plain = refs
    else:
        ek_ref, ev_ref, cross_ref, ak_ref, av_ref, scaled, plain = refs
    step = pl.program_id(0)
    w_in = w_in_ref[...]

    @pl.when(step == 0)
    def _():
        wide = w_in.astype(F32)
        center = wide - jnp.mean(wide, axis=-1, keepdims=True)
        center = (center * gain_ref[...]).astype(BF16)
        pairs = [(wq_ref, aq_ref)] if with_query else [(wk_ref, ak_ref), (wv_ref, av_ref)]
        for weight, out in pairs:
            out[...] = jnp.dot(center, weight[...], preferred_element_type=F32).astype(BF16)

    pairs = sin_b.shape[1]
    for column in range(0, pairs, STRIP):
        low, high = pl.ds(column, STRIP), pl.ds(pairs + column, STRIP)
        for part in range(scaled.shape[0] // FINE):
            sin_coarse, cos_coarse = sin_a[pl.ds(part, 1), low], cos_a[pl.ds(part, 1), low]
            for fine in range(0, FINE, 16):
                rows, thin = pl.ds(part * FINE + fine, 16), pl.ds(fine, 16)
                sin_fine, cos_fine, mean = sin_b[thin, low], cos_b[thin, low], mean_ref[rows, :]
                sines = sin_coarse * cos_fine + cos_coarse * sin_fine - mean
                cosines = cos_coarse * cos_fine - sin_coarse * sin_fine - mean
                scaled[rows, low] = (sines * gain_ref[:, low]).astype(BF16)
                scaled[rows, high] = (cosines * gain_ref[:, high]).astype(BF16)
                plain[rows, low] = sines.astype(BF16)
                plain[rows, high] = cosines.astype(BF16)

    @pl.when(step < blocks)
    def _():
        cross_ref[...] = lax.dot_general(
            plain[...], w_in, (((1,), (1,)), ((), ())), preferred_element_type=F32
        )
        ek_ref[...] = jnp.dot(scaled[...], wk_ref[...], preferred_element_type=F32).astype(BF16)
        ev_ref[...] = jnp.dot(scaled[...], wv_ref[...], preferred_element_type=F32).astype(BF16)

    if with_query:

        @pl.when(step == blocks)
        def _():
            rows = eq_ref.shape[0]
            first = pl.multiple_of(ids_ref[blocks + 1] * rows, rows)
            own = scaled[pl.ds(first, rows), :]
            eq_ref[...] = jnp.dot(own, wq_ref[...], preferred_element_type=F32).astype(BF16)


def embed_products(index, part, rows, w_in, tables, mean, gain, weights):
    sin_a, cos_a, sin_b, cos_b = tables
    channels, width = w_in.shape
    columns = weights[0].shape[1]
    tokens = sin_a.shape[0] * FINE
    block = rows * BLOCKS if tokens % (2 * rows * BLOCKS) == 0 else rows
    coarse, count = block // FINE, tokens // block // 2
    with_query = len(weights) == 3
    sin_a, cos_a = (t.reshape(2 * count, coarse, width // 2) for t in (sin_a, cos_a))
    ids = [part * count + i for i in range(count)]
    ids += [index // (block // rows), index % (block // rows)]
    ids = jnp.stack([jnp.asarray(i, jnp.int32) for i in ids])

    def whole(shape):
        return pl.BlockSpec(
            shape, lambda i, ids: (0,) * len(shape), pipeline_mode=pl.Buffered(buffer_count=1)
        )

    fixed = lambda shape: pl.BlockSpec(shape, lambda i, ids: (0, 0))
    coarse_spec = pl.BlockSpec((None, coarse, width // 2), lambda i, ids: (ids[i], 0, 0))
    token_in = pl.BlockSpec((block, 1), lambda i, ids: (ids[i], 0))
    token = lambda n: pl.BlockSpec((block, n), lambda i, ids: (jnp.minimum(i, count - 1), 0))
    struct = jax.ShapeDtypeStruct
    half = tokens // 2
    small = struct((channels, columns), BF16)
    return pl.pallas_call(
        functools.partial(embed_kernel, count, with_query),
        grid_spec=pltpu.PrefetchScalarGridSpec(
            num_scalar_prefetch=1,
            grid=(count + with_query,),
            in_specs=[
                whole(w_in.shape),
                whole((1, width)),
                token_in,
                coarse_spec,
                coarse_spec,
                whole(sin_b.shape),
                whole(cos_b.shape),
            ]
            + [whole(w.shape) for w in weights],
            out_specs=[token(columns), token(columns), token(channels)]
            + [fixed((rows if with_query else channels, columns)), fixed((channels, columns))],
            scratch_shapes=[pltpu.VMEM((block, width), BF16), pltpu.VMEM((block, width), BF16)],
        ),
        out_shape=[
            struct((half, columns), BF16),
            struct((half, columns), BF16),
            struct((half, channels), F32),
            struct((rows, columns), BF16) if with_query else small,
            small,
        ],
        compiler_params=pltpu.CompilerParams(vmem_limit_bytes=60 * 2**20),
        cost_estimate=pl.CostEstimate(flops=1, bytes_accessed=1, transcendentals=0),
        name="embed_products",
    )(ids, w_in, gain.reshape(1, width), mean, sin_a, cos_a, sin_b, cos_b, *weights)


def attend_kernel(
    width, scale, chunk, index_ref, cur_ref, gram_ref, size_ref, eq_ref, aq_ref, ak_ref, av_ref,
    ek_one, ek_two, ev_one, ev_two, cross_one, cross_two, out_ref, inverse,
):
    own = index_ref[0]
    rows, tokens = eq_ref.shape[0], cur_ref.shape[0]
    channels = cur_ref.shape[1]

    def of(refs, first):
        ref, start = refs[first >= tokens // 2], first % (tokens // 2)
        return ref.at[pl.ds(start, chunk)]

    ek_refs, ev_refs, cross_refs = (ek_one, ek_two), (ev_one, ev_two), (cross_one, cross_two)

    @pl.when(pl.program_id(0) == 0)
    def _():
        for first in range(0, tokens, chunk):
            here = pl.ds(first, chunk)
            both = jnp.dot(cur_ref[here, :], gram_ref[...], preferred_element_type=F32)
            both = both[:, :channels] + both[:, channels:] + 2.0 * of(cross_refs, first)[...]
            spread = jnp.sum(both * cur_ref[here, :].astype(F32), axis=-1, keepdims=True)
            inverse[here, :] = jnp.broadcast_to(
                lax.rsqrt(spread / width + size_ref[here, :] + EPSILON), (chunk, HEAD_DIM)
            )

    mine = pl.ds(pl.multiple_of(own * rows, rows), rows)
    ahead = lax.broadcasted_iota(jnp.int32, (rows, chunk), 1) - lax.broadcasted_iota(
        jnp.int32, (rows, chunk), 0
    )
    for head in range(0, eq_ref.shape[1], HEAD_DIM):
        columns = pl.ds(head, HEAD_DIM)
        made = jnp.dot(cur_ref[mine, :], aq_ref[:, columns], preferred_element_type=F32)
        made = (made + eq_ref[:, columns].astype(F32)) * inverse[mine, :]
        queries = (made * scale).astype(BF16)
        pair = jnp.concatenate([ak_ref[:, columns], av_ref[:, columns]], axis=1)
        totals = jnp.zeros((rows, HEAD_DIM), F32)
        weighted = jnp.zeros((rows, HEAD_DIM), F32)
        for first in range(0, tokens, chunk):
            here = pl.ds(first, chunk)
            made = jnp.dot(cur_ref[here, :], pair, preferred_element_type=F32)
            keys = (made[:, :HEAD_DIM] + of(ek_refs, first)[:, columns].astype(F32)) * inverse[here, :]
            values = (made[:, HEAD_DIM:] + of(ev_refs, first)[:, columns].astype(F32)) * inverse[here, :]
            scores = lax.dot_general(
                queries, keys.astype(BF16), (((1,), (1,)), ((), ())), preferred_element_type=F32
            )
            weights = jnp.exp(jnp.where(ahead <= own * rows - first, scores, -jnp.inf))
            for lane in range(0, chunk, HEAD_DIM):
                totals = totals + weights[:, lane : lane + HEAD_DIM]
            weighted = weighted + jnp.dot(
                weights.astype(BF16), values.astype(BF16), preferred_element_type=F32
            )
        out_ref[:, columns] = (weighted / jnp.sum(totals, axis=-1, keepdims=True)).astype(BF16)


def attend(index, current, gram, size, width, products):
    (ek_one, ev_one, cross_one, ak, av), (ek_two, ev_two, cross_two, eq, aq) = products
    half = current.shape[0] // 2
    rows, columns = eq.shape
    tokens, channels = current.shape
    whole = lambda shape: pl.BlockSpec(shape, lambda i, n: (0, 0))
    step = HEAD_DIM * (HEADS_A_STEP if columns % (HEAD_DIM * HEADS_A_STEP) == 0 else 1)
    head = lambda n: pl.BlockSpec((n, step), lambda i, k: (0, i))
    return pl.pallas_call(
        functools.partial(attend_kernel, width, HEAD_DIM**-0.5, min(CHUNK, tokens // 2)),
        grid_spec=pltpu.PrefetchScalarGridSpec(
            num_scalar_prefetch=1,
            grid=(columns // step,),
            in_specs=[whole(a.shape) for a in (current, gram, size)]
            + [head(rows)]
            + [head(channels)] * 3
            + [head(half)] * 4
            + [whole(cross_one.shape)] * 2,
            out_specs=head(rows),
            scratch_shapes=[pltpu.VMEM((tokens, HEAD_DIM), F32)],
        ),
        out_shape=jax.ShapeDtypeStruct((rows, columns), BF16),
        compiler_params=pltpu.CompilerParams(vmem_limit_bytes=60 * 2**20),
        cost_estimate=pl.CostEstimate(flops=1, bytes_accessed=1, transcendentals=0),
        name="attend",
    )(index.reshape(1).astype(jnp.int32), current, gram, size, eq, aq, ak, av, ek_one, ek_two, ev_one, ev_two, cross_one, cross_two)


def mlp_kernel(count, parts, gates, per_tile, places, *refs):
    pieces, refs = refs[:count], refs[count:]
    up_parts, down_parts, refs = refs[:parts], refs[parts : 2 * parts], refs[2 * parts + gates :]
    outs, (up, down, up_sem, down_sem) = refs[:count], refs[count:]
    loads = ([], [])
    for i in range(parts):
        for kind, part, full, sem in ((0, up_parts[i], up, up_sem), (1, down_parts[i], down, down_sem)):
            rows = part.shape[kind]
            at = pl.ds(pl.multiple_of(places[i] * rows, rows), rows)
            there = full.at[at, :] if kind == 0 else full.at[:, at]
            loads[kind].append(pltpu.make_async_copy(part, there, sem.at[i]))
    for load in loads[0] + loads[1]:
        load.start()
    for load in loads[0]:
        load.wait()
    sub = pieces[0].shape[0]
    for first in range(0, count, per_tile):
        tile = range(first, min(first + per_tile, count))
        rows = jnp.concatenate([pieces[i][...] for i in tile])
        hidden = jax.nn.gelu(
            jnp.dot(rows, up[...], preferred_element_type=F32), approximate=True
        ).astype(BF16)
        if first == 0:
            for load in loads[1]:
                load.wait()
        terms = jnp.dot(hidden, down[...], preferred_element_type=F32).astype(BF16)
        for n, i in enumerate(tile):
            outs[i][...] = terms[n * sub : (n + 1) * sub]


def mlp(pieces, weights, gates=()):
    places, up_parts, down_parts = weights
    count, (sub, width) = len(pieces), pieces[0].shape
    parts, chunk = len(up_parts), up_parts[0].shape[1]
    vmem = pl.BlockSpec(memory_space=pltpu.VMEM)
    anywhere = pl.BlockSpec(memory_space=pl.ANY)
    return pl.pallas_call(
        functools.partial(mlp_kernel, count, parts, len(gates), max(1, 320 // sub)),
        in_specs=[pl.BlockSpec(memory_space=pltpu.SMEM)]
        + [vmem] * count
        + [anywhere] * (2 * parts + len(gates)),
        out_specs=[vmem] * count,
        out_shape=[jax.ShapeDtypeStruct((sub, width), BF16)] * count,
        scratch_shapes=[
            pltpu.VMEM((width, chunk), BF16),
            pltpu.VMEM((chunk, width), BF16),
            pltpu.SemaphoreType.DMA((parts,)),
            pltpu.SemaphoreType.DMA((parts,)),
        ],
        compiler_params=pltpu.CompilerParams(vmem_limit_bytes=60 * 2**20),
        cost_estimate=pl.CostEstimate(flops=1, bytes_accessed=1, transcendentals=0),
        name="mlp",
    )(places, *pieces, *up_parts, *down_parts, *gates)


def per_device(
    latent, w_in, w_query, w_key, w_value, w_attn_out, w_up, w_down, w_final,
    gain_attn, gain_mlp, gain_final,
):
    grid = Grid()
    rows, channels = latent.shape
    width = w_in.shape[1]
    sub = rows // grid.nh
    tokens = rows * grid.ns
    tables = angle_tables(tokens, width)
    start = grid.s * rows + grid.h * sub

    weights = Weights(grid, w_up, w_down)
    first_two = weights.send(0, 0)
    latent_own = lax.dynamic_slice_in_dim(latent, grid.h * sub, sub)
    means = embedding_means(*tables)
    variance = 0.5 - means * means
    both = (w_key, w_value)
    one = embed_products(grid.s, 0, rows, w_in, tables, means, gain_attn, both)
    turn = after(grid.s, first_two + [one[0]])
    second = weights.send(1, turn - grid.s)
    second_swapped = [weights.swapped[kind, 0] for kind in range(2)] + weights.swap(0)
    two = embed_products(turn, 1, rows, w_in, tables, means, gain_attn, both + (w_query,))
    products = (one, two)
    latent_all = gather_rows(
        grid, latent_own.astype(BF16), gates=[one[0]], late_gates=[two[0]]
    )
    turn = after(grid.s, second + second_swapped + [two[0]])
    third = weights.send(2, turn - grid.s)
    third_swapped = weights.swap(1)
    next_row = grid.seq_shift(latent[:1], -1)
    latent_next = lax.dynamic_slice_in_dim(
        jnp.concatenate([latent, next_row]), grid.h * sub + 1, sub
    )
    wide = w_in.astype(F32)
    wide = wide - jnp.mean(wide, axis=-1, keepdims=True)
    gram = jnp.dot(wide, wide.T, precision=lax.Precision.HIGHEST)
    upper = gram.astype(BF16)
    gram = jnp.concatenate([upper, (gram - upper.astype(F32)).astype(BF16)], axis=1)
    position = (start + jnp.arange(sub)) // FINE
    offset = (start + jnp.arange(sub)) % FINE
    embedding = embed(
        *(jnp.take(t, position, axis=0) for t in tables[:2]),
        *(jnp.take(t, offset, axis=0) for t in tables[2:]),
    )

    current = latent_all
    for step_index in range(ITERS):
        attended = attend(turn if step_index == 0 else grid.s, current, gram, variance, width, products)
        own_rows = lax.dynamic_slice_in_dim(current, start, sub)
        stream_in = jnp.dot(own_rows, w_in, preferred_element_type=F32) + embedding
        zero = 0
        if step_index == 0:
            zero = after(grid.s, third + third_swapped + [attended]) - grid.s
            fourth = weights.send(3, zero)
            fourth_swapped = weights.swap(2)
        stream_attn = stream_in + reduce_head(
            grid,
            jnp.dot(attended, w_attn_out, preferred_element_type=F32).astype(BF16),
            zero,
        )
        if step_index == 0:
            zero = after(grid.s, fourth + fourth_swapped) - grid.s
            weights.swap(3)
        pieces = gather_ring(grid, layer_norm(stream_attn, gain_mlp).astype(BF16), zero)
        if step_index == 0:
            parts = weights.parts()
        half = max(pieces)
        terms, gates = {}, ()
        for part in (
            [k for k in sorted(pieces) if abs(k) <= half // 2],
            [k for k in sorted(pieces) if abs(k) > half // 2],
        ):
            others = [grid.core_swap(pieces[k]) for k in part]
            made = mlp(others + [pieces[k] for k in part], parts, gates)
            gates = (made[0],)
            for k, other, mine in zip(part, made, made[len(part) :]):
                terms[k] = mine.astype(F32) + grid.core_swap(other).astype(F32)
        stream_mlp = stream_attn + reduce_ring(grid, terms)
        final = layer_norm(stream_mlp, gain_final).astype(BF16)
        params = jnp.dot(final, w_final, preferred_element_type=F32)
        moved = latent_next * jnp.exp(jnp.tanh(params[:, channels:])) + params[:, :channels]
        if step_index < ITERS - 1:
            current = gather_rows(grid, moved.astype(BF16), latent_all[:16])

    def next_mirrored(s, h):
        there = s * grid.nh + h + 1
        if there == grid.ns * grid.nh:
            return None
        return grid.ns - 1 - there // grid.nh, there % grid.nh

    first = grid.move(moved[-1:], next_mirrored)
    mirrored = grid.move(moved, lambda s, h: (grid.ns - 1 - s, h))
    is_start = (grid.s == grid.ns - 1) & (grid.h == 0)
    first = jnp.where(is_start, latent_all[:1].astype(F32), first)
    block = jnp.concatenate([first, mirrored[:-1]])[::-1]
    blocks = [block] + [grid.group_shift(block, -j) for j in range(1, grid.groups)]
    heads = [((grid.y + j) % grid.groups) * 2 + grid.c for j in range(grid.groups)]
    blocks += [grid.core_swap(block) for block in blocks]
    heads += [head ^ 1 for head in heads]
    return place(blocks, [grid.nh - 1 - head for head in heads], sub)


def solution(mesh):
    in_specs = (
        P("seq", None),
        P(),
        P(None, "head"),
        P(None, "head"),
        P(None, "head"),
        P("head", None),
        P("seq", "head"),
        P("head", "seq"),
        P(),
        P(),
        P(),
        P(),
    )
    return jax.shard_map(
        per_device, mesh=mesh, in_specs=in_specs, out_specs=P("seq", None), check_vma=False
    )
```

time: 575 us -> 555 us (0.965)
  starting transfers between devices: 162 us -> 99.8 us
  Pallas kernels: 95.5 us -> 140 us
  waiting for transfers between devices: 177 us -> 220 us
  matrix products: 48.6 us -> 14.3 us
  local copies, waits for them, and re-layouts: 64.5 us -> 38.7 us
  between operations: 1.47 us -> 13.9 us
    ppermute x91 -> x108, starting transfers between devices: 162 us -> 99.8 us  [move(): return lax.ppermute(value, ('seq', 'head'), route)]
    pallas_call x6 -> x19, Pallas kernels: 95.5 us -> 140 us  [the longest x4 54.1 us: mlp(): pl.pallas_call(functools.partial(mlp_kernel, count, parts, len(gates), ma...]
    ppermute x91 -> x108, waiting for transfers between devices: 177 us -> 220 us  [move(): return lax.ppermute(value, ('seq', 'head'), route)]
    dot_general x4, matrix products: 40.2 us -> 4.58 us  [the longest x2 2.18 us: per_device(): stream_in = jnp.dot(own_rows, w_in, preferred_element_type=F32) + embedding]
    unnamed x103 -> x172, local copies, waits for them, and re-layouts: 33 us -> 10.4 us
    dynamic_update_slice x14 -> x0, local copies, waits for them, and re-layouts: 11.2 us -> none  [the longest x7 10.9 us: spread_weights(): down = lax.dynamic_update_slice_in_dim(down, part, place * rows, axis=1)]
    dynamic_slice x5 -> x9, local copies, waits for them, and re-layouts: 2.71 us -> 12.6 us  [the longest x5 10.6 us: cut(): lax.dynamic_slice_in_dim(self.sources[kind], to * self.chunk + zero, self...]
  transfers between devices with their start and end apart: 91 -> 108, of which waited for: 44 -> 44; matrix products, arithmetic and copies ran while one was open for 12% -> 9% of each run, Pallas kernels for 8% -> 18%
where the time goes in v2:
time: 555 us; the launch traced here: 550 us
  waiting for transfers between devices  220 us (40%)
  Pallas kernels  140 us (25%)
  starting transfers between devices  99.8 us (18%)
  local copies, waits for them, and re-layouts  38.7 us (7%)
  other arithmetic  22.8 us (4%)
  matrix products  14.3 us (3%)
  between operations  13.9 us (3%)
    ppermute x108, waiting for transfers between devices, move(): return lax.ppermute(value, ('seq', 'head'), route)  220 us
    ppermute x108, starting transfers between devices, move(): return lax.ppermute(value, ('seq', 'head'), route)  99.8 us
    pallas_call x4, Pallas kernels, mlp(): pl.pallas_call(functools.partial(mlp_kernel, count, parts, len(gates), ma...  54.1 us
    pallas_call x2, Pallas kernels, embed_products(): pl.pallas_call(functools.partial(embed_kernel, count, with_query), grid_s...  48.8 us
    pallas_call x2, Pallas kernels, attend(): pl.pallas_call(functools.partial(attend_kernel, width, HEAD_DIM ** (-0.5)...  25.7 us
  transfers between devices with their start and end apart: 108, of which 44 were waited for; matrix products, arithmetic and copies ran while one was open for 9% of the time, Pallas kernels for 18%

profile of v2, /device:TPU:0, one launch (start us, length us, event | category | flops | bytes accessed | tf_op | source)
XLA Modules:
  0.0 550.2 jit_solution(211872810988253510)
XLA Ops:
  0.9 6.0 %collective-permute-start.2 = (bf16[64,128]{1,0:T(8,128)(2,1)S(1)}, bf16[64,128]{1,0:T(8,128)(2,1)}, u32[]{:S(2)}, u32[]{:S(2)}) collective-permute-start(bf16[64,128]{1,0:T(8,128)(2,1)S(1)} %dynamic-slice_convert_fusion.2.refs_0_), channel_id=1, source_target_pairs={{0,28},{1,29},{2,30},{3,31},{4,0},{5,1},{6,2},{7,3},{8,4},{9,5},{1... | collective-permute-start | bytes 49160 | tf_op jit(solution)/shard_map/ppermute | solution.py:47
  7.3 2.7 constant_dynamic-slice_fusion.5
  22.8 18.1 %collective-permute-done.5.refs_4_ = bf16[64,128]{1,0:T(8,128)(2,1)S(1)} collective-permute-done((bf16[64,128]{1,0:T(8,128)(2,1)S(1)}, bf16[64,128]{1,0:T(8,128)(2,1)S(1)}, u32[]{:S(2)}, u32[]{:S(2)}) %collective-permute-start.5) | collective-permute-done | bytes 16416 | tf_op jit(solution)/shard_map/ppermute | solution.py:47
  45.6 22.4 %embed_products.2 = (bf16[1024,768]{1,0:T(8,128)(2,1)}, bf16[1024,768]{1,0:T(8,128)(2,1)}, f32[1024,128]{1,0:T(8,128)}, bf16[128,768]{1,0:T(8,128)(2,1)}, bf16[128,768]{1,0:T(8,128)(2,1)}) custom-call(s32[4]{0:T(128)} %pad_add_fusion.1.ids_ref, bf16[128,3072]{1,0:T(8,128)(2,1)} %refs_0_.3, f32[1,3072]{1,0:T(1,128)} %bitcast.145, ...), custom_call_target="tpu_custom_call" | custom-call | flops 1 | bytes 1 | tf_op jit(solution)/shard_map/embed_products/pallas_call | solution.py:334
  81.1 2.5 constant_dynamic-slice_fusion.4
  83.7 3.1 collective-permute-start.16
  89.0 2.5 collective-permute-start.13
  97.7 26.4 %embed_products.3 = (bf16[1024,768]{1,0:T(8,128)(2,1)}, bf16[1024,768]{1,0:T(8,128)(2,1)}, f32[1024,128]{1,0:T(8,128)}, bf16[256,768]{1,0:T(8,128)(2,1)}, bf16[128,768]{1,0:T(8,128)(2,1)}) custom-call(s32[4]{0:T(128)} %pad_add_fusion.2.ids_ref, bf16[128,3072]{1,0:T(8,128)(2,1)} %refs_0_.3, f32[1,3072]{1,0:T(1,128)} %bitcast.146, ...), custom_call_target="tpu_custom_call" | custom-call | flops 1 | bytes 1 | tf_op jit(solution)/shard_map/embed_products/pallas_call | solution.py:334
  137.4 13.4 %attend.2.refs_3_ = bf16[256,768]{1,0:T(8,128)(2,1)} custom-call(s32[1]{0:T(128)} %after.9.index_ref, bf16[2048,128]{1,0:T(8,128)(2,1)} %place.6.cur_ref, bf16[128,256]{1,0:T(8,128)(2,1)} %pad_maximum_fusion.5.gram_ref, f32[2048,1]{1,0:T(8,128)} %multiply_subtract_fusion.size_ref, bf16[256,768]{1,0:T(8,128)(2,1)} %get-tuple-element.51.eq_ref, ...), custom_call_target="tpu_custom_call" | custom-call | flops 1 | bytes 1 | tf_op jit(solution)/shard_map/attend/pallas_call | solution.py:428
  150.8 5.0 convolution_convert_fusion.1
  168.7 10.8 %collective-permute-done.23 = bf16[64,3072]{1,0:T(8,128)(2,1)S(1)} collective-permute-done((bf16[64,3072]{1,0:T(8,128)(2,1)S(1)}, bf16[64,3072]{1,0:T(8,128)(2,1)S(1)}, u32[]{:S(2)}, u32[]{:S(2)}) %collective-permute-start.23) | collective-permute-done | bytes 393248 | tf_op jit(solution)/shard_map/ppermute | solution.py:47
  183.8 9.0 %collective-permute-done.24.refs_6_ = bf16[64,3072]{1,0:T(8,128)(2,1)} collective-permute-done((bf16[64,3072]{1,0:T(8,128)(2,1)}, bf16[64,3072]{1,0:T(8,128)(2,1)}, u32[]{:S(2)}, u32[]{:S(2)}) %collective-permute-start.24) | collective-permute-done | bytes 393248 | tf_op jit(solution)/shard_map/ppermute | solution.py:47
  199.2 4.6 collective-permute-done.25.refs_5_
  203.8 13.8 %collective-permute-start.39 = (bf16[64,3072]{1,0:T(8,128)(2,1)}, bf16[64,3072]{1,0:T(8,128)(2,1)}, u32[]{:S(2)}, u32[]{:S(2)}) collective-permute-start(bf16[64,3072]{1,0:T(8,128)(2,1)} %collective-permute-done.25.refs_5_), channel_id=1, source_target_pairs={{0,8},{1,9},{2,0},{3,1},{4,12},{5,13},{6,4},{7,5},{8,16},{9,17},{1... | collective-permute-start | bytes 1179656 | tf_op jit(solution)/shard_map/ppermute | solution.py:47
  224.2 16.3 %collective-permute-done.41.refs_4_ = bf16[64,3072]{1,0:T(8,128)(2,1)} collective-permute-done((bf16[64,3072]{1,0:T(8,128)(2,1)}, bf16[64,3072]{1,0:T(8,128)(2,1)}, u32[]{:S(2)}, u32[]{:S(2)}) %collective-permute-start.41) | collective-permute-done | bytes 393248 | tf_op jit(solution)/shard_map/ppermute | solution.py:47
  243.2 2.9 collective-permute-done.43
  246.3 5.6 %collective-permute-done.44 = bf16[32,3072]{1,0:T(8,128)(2,1)S(1)} collective-permute-done((bf16[32,3072]{1,0:T(8,128)(2,1)S(1)}, bf16[32,3072]{1,0:T(8,128)(2,1)S(1)}, u32[]{:S(2)}, u32[]{:S(2)}) %collective-permute-start.44) | collective-permute-done | bytes 196640 | tf_op jit(solution)/shard_map/ppermute | solution.py:47
  255.3 14.7 %mlp.4 = (bf16[64,3072]{1,0:T(8,128)(2,1)}, bf16[64,3072]{1,0:T(8,128)(2,1)}, bf16[64,3072]{1,0:T(8,128)(2,1)}, bf16[64,3072]{1,0:T(8,128)(2,1)}, bf16[64,3072]{...) custom-call(s32[8]{0:T(128)} %stack.415.places, ...), custom_call_target="tpu_custom_call" | custom-call | flops 1 | bytes 1 | tf_op jit(solution)/shard_map/mlp/pallas_call | solution.py:484
  270.1 12.3 %mlp.5 = (bf16[64,3072]{1,0:T(8,128)(2,1)}, bf16[64,3072]{1,0:T(8,128)(2,1)}, bf16[64,3072]{1,0:T(8,128)(2,1)}, bf16[64,3072]{1,0:T(8,128)(2,1)}, bf16[64,3072]{1,0:T(8,128)(2,1)}, /*index=5*/bf16[64,3072]{1,0:T(8,128)(2,1)}) custom-call(s32[8]{0:T(128)} %stack.415.places, bf16[64,3072]{1,0:T(8,128)(2,1)} %collective-permute-done.40.refs_0_, ...), custom_call_target="tpu_custom_call" | custom-call | flops 1 | bytes 1 | tf_op jit(solution)/shard_map/mlp/pallas_call | solution.py:484
  290.9 5.1 collective-permute-done.48
  296.0 6.0 %collective-permute-done.55 = bf16[32,3072]{1,0:T(8,128)(2,1)S(1)} collective-permute-done((bf16[32,3072]{1,0:T(8,128)(2,1)S(1)}, bf16[32,3072]{1,0:T(8,128)(2,1)S(1)}, u32[]{:S(2)}, u32[]{:S(2)}) %collective-permute-start.55) | collective-permute-done | bytes 196640 | tf_op jit(solution)/shard_map/ppermute | solution.py:47
  304.2 7.5 %collective-permute-done.49 = bf16[64,3072]{1,0:T(8,128)(2,1)S(1)} collective-permute-done((bf16[64,3072]{1,0:T(8,128)(2,1)S(1)}, bf16[64,3072]{1,0:T(8,128)(2,1)S(1)}, u32[]{:S(2)}, u32[]{:S(2)}) %collective-permute-start.49) | collective-permute-done | bytes 393248 | tf_op jit(solution)/shard_map/ppermute | solution.py:47
  314.0 6.8 %collective-permute-done.56 = bf16[64,3072]{1,0:T(8,128)(2,1)S(1)} collective-permute-done((bf16[64,3072]{1,0:T(8,128)(2,1)S(1)}, bf16[64,3072]{1,0:T(8,128)(2,1)S(1)}, u32[]{:S(2)}, u32[]{:S(2)}) %collective-permute-start.56) | collective-permute-done | bytes 393248 | tf_op jit(solution)/shard_map/ppermute | solution.py:47
  324.0 5.5 collective-permute-done.57
  330.7 4.2 collective-permute-start.12
  334.9 3.6 collective-permute-done.58
  341.0 3.1 collective-permute-start.59
  347.2 2.4 collective-permute-start.63
  355.1 3.2 collective-permute-done.65.refs_7_
  360.5 5.2 collective-permute-done.66.refs_1_
  371.1 12.3 %attend.3 = bf16[256,768]{1,0:T(8,128)(2,1)} custom-call(s32[1]{0:T(128)} %bitcast.4.value_ref.index_ref, bf16[2048,128]{1,0:T(8,128)(2,1)} %place.8.cur_ref, bf16[128,256]{1,0:T(8,128)(2,1)} %pad_maximum_fusion.5.gram_ref, f32[2048,1]{1,0:T(8,128)} %multiply_subtract_fusion.size_ref, bf16[256,768]{1,0:T(8,128)(2,1)} %get-tuple-element.51.eq_ref, ...), custom_call_target="tpu_custom_call" | custom-call | flops 1 | bytes 1 | tf_op jit(solution)/shard_map/attend/pallas_call | solution.py:428
  383.4 3.9 convolution_convert_fusion
  392.8 11.4 %collective-permute-done.70 = bf16[64,3072]{1,0:T(8,128)(2,1)S(1)} collective-permute-done((bf16[64,3072]{1,0:T(8,128)(2,1)S(1)}, bf16[64,3072]{1,0:T(8,128)(2,1)S(1)}, u32[]{:S(2)}, u32[]{:S(2)}) %collective-permute-start.70) | collective-permute-done | bytes 393248 | tf_op jit(solution)/shard_map/ppermute | solution.py:47
  407.8 8.5 %collective-permute-done.71.refs_6_ = bf16[64,3072]{1,0:T(8,128)(2,1)S(1)} collective-permute-done((bf16[64,3072]{1,0:T(8,128)(2,1)S(1)}, bf16[64,3072]{1,0:T(8,128)(2,1)S(1)}, u32[]{:S(2)}, u32[]{:S(2)}) %collective-permute-start.71) | collective-permute-done | bytes 393248 | tf_op jit(solution)/shard_map/ppermute | solution.py:47
  418.4 7.6 %collective-permute-done.72.refs_5_ = bf16[64,3072]{1,0:T(8,128)(2,1)S(1)} collective-permute-done((bf16[64,3072]{1,0:T(8,128)(2,1)S(1)}, bf16[64,3072]{1,0:T(8,128)(2,1)S(1)}, u32[]{:S(2)}, u32[]{:S(2)}) %collective-permute-start.72) | collective-permute-done | bytes 393248 | tf_op jit(solution)/shard_map/ppermute | solution.py:47
  428.1 7.2 %collective-permute-done.83.refs_3_ = bf16[64,3072]{1,0:T(8,128)(2,1)S(1)} collective-permute-done((bf16[64,3072]{1,0:T(8,128)(2,1)S(1)}, bf16[64,3072]{1,0:T(8,128)(2,1)S(1)}, u32[]{:S(2)}, u32[]{:S(2)}) %collective-permute-start.83) | collective-permute-done | bytes 393248 | tf_op jit(solution)/shard_map/ppermute | solution.py:47
  437.0 4.0 collective-permute-done.87
  442.2 4.9 collective-permute-done.88
  449.3 14.7 %mlp.6 = (bf16[64,3072]{1,0:T(8,128)(2,1)}, bf16[64,3072]{1,0:T(8,128)(2,1)}, bf16[64,3072]{1,0:T(8,128)(2,1)}, bf16[64,3072]{1,0:T(8,128)(2,1)}, bf16[64,3072]{...) custom-call(s32[8]{0:T(128)} %stack.415.places, ...), custom_call_target="tpu_custom_call" | custom-call | flops 1 | bytes 1 | tf_op jit(solution)/shard_map/mlp/pallas_call | solution.py:484
  464.1 12.3 %mlp.7 = (bf16[64,3072]{1,0:T(8,128)(2,1)}, bf16[64,3072]{1,0:T(8,128)(2,1)}, bf16[64,3072]{1,0:T(8,128)(2,1)}, bf16[64,3072]{1,0:T(8,128)(2,1)}, bf16[64,3072]{1,0:T(8,128)(2,1)}, /*index=5*/bf16[64,3072]{1,0:T(8,128)(2,1)}) custom-call(s32[8]{0:T(128)} %stack.415.places, bf16[64,3072]{1,0:T(8,128)(2,1)} %collective-permute-done.84.refs_0_, ...), custom_call_target="tpu_custom_call" | custom-call | flops 1 | bytes 1 | tf_op jit(solution)/shard_map/mlp/pallas_call | solution.py:484
  483.8 6.4 %collective-permute-done.92 = bf16[32,3072]{1,0:T(8,128)(2,1)S(1)} collective-permute-done((bf16[32,3072]{1,0:T(8,128)(2,1)S(1)}, bf16[32,3072]{1,0:T(8,128)(2,1)S(1)}, u32[]{:S(2)}, u32[]{:S(2)}) %collective-permute-start.92) | collective-permute-done | bytes 196640 | tf_op jit(solution)/shard_map/ppermute | solution.py:47
  491.1 5.5 collective-permute-done.99
  497.6 8.9 %collective-permute-done.93 = bf16[64,3072]{1,0:T(8,128)(2,1)S(1)} collective-permute-done((bf16[64,3072]{1,0:T(8,128)(2,1)S(1)}, bf16[64,3072]{1,0:T(8,128)(2,1)S(1)}, u32[]{:S(2)}, u32[]{:S(2)}) %collective-permute-start.93) | collective-permute-done | bytes 393248 | tf_op jit(solution)/shard_map/ppermute | solution.py:47
  508.7 6.8 %collective-permute-done.100 = bf16[64,3072]{1,0:T(8,128)(2,1)S(1)} collective-permute-done((bf16[64,3072]{1,0:T(8,128)(2,1)S(1)}, bf16[64,3072]{1,0:T(8,128)(2,1)S(1)}, u32[]{:S(2)}, u32[]{:S(2)}) %collective-permute-start.100) | collective-permute-done | bytes 393248 | tf_op jit(solution)/shard_map/ppermute | solution.py:47
  518.0 6.8 %collective-permute-done.101 = bf16[64,3072]{1,0:T(8,128)(2,1)S(1)} collective-permute-done((bf16[64,3072]{1,0:T(8,128)(2,1)S(1)}, bf16[64,3072]{1,0:T(8,128)(2,1)S(1)}, u32[]{:S(2)}, u32[]{:S(2)}) %collective-permute-start.101) | collective-permute-done | bytes 393248 | tf_op jit(solution)/shard_map/ppermute | solution.py:47
  525.8 7.0 %collective-permute-done.102 = bf16[64,3072]{1,0:T(8,128)(2,1)S(1)} collective-permute-done((bf16[64,3072]{1,0:T(8,128)(2,1)S(1)}, bf16[64,3072]{1,0:T(8,128)(2,1)S(1)}, u32[]{:S(2)}, u32[]{:S(2)}) %collective-permute-start.102) | collective-permute-done | bytes 393248 | tf_op jit(solution)/shard_map/ppermute | solution.py:47
  536.1 5.5 %collective-permute-done.103 = f32[1,128]{1,0:T(1,128)S(1)} collective-permute-done((f32[1,128]{1,0:T(1,128)S(1)}, f32[1,128]{1,0:T(1,128)S(1)}, u32[]{:S(2)}, u32[]{:S(2)}) %collective-permute-start.103) | collective-permute-done | bytes 544 | tf_op jit(solution)/shard_map/ppermute | solution.py:47
  544.1 2.7 collective-permute-done.105.refs_1_
  (466 shorter events, 155.1 us)
Async XLA Ops:
  0.9 17.0 %collective-permute-start.2 = (bf16[64,128]{1,0:T(8,128)(2,1)S(1)}, bf16[64,128]{1,0:T(8,128)(2,1)}, u32[]{:S(2)}, u32[]{:S(2)}) collective-permute-start(bf16[64,128]{1,0:T(8,128)(2,1)S(1)} %dynamic-slice_convert_fusion.2.refs_0_), channel_id=1, source_target_pairs={{0,28},{1,29},{2,30},{3,31},{4,0},{5,1},{6,2},{7,3},{8,4},{9,5},{1... | collective-permute-start | bytes 49160 | tf_op jit(solution)/shard_map/ppermute | solution.py:47
  6.9 13.1 %collective-permute-start.3 = (bf16[64,128]{1,0:T(8,128)(2,1)S(1)}, bf16[64,128]{1,0:T(8,128)(2,1)}, u32[]{:S(2)}, u32[]{:S(2)}) collective-permute-start(bf16[64,128]{1,0:T(8,128)(2,1)S(1)} %dynamic-slice_convert_fusion.2.refs_0_), channel_id=1, source_target_pairs={{0,24},{1,25},{2,26},{3,27},{4,28},{5,29},{6,30},{7,31},{8,0},{9,1... | collective-permute-start | bytes 49160 | tf_op jit(solution)/shard_map/ppermute | solution.py:47
  7.3 14.5 %collective-permute-start.4 = (bf16[64,128]{1,0:T(8,128)(2,1)S(1)}, bf16[64,128]{1,0:T(8,128)(2,1)}, u32[]{:S(2)}, u32[]{:S(2)}) collective-permute-start(bf16[64,128]{1,0:T(8,128)(2,1)S(1)} %dynamic-slice_convert_fusion.2.refs_0_), channel_id=1, source_target_pairs={{0,20},{1,21},{2,22},{3,23},{4,24},{5,25},{6,26},{7,27},{8,28},{9,... | collective-permute-start | bytes 49160 | tf_op jit(solution)/shard_map/ppermute | solution.py:47
  10.0 69.9 %collective-permute-start = (bf16[384,768]{1,0:T(8,128)(2,1)}, bf16[384,768]{1,0:T(8,128)(2,1)}, u32[]{:S(2)}, u32[]{:S(2)}) collective-permute-start(bf16[384,768]{1,0:T(8,128)(2,1)} %get-tuple-element.101), channel_id=1, source_target_pairs={{0,8},{1,9},{2,10},{3,11},{4,12},{5,13},{6,14},{7,15},{8,0},{9,1},... | collective-permute-start | bytes 1769480 | tf_op jit(solution)/shard_map/ppermute | solution.py:47
  11.6 68.4 %collective-permute-start.1 = (bf16[384,768]{1,0:T(8,128)(2,1)}, bf16[384,768]{1,0:T(8,128)(2,1)}, u32[]{:S(2)}, u32[]{:S(2)}) collective-permute-start(bf16[384,768]{1,0:T(8,128)(2,1)} %get-tuple-element.100), channel_id=1, source_target_pairs={{0,16},{1,17},{2,18},{3,19},{4,20},{5,21},{6,22},{7,23},{8,24},{9,... | collective-permute-start | bytes 1769480 | tf_op jit(solution)/shard_map/ppermute | solution.py:47
  17.8 74.7 %collective-permute-start.15 = (bf16[384,768]{1,0:T(8,128)(2,1)}, bf16[384,768]{1,0:T(8,128)(2,1)}, u32[]{:S(2)}, u32[]{:S(2)}) collective-permute-start(bf16[384,768]{1,0:T(8,128)(2,1)} %get-tuple-element.99.refs_10_.refs_6_), channel_id=1, source_target_pairs={{0,4},{1,5},{2,6},{3,7},{4,0},{5,1},{6,2},{7,3},{8,12},{9,13},{10,... | collective-permute-start | bytes 1769480 | tf_op jit(solution)/shard_map/ppermute | solution.py:47
  19.9 20.9 %collective-permute-start.5 = (bf16[64,128]{1,0:T(8,128)(2,1)S(1)}, bf16[64,128]{1,0:T(8,128)(2,1)S(1)}, u32[]{:S(2)}, u32[]{:S(2)}) collective-permute-start(bf16[64,128]{1,0:T(8,128)(2,1)S(1)} %dynamic-slice_convert_fusion.2.refs_0_), channel_id=1, source_target_pairs={{0,16},{1,17},{2,18},{3,19},{4,20},{5,21},{6,22},{7,23},{8,24},{9,... | collective-permute-start | bytes 49160 | tf_op jit(solution)/shard_map/ppermute | solution.py:47
  21.9 20.4 %collective-permute-start.6 = (bf16[64,128]{1,0:T(8,128)(2,1)S(1)}, bf16[64,128]{1,0:T(8,128)(2,1)S(1)}, u32[]{:S(2)}, u32[]{:S(2)}) collective-permute-start(bf16[64,128]{1,0:T(8,128)(2,1)S(1)} %dynamic-slice_convert_fusion.2.refs_0_), channel_id=1, source_target_pairs={{0,12},{1,13},{2,14},{3,15},{4,16},{5,17},{6,18},{7,19},{8,20},{9,... | collective-permute-start | bytes 49160 | tf_op jit(solution)/shard_map/ppermute | solution.py:47
  40.8 34.9 %collective-permute-start.7 = (bf16[64,128]{1,0:T(8,128)(2,1)S(1)}, bf16[64,128]{1,0:T(8,128)(2,1)S(1)}, u32[]{:S(2)}, u32[]{:S(2)}) collective-permute-start(bf16[64,128]{1,0:T(8,128)(2,1)S(1)} %dynamic-slice_convert_fusion.2.refs_0_), channel_id=1, source_target_pairs={{0,8},{1,9},{2,10},{3,11},{4,12},{5,13},{6,14},{7,15},{8,16},{9,17... | collective-permute-start | bytes 49160 | tf_op jit(solution)/shard_map/ppermute | solution.py:47
  42.2 33.5 %collective-permute-start.8 = (bf16[64,128]{1,0:T(8,128)(2,1)S(1)}, bf16[64,128]{1,0:T(8,128)(2,1)S(1)}, u32[]{:S(2)}, u32[]{:S(2)}) collective-permute-start(bf16[64,128]{1,0:T(8,128)(2,1)S(1)} %dynamic-slice_convert_fusion.2.refs_0_), channel_id=1, source_target_pairs={{0,4},{1,5},{2,6},{3,7},{4,8},{5,9},{6,10},{7,11},{8,12},{9,13},{1... | collective-permute-start | bytes 49160 | tf_op jit(solution)/shard_map/ppermute | solution.py:47
  78.4 13.1 %collective-permute-start.9 = (bf16[512,128]{1,0:T(8,128)(2,1)}, bf16[512,128]{1,0:T(8,128)(2,1)}, u32[]{:S(2)}, u32[]{:S(2)}) collective-permute-start(bf16[512,128]{1,0:T(8,128)(2,1)} %place.5.refs_0_), channel_id=1, source_target_pairs={{0,2},{1,3},{2,0},{3,1},{4,6},{5,7},{6,4},{7,5},{8,10},{9,11},{10,... | collective-permute-start | bytes 393224 | tf_op jit(solution)/shard_map/ppermute | solution.py:47
  83.6 40.6 %collective-permute-start.14 = (bf16[768,384]{1,0:T(8,128)(2,1)}, bf16[768,384]{1,0:T(8,128)(2,1)}, u32[]{:S(2)}, u32[]{:S(2)}) collective-permute-start(bf16[768,384]{1,0:T(8,128)(2,1)} %get-tuple-element.98), channel_id=1, source_target_pairs={{0,8},{1,9},{2,10},{3,11},{4,12},{5,13},{6,14},{7,15},{8,0},{9,1},... | collective-permute-start | bytes 1769480 | tf_op jit(solution)/shard_map/ppermute | solution.py:47
  83.7 40.6 %collective-permute-start.16 = (bf16[768,384]{1,0:T(8,128)(2,1)}, bf16[768,384]{1,0:T(8,128)(2,1)}, u32[]{:S(2)}, u32[]{:S(2)}) collective-permute-start(bf16[768,384]{1,0:T(8,128)(2,1)} %get-tuple-element.97.refs_18_.refs_14_), channel_id=1, source_target_pairs={{0,4},{1,5},{2,6},{3,7},{4,0},{5,1},{6,2},{7,3},{8,12},{9,13},{10,... | collective-permute-start | bytes 1769480 | tf_op jit(solution)/shard_map/ppermute | solution.py:47
  89.0 35.8 %collective-permute-start.13 = (bf16[384,768]{1,0:T(8,128)(2,1)}, bf16[384,768]{1,0:T(8,128)(2,1)}, u32[]{:S(2)}, u32[]{:S(2)}) collective-permute-start(bf16[384,768]{1,0:T(8,128)(2,1)} %constant_dynamic-slice_fusion.7), channel_id=1, source_target_pairs={{0,24},{1,25},{2,26},{3,27},{4,28},{5,29},{6,30},{7,31},{8,16},{9,... | collective-permute-start | bytes 1769480 | tf_op jit(solution)/shard_map/ppermute | solution.py:47
  91.5 33.3 %collective-permute-start.17 = (bf16[384,768]{1,0:T(8,128)(2,1)}, bf16[384,768]{1,0:T(8,128)(2,1)}, u32[]{:S(2)}, u32[]{:S(2)}) collective-permute-start(bf16[384,768]{1,0:T(8,128)(2,1)} %collective-permute-done.refs_0_.refs_12_.refs_8_), channel_id=1, source_target_pairs={{0,4},{1,5},{2,6},{3,7},{4,0},{5,1},{6,2},{7,3},{8,12},{9,13},{10,... | collective-permute-start | bytes 1769480 | tf_op jit(solution)/shard_map/ppermute | solution.py:47
  92.5 32.3 %collective-permute-start.18 = (bf16[384,768]{1,0:T(8,128)(2,1)}, bf16[384,768]{1,0:T(8,128)(2,1)}, u32[]{:S(2)}, u32[]{:S(2)}) collective-permute-start(bf16[384,768]{1,0:T(8,128)(2,1)} %collective-permute-done.1.refs_1_.refs_14_.refs_10_), channel_id=1, source_target_pairs={{0,4},{1,5},{2,6},{3,7},{4,0},{5,1},{6,2},{7,3},{8,12},{9,13},{10,... | collective-permute-start | bytes 1769480 | tf_op jit(solution)/shard_map/ppermute | solution.py:47
  127.9 28.9 %collective-permute-start.19 = (bf16[768,384]{1,0:T(8,128)(2,1)}, bf16[768,384]{1,0:T(8,128)(2,1)}, u32[]{:S(2)}, u32[]{:S(2)}) collective-permute-start(bf16[768,384]{1,0:T(8,128)(2,1)} %constant_dynamic-slice_fusion.3), channel_id=1, source_target_pairs={{0,16},{1,17},{2,18},{3,19},{4,20},{5,21},{6,22},{7,23},{8,24},{9,... | collective-permute-start | bytes 1769480 | tf_op jit(solution)/shard_map/ppermute | solution.py:47
  127.9 28.9 %collective-permute-start.21 = (bf16[768,384]{1,0:T(8,128)(2,1)}, bf16[768,384]{1,0:T(8,128)(2,1)}, u32[]{:S(2)}, u32[]{:S(2)}) collective-permute-start(bf16[768,384]{1,0:T(8,128)(2,1)} %collective-permute-done.14.refs_1_.refs_20_.refs_16_), channel_id=1, source_target_pairs={{0,4},{1,5},{2,6},{3,7},{4,0},{5,1},{6,2},{7,3},{8,12},{9,13},{10,... | collective-permute-start | bytes 1769480 | tf_op jit(solution)/shard_map/ppermute | solution.py:47
  129.0 27.9 %collective-permute-start.20 = (bf16[384,768]{1,0:T(8,128)(2,1)}, bf16[384,768]{1,0:T(8,128)(2,1)}, u32[]{:S(2)}, u32[]{:S(2)}) collective-permute-start(bf16[384,768]{1,0:T(8,128)(2,1)} %collective-permute-done.13.refs_0_.refs_16_.refs_12_), channel_id=1, source_target_pairs={{0,4},{1,5},{2,6},{3,7},{4,0},{5,1},{6,2},{7,3},{8,12},{9,13},{10,... | collective-permute-start | bytes 1769480 | tf_op jit(solution)/shard_map/ppermute | solution.py:47
  182.8 14.6 %collective-permute-start.29 = (bf16[64,3072]{1,0:T(8,128)(2,1)}, bf16[64,3072]{1,0:T(8,128)(2,1)}, u32[]{:S(2)}, u32[]{:S(2)}) collective-permute-start(bf16[64,3072]{1,0:T(8,128)(2,1)} %multiply_convert_fusion.3.refs_7_), channel_id=1, source_target_pairs={{0,2},{1,3},{2,10},{3,11},{4,6},{5,7},{6,14},{7,15},{8,0},{9,1},{1... | collective-permute-start | bytes 1179656 | tf_op jit(solution)/shard_map/ppermute | solution.py:47
  195.1 24.3 %collective-permute-start.34 = (bf16[768,384]{1,0:T(8,128)(2,1)S(1)}, bf16[768,384]{1,0:T(8,128)(2,1)S(1)}, u32[]{:S(2)}, u32[]{:S(2)}) collective-permute-start(bf16[768,384]{1,0:T(8,128)(2,1)S(1)} %constant_dynamic-slice_fusion.2), channel_id=1, source_target_pairs={{0,24},{1,25},{2,26},{3,27},{4,28},{5,29},{6,30},{7,31},{8,16},{9,... | collective-permute-start | bytes 1769480 | tf_op jit(solution)/shard_map/ppermute | solution.py:47
  196.4 23.0 %collective-permute-start.33 = (bf16[768,384]{1,0:T(8,128)(2,1)}, bf16[768,384]{1,0:T(8,128)(2,1)S(1)}, u32[]{:S(2)}, u32[]{:S(2)}) collective-permute-start(bf16[768,384]{1,0:T(8,128)(2,1)} %collective-permute-done.19.refs_0_.refs_22_.refs_18_), channel_id=1, source_target_pairs={{0,4},{1,5},{2,6},{3,7},{4,0},{5,1},{6,2},{7,3},{8,12},{9,13},{10,... | collective-permute-start | bytes 1769480 | tf_op jit(solution)/shard_map/ppermute | solution.py:47
  197.4 21.9 %collective-permute-start.31 = (bf16[64,3072]{1,0:T(8,128)(2,1)}, bf16[64,3072]{1,0:T(8,128)(2,1)}, u32[]{:S(2)}, u32[]{:S(2)}) collective-permute-start(bf16[64,3072]{1,0:T(8,128)(2,1)} %collective-permute-done.29.refs_8_), channel_id=1, source_target_pairs={{0,2},{1,3},{2,10},{3,11},{4,6},{5,7},{6,14},{7,15},{8,0},{9,1},{1... | collective-permute-start | bytes 1179656 | tf_op jit(solution)/shard_map/ppermute | solution.py:47
  203.8 19.4 %collective-permute-start.39 = (bf16[64,3072]{1,0:T(8,128)(2,1)}, bf16[64,3072]{1,0:T(8,128)(2,1)}, u32[]{:S(2)}, u32[]{:S(2)}) collective-permute-start(bf16[64,3072]{1,0:T(8,128)(2,1)} %collective-permute-done.25.refs_5_), channel_id=1, source_target_pairs={{0,8},{1,9},{2,0},{3,1},{4,12},{5,13},{6,4},{7,5},{8,16},{9,17},{1... | collective-permute-start | bytes 1179656 | tf_op jit(solution)/shard_map/ppermute | solution.py:47
  219.4 21.1 %collective-permute-start.41 = (bf16[64,3072]{1,0:T(8,128)(2,1)}, bf16[64,3072]{1,0:T(8,128)(2,1)}, u32[]{:S(2)}, u32[]{:S(2)}) collective-permute-start(bf16[64,3072]{1,0:T(8,128)(2,1)} %collective-permute-done.31.refs_9_), channel_id=1, source_target_pairs={{0,2},{1,3},{2,10},{3,11},{4,6},{5,7},{6,14},{7,15},{8,0},{9,1},{1... | collective-permute-start | bytes 1179656 | tf_op jit(solution)/shard_map/ppermute | solution.py:47
  222.2 29.8 %collective-permute-start.35 = (bf16[768,384]{1,0:T(8,128)(2,1)}, bf16[768,384]{1,0:T(8,128)(2,1)S(1)}, u32[]{:S(2)}, u32[]{:S(2)}) collective-permute-start(bf16[768,384]{1,0:T(8,128)(2,1)} %copy-done.6), channel_id=1, source_target_pairs={{0,4},{1,5},{2,6},{3,7},{4,0},{5,1},{6,2},{7,3},{8,12},{9,13},{10,... | collective-permute-start | bytes 1769480 | tf_op jit(solution)/shard_map/ppermute | solution.py:47
  222.6 30.0 %collective-permute-start.28 = (bf16[64,3072]{1,0:T(8,128)(2,1)}, bf16[64,3072]{1,0:T(8,128)(2,1)S(1)}, u32[]{:S(2)}, u32[]{:S(2)}) collective-permute-start(bf16[64,3072]{1,0:T(8,128)(2,1)} %multiply_convert_fusion.3.refs_7_), channel_id=1, source_target_pairs={{0,1},{1,0},{2,3},{3,2},{4,5},{5,4},{6,7},{7,6},{8,9},{9,8},{10,11... | collective-permute-start | bytes 1179656 | tf_op jit(solution)/shard_map/ppermute | solution.py:47
  222.6 30.1 %collective-permute-start.27 = (bf16[64,3072]{1,0:T(8,128)(2,1)}, bf16[64,3072]{1,0:T(8,128)(2,1)S(1)}, u32[]{:S(2)}, u32[]{:S(2)}) collective-permute-start(bf16[64,3072]{1,0:T(8,128)(2,1)} %collective-permute-done.24.refs_6_), channel_id=1, source_target_pairs={{0,1},{1,0},{2,3},{3,2},{4,5},{5,4},{6,7},{7,6},{8,9},{9,8},{10,11... | collective-permute-start | bytes 1179656 | tf_op jit(solution)/shard_map/ppermute | solution.py:47
  223.2 30.1 %collective-permute-start.30 = (bf16[64,3072]{1,0:T(8,128)(2,1)}, bf16[64,3072]{1,0:T(8,128)(2,1)S(1)}, u32[]{:S(2)}, u32[]{:S(2)}) collective-permute-start(bf16[64,3072]{1,0:T(8,128)(2,1)} %collective-permute-done.29.refs_8_), channel_id=1, source_target_pairs={{0,1},{1,0},{2,3},{3,2},{4,5},{5,4},{6,7},{7,6},{8,9},{9,8},{10,11... | collective-permute-start | bytes 1179656 | tf_op jit(solution)/shard_map/ppermute | solution.py:47
  252.6 17.5 %collective-permute-start.40 = (bf16[64,3072]{1,0:T(8,128)(2,1)}, bf16[64,3072]{1,0:T(8,128)(2,1)}, u32[]{:S(2)}, u32[]{:S(2)}) collective-permute-start(bf16[64,3072]{1,0:T(8,128)(2,1)} %collective-permute-done.39.refs_3_), channel_id=1, source_target_pairs={{0,1},{1,0},{2,3},{3,2},{4,5},{5,4},{6,7},{7,6},{8,9},{9,8},{10,11... | collective-permute-start | bytes 1179656 | tf_op jit(solution)/shard_map/ppermute | solution.py:47
  252.7 17.4 %collective-permute-start.42 = (bf16[64,3072]{1,0:T(8,128)(2,1)}, bf16[64,3072]{1,0:T(8,128)(2,1)}, u32[]{:S(2)}, u32[]{:S(2)}) collective-permute-start(bf16[64,3072]{1,0:T(8,128)(2,1)} %collective-permute-done.41.refs_4_), channel_id=1, source_target_pairs={{0,1},{1,0},{2,3},{3,2},{4,5},{5,4},{6,7},{7,6},{8,9},{9,8},{10,11... | collective-permute-start | bytes 1179656 | tf_op jit(solution)/shard_map/ppermute | solution.py:47
  254.2 15.8 %collective-permute-start.45 = (bf16[64,3072]{1,0:T(8,128)(2,1)S(1)}, bf16[64,3072]{1,0:T(8,128)(2,1)}, u32[]{:S(2)}, u32[]{:S(2)}) collective-permute-start(bf16[64,3072]{1,0:T(8,128)(2,1)S(1)} %constant_dynamic-update-slice_fusion.refs_5_), channel_id=1, source_target_pairs={{0,1},{1,0},{2,3},{3,2},{4,5},{5,4},{6,7},{7,6},{8,9},{9,8},{10,11... | collective-permute-start | bytes 1179656 | tf_op jit(solution)/shard_map/ppermute | solution.py:47
  282.7 29.8 %collective-permute-start.53 = (bf16[64,3072]{1,0:T(8,128)(2,1)S(1)}, bf16[64,3072]{1,0:T(8,128)(2,1)S(1)}, u32[]{:S(2)}, u32[]{:S(2)}) collective-permute-start(bf16[64,3072]{1,0:T(8,128)(2,1)S(1)} %copy-done.29), channel_id=1, source_target_pairs={{0,1},{1,0},{2,3},{3,2},{4,5},{5,4},{6,7},{7,6},{8,9},{9,8},{10,11... | collective-permute-start | bytes 1179656 | tf_op jit(solution)/shard_map/ppermute | solution.py:47
  283.0 21.1 %collective-permute-start.38 = (bf16[64,3072]{1,0:T(8,128)(2,1)}, bf16[64,3072]{1,0:T(8,128)(2,1)S(1)}, u32[]{:S(2)}, u32[]{:S(2)}) collective-permute-start(bf16[64,3072]{1,0:T(8,128)(2,1)} %get-tuple-element.64), channel_id=1, source_target_pairs={{0,1},{1,0},{2,3},{3,2},{4,5},{5,4},{6,7},{7,6},{8,9},{9,8},{10,11... | collective-permute-start | bytes 1179656 | tf_op jit(solution)/shard_map/ppermute | solution.py:47
  283.2 38.4 %collective-permute-start.37 = (bf16[64,3072]{1,0:T(8,128)(2,1)}, bf16[64,3072]{1,0:T(8,128)(2,1)S(1)}, u32[]{:S(2)}, u32[]{:S(2)}) collective-permute-start(bf16[64,3072]{1,0:T(8,128)(2,1)} %get-tuple-element.62), channel_id=1, source_target_pairs={{0,1},{1,0},{2,3},{3,2},{4,5},{5,4},{6,7},{7,6},{8,9},{9,8},{10,11... | collective-permute-start | bytes 1179656 | tf_op jit(solution)/shard_map/ppermute | solution.py:47
  283.5 40.5 %collective-permute-start.52 = (bf16[64,3072]{1,0:T(8,128)(2,1)}, bf16[64,3072]{1,0:T(8,128)(2,1)S(1)}, u32[]{:S(2)}, u32[]{:S(2)}) collective-permute-start(bf16[64,3072]{1,0:T(8,128)(2,1)} %get-tuple-element.71), channel_id=1, source_target_pairs={{0,1},{1,0},{2,3},{3,2},{4,5},{5,4},{6,7},{7,6},{8,9},{9,8},{10,11... | collective-permute-start | bytes 1179656 | tf_op jit(solution)/shard_map/ppermute | solution.py:47
  304.1 30.8 %collective-permute-start.36 = (bf16[64,3072]{1,0:T(8,128)(2,1)}, bf16[64,3072]{1,0:T(8,128)(2,1)}, u32[]{:S(2)}, u32[]{:S(2)}) collective-permute-start(bf16[64,3072]{1,0:T(8,128)(2,1)} %get-tuple-element.60), channel_id=1, source_target_pairs={{0,1},{1,0},{2,3},{3,2},{4,5},{5,4},{6,7},{7,6},{8,9},{9,8},{10,11... | collective-permute-start | bytes 1179656 | tf_op jit(solution)/shard_map/ppermute | solution.py:47
  322.6 12.3 %collective-permute-start.51 = (bf16[64,3072]{1,0:T(8,128)(2,1)}, bf16[64,3072]{1,0:T(8,128)(2,1)}, u32[]{:S(2)}, u32[]{:S(2)}) collective-permute-start(bf16[64,3072]{1,0:T(8,128)(2,1)} %add_convert_fusion.7), channel_id=1, source_target_pairs={{0,8},{1,9},{2,0},{3,1},{4,12},{5,13},{6,4},{7,5},{8,16},{9,17},{1... | collective-permute-start | bytes 1179656 | tf_op jit(solution)/shard_map/ppermute | solution.py:47
  435.9 11.7 %collective-permute-start.74 = (bf16[64,3072]{1,0:T(8,128)(2,1)S(1)}, bf16[64,3072]{1,0:T(8,128)(2,1)S(1)}, u32[]{:S(2)}, u32[]{:S(2)}) collective-permute-start(bf16[64,3072]{1,0:T(8,128)(2,1)S(1)} %collective-permute-done.71.refs_6_), channel_id=1, source_target_pairs={{0,1},{1,0},{2,3},{3,2},{4,5},{5,4},{6,7},{7,6},{8,9},{9,8},{10,11... | collective-permute-start | bytes 1179656 | tf_op jit(solution)/shard_map/ppermute | solution.py:47
  436.4 11.8 %collective-permute-start.73 = (bf16[64,3072]{1,0:T(8,128)(2,1)S(1)}, bf16[64,3072]{1,0:T(8,128)(2,1)S(1)}, u32[]{:S(2)}, u32[]{:S(2)}) collective-permute-start(bf16[64,3072]{1,0:T(8,128)(2,1)S(1)} %collective-permute-done.72.refs_5_), channel_id=1, source_target_pairs={{0,1},{1,0},{2,3},{3,2},{4,5},{5,4},{6,7},{7,6},{8,9},{9,8},{10,11... | collective-permute-start | bytes 1179656 | tf_op jit(solution)/shard_map/ppermute | solution.py:47
  447.1 17.0 %collective-permute-start.84 = (bf16[64,3072]{1,0:T(8,128)(2,1)S(1)}, bf16[64,3072]{1,0:T(8,128)(2,1)}, u32[]{:S(2)}, u32[]{:S(2)}) collective-permute-start(bf16[64,3072]{1,0:T(8,128)(2,1)S(1)} %collective-permute-done.83.refs_3_), channel_id=1, source_target_pairs={{0,1},{1,0},{2,3},{3,2},{4,5},{5,4},{6,7},{7,6},{8,9},{9,8},{10,11... | collective-permute-start | bytes 1179656 | tf_op jit(solution)/shard_map/ppermute | solution.py:47
  447.7 16.4 %collective-permute-start.86 = (bf16[64,3072]{1,0:T(8,128)(2,1)S(1)}, bf16[64,3072]{1,0:T(8,128)(2,1)}, u32[]{:S(2)}, u32[]{:S(2)}) collective-permute-start(bf16[64,3072]{1,0:T(8,128)(2,1)S(1)} %collective-permute-done.85.refs_4_), channel_id=1, source_target_pairs={{0,1},{1,0},{2,3},{3,2},{4,5},{5,4},{6,7},{7,6},{8,9},{9,8},{10,11... | collective-permute-start | bytes 1179656 | tf_op jit(solution)/shard_map/ppermute | solution.py:47
  447.8 16.3 %collective-permute-start.89 = (bf16[64,3072]{1,0:T(8,128)(2,1)S(1)}, bf16[64,3072]{1,0:T(8,128)(2,1)}, u32[]{:S(2)}, u32[]{:S(2)}) collective-permute-start(bf16[64,3072]{1,0:T(8,128)(2,1)S(1)} %constant_dynamic-update-slice_fusion.2.refs_5_), channel_id=1, source_target_pairs={{0,1},{1,0},{2,3},{3,2},{4,5},{5,4},{6,7},{7,6},{8,9},{9,8},{10,11... | collective-permute-start | bytes 1179656 | tf_op jit(solution)/shard_map/ppermute | solution.py:47
  477.0 30.4 %collective-permute-start.97 = (bf16[64,3072]{1,0:T(8,128)(2,1)S(1)}, bf16[64,3072]{1,0:T(8,128)(2,1)S(1)}, u32[]{:S(2)}, u32[]{:S(2)}) collective-permute-start(bf16[64,3072]{1,0:T(8,128)(2,1)S(1)} %copy-done.28), channel_id=1, source_target_pairs={{0,1},{1,0},{2,3},{3,2},{4,5},{5,4},{6,7},{7,6},{8,9},{9,8},{10,11... | collective-permute-start | bytes 1179656 | tf_op jit(solution)/shard_map/ppermute | solution.py:47
  477.1 20.4 %collective-permute-start.82 = (bf16[64,3072]{1,0:T(8,128)(2,1)}, bf16[64,3072]{1,0:T(8,128)(2,1)S(1)}, u32[]{:S(2)}, u32[]{:S(2)}) collective-permute-start(bf16[64,3072]{1,0:T(8,128)(2,1)} %get-tuple-element.80), channel_id=1, source_target_pairs={{0,1},{1,0},{2,3},{3,2},{4,5},{5,4},{6,7},{7,6},{8,9},{9,8},{10,11... | collective-permute-start | bytes 1179656 | tf_op jit(solution)/shard_map/ppermute | solution.py:47
  477.5 39.0 %collective-permute-start.81 = (bf16[64,3072]{1,0:T(8,128)(2,1)S(1)}, bf16[64,3072]{1,0:T(8,128)(2,1)S(1)}, u32[]{:S(2)}, u32[]{:S(2)}) collective-permute-start(bf16[64,3072]{1,0:T(8,128)(2,1)S(1)} %copy-done.81), channel_id=1, source_target_pairs={{0,1},{1,0},{2,3},{3,2},{4,5},{5,4},{6,7},{7,6},{8,9},{9,8},{10,11... | collective-permute-start | bytes 1179656 | tf_op jit(solution)/shard_map/ppermute | solution.py:47
  477.6 40.4 %collective-permute-start.96 = (bf16[64,3072]{1,0:T(8,128)(2,1)S(1)}, bf16[64,3072]{1,0:T(8,128)(2,1)S(1)}, u32[]{:S(2)}, u32[]{:S(2)}) collective-permute-start(bf16[64,3072]{1,0:T(8,128)(2,1)S(1)} %copy-done.80), channel_id=1, source_target_pairs={{0,1},{1,0},{2,3},{3,2},{4,5},{5,4},{6,7},{7,6},{8,9},{9,8},{10,11... | collective-permute-start | bytes 1179656 | tf_op jit(solution)/shard_map/ppermute | solution.py:47
  497.5 28.3 %collective-permute-start.80 = (bf16[64,3072]{1,0:T(8,128)(2,1)S(1)}, bf16[64,3072]{1,0:T(8,128)(2,1)S(1)}, u32[]{:S(2)}, u32[]{:S(2)}) collective-permute-start(bf16[64,3072]{1,0:T(8,128)(2,1)S(1)} %copy-done.79), channel_id=1, source_target_pairs={{0,1},{1,0},{2,3},{3,2},{4,5},{5,4},{6,7},{7,6},{8,9},{9,8},{10,11... | collective-permute-start | bytes 1179656 | tf_op jit(solution)/shard_map/ppermute | solution.py:47
  (145 other events, 1572.0 us)

commit v3 on v2

--- a/solution.py
+++ b/solution.py
@@ -115,21 +115,24 @@
     )(jnp.stack(dests).astype(jnp.int32), *parts, *extra)
 
 
-def gather_rows(grid, own, first=None, gates=(), late_gates=()):
+def gather_seq(grid, own):
+    return [own] + [grid.seq_shift(own, -j) for j in range(1, grid.ns)]
+
+
+def gather_rows(grid, own, first=None, over_seq=None, gates=()):
     sub = own.shape[0]
-    over_seq = [own] + [grid.seq_shift(own, -j) for j in range(1, grid.ns)]
+    over_seq = over_seq or gather_seq(grid, own)
     turn = after(grid.s, gates) if gates else grid.s
     line = place(over_seq, [(turn + j) % grid.ns for j in range(grid.ns)], sub)
     lines = [line] + [grid.group_shift(line, -j) for j in range(1, grid.groups)]
     heads = [((grid.y + j) % grid.groups) * 2 + grid.c for j in range(grid.groups)]
     lines += [grid.core_swap(line) for line in lines]
     heads += [head ^ 1 for head in heads]
-    zero = after(grid.s, late_gates) - grid.s if late_gates else 0
-    dests = [zero + seq * grid.nh + head for head in heads for seq in range(grid.ns)]
+    dests = [seq * grid.nh + head for head in heads for seq in range(grid.ns)]
     return place(lines, dests, sub, first)
 
 
-def gather_ring(grid, own, zero):
+def gather_ring(grid, own):
     size = len(grid.ring)
     half, cut = size // 2, own.shape[0] // 2
     pieces = {0: own}
@@ -139,8 +142,8 @@
         pieces[-j], pieces[j] = ahead, back
     pieces[half] = jnp.concatenate(
         [
-            grid.ring_step(lax.dynamic_slice_in_dim(ahead, zero, cut), 1),
-            grid.ring_step(lax.dynamic_slice_in_dim(back, zero + cut, cut), -1),
+            grid.ring_step(ahead[:cut], 1),
+            grid.ring_step(back[cut:], -1),
         ],
         axis=0,
     )
@@ -166,10 +169,10 @@
 def reduce_head(grid, term, zero):
     rows, width = term.shape
     blocks = term.reshape(grid.groups, 2, rows // grid.nh, width)
-    keep = lax.dynamic_index_in_dim(blocks, grid.c + zero, 1, keepdims=False)
-    give = lax.dynamic_index_in_dim(blocks, 1 - grid.c + zero, 1, keepdims=False)
+    keep = lax.dynamic_index_in_dim(blocks, grid.c, 1, keepdims=False)
+    give = lax.dynamic_index_in_dim(blocks, 1 - grid.c, 1, keepdims=False)
     both = keep.astype(F32) + grid.core_swap(give).astype(F32)
-    total = lax.dynamic_index_in_dim(both, grid.y, 0, keepdims=False)
+    total = lax.dynamic_index_in_dim(both, grid.y + zero, 0, keepdims=False)
     rounded = both.astype(BF16)
     for j in range(1, grid.groups):
         send = lax.dynamic_index_in_dim(rounded, (grid.y + j) % grid.groups, 0, keepdims=False)
@@ -179,60 +182,61 @@
 
 class Weights:
     def __init__(self, grid, w_up, w_down):
-        self.grid, self.sources = grid, (w_up, w_down)
+        self.grid, self.w_up, self.w_down = grid, w_up, w_down
         self.chunk, self.rows = w_up.shape[1] // grid.outer, w_up.shape[0]
-        steps = [(kind, j) for kind in range(2) for j in range(1, grid.outer)]
-        size, longer = divmod(len(steps), 4)
-        self.phases = []
-        for i in range(4):
-            count = size + (i < longer)
-            self.phases.append(steps[:count])
-            steps = steps[count:]
-        self.arrived, self.swapped = {}, {}
-        for kind in range(2):
-            self.arrived[kind, 0] = self.cut(kind, grid.z, 0)
-            self.swapped[kind, 0] = grid.pair_swap(self.arrived[kind, 0])
+        self.arrived = {0: self.cut(grid.z)}
+        self.swapped = {}
 
     def partner(self, z, j):
         outer = self.grid.outer
-        return z ^ j if outer & (outer - 1) == 0 else (2 * outer + j - z) % outer if j else z
-
-    def cut(self, kind, to, zero):
-        return lax.dynamic_slice_in_dim(
-            self.sources[kind], to * self.chunk + zero, self.chunk, axis=1 - kind
+        if j == 0:
+            return z
+        return z ^ j if outer & (outer - 1) == 0 else (2 * outer + j - z) % outer
+
+    def cut(self, to):
+        rows, chunk = self.rows, self.chunk
+        up = lax.dynamic_slice_in_dim(self.w_up, to * chunk, chunk, axis=1)
+        if chunk % rows:
+            down = lax.dynamic_slice_in_dim(self.w_down, to * chunk, chunk).reshape(rows, chunk)
+            return jnp.concatenate([up, down], axis=1)
+        blocks = [
+            lax.dynamic_slice_in_dim(self.w_down, to * chunk + first, rows)
+            for first in range(0, chunk, rows)
+        ]
+        return jnp.concatenate([up] + blocks, axis=1)
+
+    def send(self, j):
+        self.arrived[j] = self.grid.move(
+            self.cut(self.partner(self.grid.z, j)),
+            lambda s, h: (self.partner(s // 2, j) * 2 + s % 2, h),
         )
-
-    def send(self, phase, zero):
-        grid = self.grid
-        for kind, j in self.phases[phase]:
-            part = self.cut(kind, self.partner(grid.z, j), zero)
-            self.arrived[kind, j] = grid.move(
-                part, lambda s, h, j=j: (self.partner(s // 2, j) * 2 + s % 2, h)
-            )
-        return [self.arrived[step] for step in self.phases[phase]]
-
-    def swap(self, phase):
-        for step in self.phases[phase]:
-            self.swapped[step] = self.grid.pair_swap(self.arrived[step])
-        return [self.swapped[step] for step in self.phases[phase]]
+        return self.arrived[j]
+
+    def swap(self, j):
+        self.swapped[j] = self.grid.pair_swap(self.arrived[j])
+        return self.swapped[j]
 
     def parts(self):
-        grid, places, made = self.grid, [], ([], [])
+        grid, rows, chunk, places, parts = self.grid, self.rows, self.chunk, [], []
         for j in range(grid.outer):
             at = self.partner(grid.z, j) * 2
             places += [at + grid.x, at + 1 - grid.x]
-            for kind in range(2):
-                made[kind].extend([self.arrived[kind, j], self.swapped[kind, j]])
-        if self.rows % 128:
-            for kind in range(2):
-                shape = [self.rows * grid.ns] * 2
-                shape[1 - kind] = self.chunk
-                full = jnp.zeros(shape, BF16)
-                for at, part in zip(places, made[kind]):
-                    full = lax.dynamic_update_slice_in_dim(full, part, at * self.rows, axis=kind)
-                made[kind][:] = [full]
-            places = [jnp.zeros_like(grid.s)]
-        return jnp.stack(places).astype(jnp.int32), *made
+            parts += [self.arrived[j], self.swapped[j]]
+        if rows % 128 == 0 and chunk % rows == 0:
+            return jnp.stack(places).astype(jnp.int32), parts
+        up = jnp.zeros((rows * grid.ns, chunk), BF16)
+        down = jnp.zeros((chunk, rows * grid.ns), BF16)
+        for at, part in zip(places, parts):
+            right = part[:, chunk:]
+            if chunk % rows:
+                right = right.reshape(chunk, rows)
+            else:
+                right = jnp.concatenate(
+                    [right[:, first : first + rows] for first in range(0, chunk, rows)]
+                )
+            up = lax.dynamic_update_slice_in_dim(up, part[:, :chunk], at * rows, axis=0)
+            down = lax.dynamic_update_slice_in_dim(down, right, at * rows, axis=1)
+        return jnp.zeros((1,), jnp.int32), [up, down]
 
 
 def angle_tables(tokens, width):
@@ -358,7 +362,11 @@
             small,
         ],
         compiler_params=pltpu.CompilerParams(vmem_limit_bytes=60 * 2**20),
-        cost_estimate=pl.CostEstimate(flops=1, bytes_accessed=1, transcendentals=0),
+        cost_estimate=pl.CostEstimate(
+            flops=8 * tokens * width * columns,
+            bytes_accessed=6 * width * columns,
+            transcendentals=0,
+        ),
         name="embed_products",
     )(ids, w_in, gain.reshape(1, width), mean, sin_a, cos_a, sin_b, cos_b, *weights)
 
@@ -440,25 +448,37 @@
         ),
         out_shape=jax.ShapeDtypeStruct((rows, columns), BF16),
         compiler_params=pltpu.CompilerParams(vmem_limit_bytes=60 * 2**20),
-        cost_estimate=pl.CostEstimate(flops=1, bytes_accessed=1, transcendentals=0),
+        cost_estimate=pl.CostEstimate(
+            flops=16 * rows * tokens * columns,
+            bytes_accessed=4 * tokens * columns,
+            transcendentals=0,
+        ),
         name="attend",
     )(index.reshape(1).astype(jnp.int32), current, gram, size, eq, aq, ak, av, ek_one, ek_two, ev_one, ev_two, cross_one, cross_two)
 
 
 def mlp_kernel(count, parts, gates, per_tile, places, *refs):
     pieces, refs = refs[:count], refs[count:]
-    up_parts, down_parts, refs = refs[:parts], refs[parts : 2 * parts], refs[2 * parts + gates :]
+    parts, refs = refs[:parts], refs[parts + gates :]
     outs, (up, down, up_sem, down_sem) = refs[:count], refs[count:]
-    loads = ([], [])
-    for i in range(parts):
-        for kind, part, full, sem in ((0, up_parts[i], up, up_sem), (1, down_parts[i], down, down_sem)):
-            rows = part.shape[kind]
+    width, chunk = up.shape
+    ups, downs = [], []
+    if parts[0].shape == up.shape:
+        ups.append(pltpu.make_async_copy(parts[0], up, up_sem.at[0]))
+        downs.append(pltpu.make_async_copy(parts[1], down, down_sem.at[0]))
+    else:
+        for i, part in enumerate(parts):
+            rows = part.shape[0]
             at = pl.ds(pl.multiple_of(places[i] * rows, rows), rows)
-            there = full.at[at, :] if kind == 0 else full.at[:, at]
-            loads[kind].append(pltpu.make_async_copy(part, there, sem.at[i]))
-    for load in loads[0] + loads[1]:
+            left = part.at[:, pl.ds(0, chunk)]
+            ups.append(pltpu.make_async_copy(left, up.at[at, :], up_sem.at[i]))
+            for n in range(chunk // rows):
+                block = part.at[:, pl.ds(chunk + n * rows, rows)]
+                there = down.at[pl.ds(n * rows, rows), at]
+                downs.append(pltpu.make_async_copy(block, there, down_sem.at[len(downs)]))
+    for load in ups + downs:
         load.start()
-    for load in loads[0]:
+    for load in ups:
         load.wait()
     sub = pieces[0].shape[0]
     for first in range(0, count, per_tile):
@@ -468,7 +488,7 @@
             jnp.dot(rows, up[...], preferred_element_type=F32), approximate=True
         ).astype(BF16)
         if first == 0:
-            for load in loads[1]:
+            for load in downs:
                 load.wait()
         terms = jnp.dot(hidden, down[...], preferred_element_type=F32).astype(BF16)
         for n, i in enumerate(tile):
@@ -476,28 +496,32 @@
 
 
 def mlp(pieces, weights, gates=()):
-    places, up_parts, down_parts = weights
+    places, parts = weights
     count, (sub, width) = len(pieces), pieces[0].shape
-    parts, chunk = len(up_parts), up_parts[0].shape[1]
+    chunk = parts[0].shape[1] if parts[0].shape[0] == width else parts[0].shape[1] // 2
     vmem = pl.BlockSpec(memory_space=pltpu.VMEM)
     anywhere = pl.BlockSpec(memory_space=pl.ANY)
     return pl.pallas_call(
-        functools.partial(mlp_kernel, count, parts, len(gates), max(1, 320 // sub)),
+        functools.partial(mlp_kernel, count, len(parts), len(gates), max(1, 320 // sub)),
         in_specs=[pl.BlockSpec(memory_space=pltpu.SMEM)]
         + [vmem] * count
-        + [anywhere] * (2 * parts + len(gates)),
+        + [anywhere] * (len(parts) + len(gates)),
         out_specs=[vmem] * count,
         out_shape=[jax.ShapeDtypeStruct((sub, width), BF16)] * count,
         scratch_shapes=[
             pltpu.VMEM((width, chunk), BF16),
             pltpu.VMEM((chunk, width), BF16),
-            pltpu.SemaphoreType.DMA((parts,)),
-            pltpu.SemaphoreType.DMA((parts,)),
+            pltpu.SemaphoreType.DMA((len(parts),)),
+            pltpu.SemaphoreType.DMA((len(parts) * max(1, chunk * len(parts) // width),)),
         ],
         compiler_params=pltpu.CompilerParams(vmem_limit_bytes=60 * 2**20),
-        cost_estimate=pl.CostEstimate(flops=1, bytes_accessed=1, transcendentals=0),
+        cost_estimate=pl.CostEstimate(
+            flops=8 * count * sub * width * chunk,
+            bytes_accessed=4 * width * chunk,
+            transcendentals=0,
+        ),
         name="mlp",
-    )(places, *pieces, *up_parts, *down_parts, *gates)
+    )(places, *pieces, *parts, *gates)
 
 
 def per_device(
@@ -513,23 +537,28 @@
     start = grid.s * rows + grid.h * sub
 
     weights = Weights(grid, w_up, w_down)
-    first_two = weights.send(0, 0)
+    own_swap = weights.swap(0)
+    arrivals = [weights.send(j) for j in range(1, grid.outer)]
+    early = max(1, len(arrivals) * 2 // 3)
     latent_own = lax.dynamic_slice_in_dim(latent, grid.h * sub, sub)
     means = embedding_means(*tables)
     variance = 0.5 - means * means
     both = (w_key, w_value)
-    one = embed_products(grid.s, 0, rows, w_in, tables, means, gain_attn, both)
-    turn = after(grid.s, first_two + [one[0]])
-    second = weights.send(1, turn - grid.s)
-    second_swapped = [weights.swapped[kind, 0] for kind in range(2)] + weights.swap(0)
+    latent_own_rounded = latent_own.astype(BF16)
+    over_seq = gather_seq(grid, latent_own_rounded)
+    turn = after(grid.s, over_seq)
+    one = embed_products(turn, 0, rows, w_in, tables, means, gain_attn, both)
+    turn = after(turn, [one[0]])
     two = embed_products(turn, 1, rows, w_in, tables, means, gain_attn, both + (w_query,))
     products = (one, two)
     latent_all = gather_rows(
-        grid, latent_own.astype(BF16), gates=[one[0]], late_gates=[two[0]]
+        grid,
+        latent_own_rounded,
+        over_seq=over_seq,
+        gates=arrivals[:early] + [own_swap, two[0]],
     )
-    turn = after(grid.s, second + second_swapped + [two[0]])
-    third = weights.send(2, turn - grid.s)
-    third_swapped = weights.swap(1)
+    early_swaps = [weights.swap(j) for j in range(1, early + 1)]
+    turn = after(grid.s, arrivals[early:] + early_swaps[:1])
     next_row = grid.seq_shift(latent[:1], -1)
     latent_next = lax.dynamic_slice_in_dim(
         jnp.concatenate([latent, next_row]), grid.h * sub + 1, sub
@@ -553,18 +582,15 @@
         stream_in = jnp.dot(own_rows, w_in, preferred_element_type=F32) + embedding
         zero = 0
         if step_index == 0:
-            zero = after(grid.s, third + third_swapped + [attended]) - grid.s
-            fourth = weights.send(3, zero)
-            fourth_swapped = weights.swap(2)
+            zero = after(grid.s, early_swaps[1:]) - grid.s
+            for j in range(early + 1, grid.outer):
+                weights.swap(j)
         stream_attn = stream_in + reduce_head(
             grid,
             jnp.dot(attended, w_attn_out, preferred_element_type=F32).astype(BF16),
             zero,
         )
-        if step_index == 0:
-            zero = after(grid.s, fourth + fourth_swapped) - grid.s
-            weights.swap(3)
-        pieces = gather_ring(grid, layer_norm(stream_attn, gain_mlp).astype(BF16), zero)
+        pieces = gather_ring(grid, layer_norm(stream_attn, gain_mlp).astype(BF16))
         if step_index == 0:
             parts = weights.parts()
         half = max(pieces)

time: 555 us -> 553 us (level)
  starting transfers between devices: 99.8 us -> 92.2 us
    dynamic_slice x9 -> x2, local copies, waits for them, and re-layouts: 12.6 us -> 2.17 us  [the longest x1 1.91 us: cut(): up = lax.dynamic_slice_in_dim(self.w_up, to * chunk, chunk, axis=1)]
    ppermute x108 -> x101, starting transfers between devices: 99.8 us -> 92.2 us  [move(): return lax.ppermute(value, ('seq', 'head'), route)]
    ppermute x108 -> x101, waiting for transfers between devices: 220 us -> 224 us  [move(): return lax.ppermute(value, ('seq', 'head'), route)]
  transfers between devices with their start and end apart: 108 -> 101, of which waited for: 44 -> 45; matrix products, arithmetic and copies ran while one was open for 9% -> 9% of each run, Pallas kernels for 18% -> 16%
where the time goes in v3:
time: 553 us; the launch traced here: 548 us
  waiting for transfers between devices  224 us (41%)
  Pallas kernels  141 us (25%)
  starting transfers between devices  92.2 us (17%)
  local copies, waits for them, and re-layouts  34.9 us (6%)
  other arithmetic  26.5 us (5%)
  matrix products  14.5 us (3%)
  between operations  13.6 us (2%)
    ppermute x101, waiting for transfers between devices, move(): return lax.ppermute(value, ('seq', 'head'), route)  224 us
    ppermute x101, starting transfers between devices, move(): return lax.ppermute(value, ('seq', 'head'), route)  92.2 us
    pallas_call x4, Pallas kernels, mlp(): pl.pallas_call(functools.partial(mlp_kernel, count, len(parts), len(gates...  55 us
    pallas_call x2, Pallas kernels, embed_products(): pl.pallas_call(functools.partial(embed_kernel, count, with_query), grid_s...  48.7 us
    pallas_call x2, Pallas kernels, attend(): pl.pallas_call(functools.partial(attend_kernel, width, HEAD_DIM ** (-0.5)...  25.8 us
    unnamed x172, local copies, waits for them, and re-layouts  15.2 us
  transfers between devices with their start and end apart: 101, of which 45 were waited for; matrix products, arithmetic and copies ran while one was open for 9% of the time, Pallas kernels for 16%

profile of v3, /device:TPU:0, one launch (start us, length us, event | category | flops | bytes accessed | tf_op | source)
XLA Modules:
  0.0 547.5 jit_solution(16751628171191631146)
XLA Ops:
  0.9 6.0 %collective-permute-start.3 = (bf16[64,128]{1,0:T(8,128)(2,1)S(1)}, bf16[64,128]{1,0:T(8,128)(2,1)S(1)}, u32[]{:S(2)}, u32[]{:S(2)}) collective-permute-start(bf16[64,128]{1,0:T(8,128)(2,1)S(1)} %dynamic-slice_convert_fusion.2.refs_0_), channel_id=1, source_target_pairs={{0,28},{1,29},{2,30},{3,31},{4,0},{5,1},{6,2},{7,3},{8,4},{9,5},{1... | collective-permute-start | bytes 49160 | tf_op jit(solution)/shard_map/ppermute | solution.py:47
  7.3 3.0 collective-permute-start.6
  10.4 2.3 multiply_cosine_fusion
  17.8 2.3 multiply_subtract_fusion.size_ref
  30.8 2.4 collective-permute-start.1
  35.6 2.1 collective-permute-start.14
  42.0 22.3 %embed_products.2 = (bf16[1024,768]{1,0:T(8,128)(2,1)}, bf16[1024,768]{1,0:T(8,128)(2,1)}, f32[1024,128]{1,0:T(8,128)}, bf16[128,768]{1,0:T(8,128)(2,1)}, bf16[128,768]{1,0:T(8,128)(2,1)}) custom-call(s32[4]{0:T(128)} %pad_add_fusion.1.ids_ref, bf16[128,3072]{1,0:T(8,128)(2,1)} %refs_0_.3, f32[1,3072]{1,0:T(1,128)} %bitcast.112, ...), custom_call_target="tpu_custom_call" | custom-call | flops 38654705664 | bytes 14155776 | tf_op jit(solution)/shard_map/embed_products/pallas_call | solution.py:338
  68.4 41.6 %collective-permute-done.refs_0_.refs_12_.refs_8_ = bf16[384,1536]{1,0:T(8,128)(2,1)} collective-permute-done((bf16[384,1536]{1,0:T(8,128)(2,1)}, bf16[384,1536]{1,0:T(8,128)(2,1)}, u32[]{:S(2)}, u32[]{:S(2)}) %collective-permute-start) | collective-permute-done | bytes 1179680 | tf_op jit(solution)/shard_map/ppermute | solution.py:47
  110.0 26.3 %embed_products.3 = (bf16[1024,768]{1,0:T(8,128)(2,1)}, bf16[1024,768]{1,0:T(8,128)(2,1)}, f32[1024,128]{1,0:T(8,128)}, bf16[256,768]{1,0:T(8,128)(2,1)}, bf16[128,768]{1,0:T(8,128)(2,1)}) custom-call(s32[4]{0:T(128)} %pad_add_fusion.2.ids_ref, bf16[128,3072]{1,0:T(8,128)(2,1)} %refs_0_.3, f32[1,3072]{1,0:T(1,128)} %bitcast.113, ...), custom_call_target="tpu_custom_call" | custom-call | flops 38654705664 | bytes 14155776 | tf_op jit(solution)/shard_map/embed_products/pallas_call | solution.py:338
  147.2 3.6 collective-permute-done.10.refs_1_
  157.7 13.5 %attend.2 = bf16[256,768]{1,0:T(8,128)(2,1)} custom-call(s32[1]{0:T(128)} %after.8.index_ref, bf16[2048,128]{1,0:T(8,128)(2,1)} %place.6.cur_ref, bf16[128,256]{1,0:T(8,128)(2,1)} %pad_maximum_fusion.9.gram_ref, f32[2048,1]{1,0:T(8,128)} %multiply_subtract_fusion.size_ref, bf16[256,768]{1,0:T(8,128)(2,1)} %get-tuple-element.51.eq_ref, ...), custom_call_target="tpu_custom_call" | custom-call | flops 6442450944 | bytes 6291456 | tf_op jit(solution)/shard_map/attend/pallas_call | solution.py:436
  171.2 3.9 convolution_convert_fusion.1
  182.2 2.1 collective-permute-start.17
  189.3 21.5 %collective-permute-done.17.refs_0_.refs_15_.refs_11_ = bf16[384,1536]{1,0:T(8,128)(2,1)} collective-permute-done((bf16[384,1536]{1,0:T(8,128)(2,1)}, bf16[384,1536]{1,0:T(8,128)(2,1)}, u32[]{:S(2)}, u32[]{:S(2)}) %collective-permute-start.17) | collective-permute-done | bytes 1179680 | tf_op jit(solution)/shard_map/ppermute | solution.py:47
  218.2 6.5 %collective-permute-done.19.refs_6_ = bf16[64,3072]{1,0:T(8,128)(2,1)S(1)} collective-permute-done((bf16[64,3072]{1,0:T(8,128)(2,1)S(1)}, bf16[64,3072]{1,0:T(8,128)(2,1)S(1)}, u32[]{:S(2)}, u32[]{:S(2)}) %collective-permute-start.19) | collective-permute-done | bytes 393248 | tf_op jit(solution)/shard_map/ppermute | solution.py:47
  227.0 7.4 %collective-permute-done.20.refs_5_ = bf16[64,3072]{1,0:T(8,128)(2,1)S(1)} collective-permute-done((bf16[64,3072]{1,0:T(8,128)(2,1)S(1)}, bf16[64,3072]{1,0:T(8,128)(2,1)S(1)}, u32[]{:S(2)}, u32[]{:S(2)}) %collective-permute-start.20) | collective-permute-done | bytes 393248 | tf_op jit(solution)/shard_map/ppermute | solution.py:47
  236.7 6.6 %collective-permute-done.32.refs_3_ = bf16[64,3072]{1,0:T(8,128)(2,1)S(1)} collective-permute-done((bf16[64,3072]{1,0:T(8,128)(2,1)S(1)}, bf16[64,3072]{1,0:T(8,128)(2,1)S(1)}, u32[]{:S(2)}, u32[]{:S(2)}) %collective-permute-start.32) | collective-permute-done | bytes 393248 | tf_op jit(solution)/shard_map/ppermute | solution.py:47
  250.7 2.5 collective-permute-done.37
  258.0 15.0 %mlp.4 = (bf16[64,3072]{1,0:T(8,128)(2,1)}, bf16[64,3072]{1,0:T(8,128)(2,1)}, bf16[64,3072]{1,0:T(8,128)(2,1)}, bf16[64,3072]{1,0:T(8,128)(2,1)}, bf16[64,3072]{...) custom-call(s32[8]{0:T(128)} %stack.316.places, ...), custom_call_target="tpu_custom_call" | custom-call | flops 12079595520 | bytes 9437184 | tf_op jit(solution)/shard_map/mlp/pallas_call | solution.py:504
  273.1 12.5 %mlp.5 = (bf16[64,3072]{1,0:T(8,128)(2,1)}, bf16[64,3072]{1,0:T(8,128)(2,1)}, bf16[64,3072]{1,0:T(8,128)(2,1)}, bf16[64,3072]{1,0:T(8,128)(2,1)}, bf16[64,3072]{1,0:T(8,128)(2,1)}, /*index=5*/bf16[64,3072]{1,0:T(8,128)(2,1)}) custom-call(s32[8]{0:T(128)} %stack.316.places, bf16[64,3072]{1,0:T(8,128)(2,1)} %collective-permute-done.33.refs_0_, ...), custom_call_target="tpu_custom_call" | custom-call | flops 7247757312 | bytes 9437184 | tf_op jit(solution)/shard_map/mlp/pallas_call | solution.py:504
  293.3 6.0 %collective-permute-done.41 = bf16[32,3072]{1,0:T(8,128)(2,1)S(1)} collective-permute-done((bf16[32,3072]{1,0:T(8,128)(2,1)S(1)}, bf16[32,3072]{1,0:T(8,128)(2,1)S(1)}, u32[]{:S(2)}, u32[]{:S(2)}) %collective-permute-start.41) | collective-permute-done | bytes 196640 | tf_op jit(solution)/shard_map/ppermute | solution.py:47
  300.5 4.9 collective-permute-done.48
  306.6 8.2 %collective-permute-done.42 = bf16[64,3072]{1,0:T(8,128)(2,1)S(1)} collective-permute-done((bf16[64,3072]{1,0:T(8,128)(2,1)S(1)}, bf16[64,3072]{1,0:T(8,128)(2,1)S(1)}, u32[]{:S(2)}, u32[]{:S(2)}) %collective-permute-start.42) | collective-permute-done | bytes 393248 | tf_op jit(solution)/shard_map/ppermute | solution.py:47
  317.0 6.6 %collective-permute-done.49 = bf16[64,3072]{1,0:T(8,128)(2,1)S(1)} collective-permute-done((bf16[64,3072]{1,0:T(8,128)(2,1)S(1)}, bf16[64,3072]{1,0:T(8,128)(2,1)S(1)}, u32[]{:S(2)}, u32[]{:S(2)}) %collective-permute-start.49) | collective-permute-done | bytes 393248 | tf_op jit(solution)/shard_map/ppermute | solution.py:47
  326.8 5.2 collective-permute-done.50
  335.8 2.8 collective-permute-start.13
  338.6 2.4 collective-permute-done.51
  343.7 4.0 collective-permute-start.52
  348.2 3.6 collective-permute-start.55
  355.2 2.3 collective-permute-done.56.refs_5_
  363.1 3.5 collective-permute-done.59.refs_1_
  369.2 2.2 place.8.cur_ref
  371.4 12.3 %attend.3 = bf16[256,768]{1,0:T(8,128)(2,1)} custom-call(s32[1]{0:T(128)} %bitcast.36.value_ref.index_ref, bf16[2048,128]{1,0:T(8,128)(2,1)} %place.8.cur_ref, bf16[128,256]{1,0:T(8,128)(2,1)} %pad_maximum_fusion.9.gram_ref, f32[2048,1]{1,0:T(8,128)} %multiply_subtract_fusion.size_ref, bf16[256,768]{1,0:T(8,128)(2,1)} %get-tuple-element.51.eq_ref, ...), custom_call_target="tpu_custom_call" | custom-call | flops 6442450944 | bytes 6291456 | tf_op jit(solution)/shard_map/attend/pallas_call | solution.py:436
  383.7 3.9 convolution_convert_fusion
  393.2 9.8 %collective-permute-done.63 = bf16[64,3072]{1,0:T(8,128)(2,1)} collective-permute-done((bf16[64,3072]{1,0:T(8,128)(2,1)S(1)}, bf16[64,3072]{1,0:T(8,128)(2,1)}, u32[]{:S(2)}, u32[]{:S(2)}) %collective-permute-start.63) | collective-permute-done | bytes 393248 | tf_op jit(solution)/shard_map/ppermute | solution.py:47
  407.3 8.6 %collective-permute-done.64.refs_6_ = bf16[64,3072]{1,0:T(8,128)(2,1)S(1)} collective-permute-done((bf16[64,3072]{1,0:T(8,128)(2,1)S(1)}, bf16[64,3072]{1,0:T(8,128)(2,1)S(1)}, u32[]{:S(2)}, u32[]{:S(2)}) %collective-permute-start.64) | collective-permute-done | bytes 393248 | tf_op jit(solution)/shard_map/ppermute | solution.py:47
  417.9 7.6 %collective-permute-done.65.refs_5_ = bf16[64,3072]{1,0:T(8,128)(2,1)S(1)} collective-permute-done((bf16[64,3072]{1,0:T(8,128)(2,1)S(1)}, bf16[64,3072]{1,0:T(8,128)(2,1)S(1)}, u32[]{:S(2)}, u32[]{:S(2)}) %collective-permute-start.65) | collective-permute-done | bytes 393248 | tf_op jit(solution)/shard_map/ppermute | solution.py:47
  427.6 7.2 %collective-permute-done.76.refs_3_ = bf16[64,3072]{1,0:T(8,128)(2,1)S(1)} collective-permute-done((bf16[64,3072]{1,0:T(8,128)(2,1)S(1)}, bf16[64,3072]{1,0:T(8,128)(2,1)S(1)}, u32[]{:S(2)}, u32[]{:S(2)}) %collective-permute-start.76) | collective-permute-done | bytes 393248 | tf_op jit(solution)/shard_map/ppermute | solution.py:47
  437.8 2.6 collective-permute-done.80
  445.1 15.0 %mlp.6 = (bf16[64,3072]{1,0:T(8,128)(2,1)}, bf16[64,3072]{1,0:T(8,128)(2,1)}, bf16[64,3072]{1,0:T(8,128)(2,1)}, bf16[64,3072]{1,0:T(8,128)(2,1)}, bf16[64,3072]{...) custom-call(s32[8]{0:T(128)} %stack.316.places, ...), custom_call_target="tpu_custom_call" | custom-call | flops 12079595520 | bytes 9437184 | tf_op jit(solution)/shard_map/mlp/pallas_call | solution.py:504
  460.9 12.5 %mlp.7 = (bf16[64,3072]{1,0:T(8,128)(2,1)}, bf16[64,3072]{1,0:T(8,128)(2,1)}, bf16[64,3072]{1,0:T(8,128)(2,1)}, bf16[64,3072]{1,0:T(8,128)(2,1)}, bf16[64,3072]{1,0:T(8,128)(2,1)}, /*index=5*/bf16[64,3072]{1,0:T(8,128)(2,1)}) custom-call(s32[8]{0:T(128)} %stack.316.places, bf16[64,3072]{1,0:T(8,128)(2,1)} %copy-done.78, ...), custom_call_target="tpu_custom_call" | custom-call | flops 7247757312 | bytes 9437184 | tf_op jit(solution)/shard_map/mlp/pallas_call | solution.py:504
  482.3 5.2 collective-permute-done.85
  489.0 4.9 collective-permute-done.92
  495.8 7.8 %collective-permute-done.86 = bf16[64,3072]{1,0:T(8,128)(2,1)S(1)} collective-permute-done((bf16[64,3072]{1,0:T(8,128)(2,1)S(1)}, bf16[64,3072]{1,0:T(8,128)(2,1)S(1)}, u32[]{:S(2)}, u32[]{:S(2)}) %collective-permute-start.86) | collective-permute-done | bytes 393248 | tf_op jit(solution)/shard_map/ppermute | solution.py:47
  505.9 6.8 %collective-permute-done.93 = bf16[64,3072]{1,0:T(8,128)(2,1)S(1)} collective-permute-done((bf16[64,3072]{1,0:T(8,128)(2,1)S(1)}, bf16[64,3072]{1,0:T(8,128)(2,1)S(1)}, u32[]{:S(2)}, u32[]{:S(2)}) %collective-permute-start.93) | collective-permute-done | bytes 393248 | tf_op jit(solution)/shard_map/ppermute | solution.py:47
  515.2 6.8 %collective-permute-done.94 = bf16[64,3072]{1,0:T(8,128)(2,1)S(1)} collective-permute-done((bf16[64,3072]{1,0:T(8,128)(2,1)S(1)}, bf16[64,3072]{1,0:T(8,128)(2,1)S(1)}, u32[]{:S(2)}, u32[]{:S(2)}) %collective-permute-start.94) | collective-permute-done | bytes 393248 | tf_op jit(solution)/shard_map/ppermute | solution.py:47
  523.5 6.5 %collective-permute-done.95 = bf16[64,3072]{1,0:T(8,128)(2,1)S(1)} collective-permute-done((bf16[64,3072]{1,0:T(8,128)(2,1)S(1)}, bf16[64,3072]{1,0:T(8,128)(2,1)S(1)}, u32[]{:S(2)}, u32[]{:S(2)}) %collective-permute-start.95) | collective-permute-done | bytes 393248 | tf_op jit(solution)/shard_map/ppermute | solution.py:47
  533.9 5.0 collective-permute-done.96
  (451 shorter events, 155.8 us)
Async XLA Ops:
  0.9 26.4 %collective-permute-start.3 = (bf16[64,128]{1,0:T(8,128)(2,1)S(1)}, bf16[64,128]{1,0:T(8,128)(2,1)S(1)}, u32[]{:S(2)}, u32[]{:S(2)}) collective-permute-start(bf16[64,128]{1,0:T(8,128)(2,1)S(1)} %dynamic-slice_convert_fusion.2.refs_0_), channel_id=1, source_target_pairs={{0,28},{1,29},{2,30},{3,31},{4,0},{5,1},{6,2},{7,3},{8,4},{9,5},{1... | collective-permute-start | bytes 49160 | tf_op jit(solution)/shard_map/ppermute | solution.py:47
  6.9 22.2 %collective-permute-start.4 = (bf16[64,128]{1,0:T(8,128)(2,1)S(1)}, bf16[64,128]{1,0:T(8,128)(2,1)S(1)}, u32[]{:S(2)}, u32[]{:S(2)}) collective-permute-start(bf16[64,128]{1,0:T(8,128)(2,1)S(1)} %dynamic-slice_convert_fusion.2.refs_0_), channel_id=1, source_target_pairs={{0,24},{1,25},{2,26},{3,27},{4,28},{5,29},{6,30},{7,31},{8,0},{9,1... | collective-permute-start | bytes 49160 | tf_op jit(solution)/shard_map/ppermute | solution.py:47
  7.3 23.4 %collective-permute-start.5 = (bf16[64,128]{1,0:T(8,128)(2,1)S(1)}, bf16[64,128]{1,0:T(8,128)(2,1)S(1)}, u32[]{:S(2)}, u32[]{:S(2)}) collective-permute-start(bf16[64,128]{1,0:T(8,128)(2,1)S(1)} %dynamic-slice_convert_fusion.2.refs_0_), channel_id=1, source_target_pairs={{0,20},{1,21},{2,22},{3,23},{4,24},{5,25},{6,26},{7,27},{8,28},{9,... | collective-permute-start | bytes 49160 | tf_op jit(solution)/shard_map/ppermute | solution.py:47
  7.3 25.9 %collective-permute-start.6 = (bf16[64,128]{1,0:T(8,128)(2,1)S(1)}, bf16[64,128]{1,0:T(8,128)(2,1)S(1)}, u32[]{:S(2)}, u32[]{:S(2)}) collective-permute-start(bf16[64,128]{1,0:T(8,128)(2,1)S(1)} %dynamic-slice_convert_fusion.2.refs_0_), channel_id=1, source_target_pairs={{0,16},{1,17},{2,18},{3,19},{4,20},{5,21},{6,22},{7,23},{8,24},{9,... | collective-permute-start | bytes 49160 | tf_op jit(solution)/shard_map/ppermute | solution.py:47
  10.3 24.4 %collective-permute-start.7 = (bf16[64,128]{1,0:T(8,128)(2,1)S(1)}, bf16[64,128]{1,0:T(8,128)(2,1)S(1)}, u32[]{:S(2)}, u32[]{:S(2)}) collective-permute-start(bf16[64,128]{1,0:T(8,128)(2,1)S(1)} %dynamic-slice_convert_fusion.2.refs_0_), channel_id=1, source_target_pairs={{0,12},{1,13},{2,14},{3,15},{4,16},{5,17},{6,18},{7,19},{8,20},{9,... | collective-permute-start | bytes 49160 | tf_op jit(solution)/shard_map/ppermute | solution.py:47
  30.8 105.6 %collective-permute-start.1 = (bf16[384,1536]{1,0:T(8,128)(2,1)}, bf16[384,1536]{1,0:T(8,128)(2,1)}, u32[]{:S(2)}, u32[]{:S(2)}) collective-permute-start(bf16[384,1536]{1,0:T(8,128)(2,1)} %pad_maximum_fusion.1), channel_id=1, source_target_pairs={{0,16},{1,17},{2,18},{3,19},{4,20},{5,21},{6,22},{7,23},{8,24},{9,... | collective-permute-start | bytes 3538952 | tf_op jit(solution)/shard_map/ppermute | solution.py:47
  33.2 103.2 %collective-permute-start.2 = (bf16[384,1536]{1,0:T(8,128)(2,1)}, bf16[384,1536]{1,0:T(8,128)(2,1)}, u32[]{:S(2)}, u32[]{:S(2)}) collective-permute-start(bf16[384,1536]{1,0:T(8,128)(2,1)} %pad_maximum_fusion.2.refs_10_.refs_6_), channel_id=1, source_target_pairs={{0,4},{1,5},{2,6},{3,7},{4,0},{5,1},{6,2},{7,3},{8,12},{9,13},{10,... | collective-permute-start | bytes 3538952 | tf_op jit(solution)/shard_map/ppermute | solution.py:47
  34.7 75.4 %collective-permute-start = (bf16[384,1536]{1,0:T(8,128)(2,1)}, bf16[384,1536]{1,0:T(8,128)(2,1)}, u32[]{:S(2)}, u32[]{:S(2)}) collective-permute-start(bf16[384,1536]{1,0:T(8,128)(2,1)} %pad_maximum_fusion), channel_id=1, source_target_pairs={{0,8},{1,9},{2,10},{3,11},{4,12},{5,13},{6,14},{7,15},{8,0},{9,1},... | collective-permute-start | bytes 3538952 | tf_op jit(solution)/shard_map/ppermute | solution.py:47
  35.6 121.6 %collective-permute-start.14 = (bf16[384,1536]{1,0:T(8,128)(2,1)}, bf16[384,1536]{1,0:T(8,128)(2,1)}, u32[]{:S(2)}, u32[]{:S(2)}) collective-permute-start(bf16[384,1536]{1,0:T(8,128)(2,1)} %pad_maximum_fusion.3), channel_id=1, source_target_pairs={{0,24},{1,25},{2,26},{3,27},{4,28},{5,29},{6,30},{7,31},{8,16},{9,... | collective-permute-start | bytes 3538952 | tf_op jit(solution)/shard_map/ppermute | solution.py:47
  110.0 47.1 %collective-permute-start.15 = (bf16[384,1536]{1,0:T(8,128)(2,1)}, bf16[384,1536]{1,0:T(8,128)(2,1)}, u32[]{:S(2)}, u32[]{:S(2)}) collective-permute-start(bf16[384,1536]{1,0:T(8,128)(2,1)} %collective-permute-done.refs_0_.refs_12_.refs_8_), channel_id=1, source_target_pairs={{0,4},{1,5},{2,6},{3,7},{4,0},{5,1},{6,2},{7,3},{8,12},{9,13},{10,... | collective-permute-start | bytes 3538952 | tf_op jit(solution)/shard_map/ppermute | solution.py:47
  182.2 28.5 %collective-permute-start.17 = (bf16[384,1536]{1,0:T(8,128)(2,1)}, bf16[384,1536]{1,0:T(8,128)(2,1)}, u32[]{:S(2)}, u32[]{:S(2)}) collective-permute-start(bf16[384,1536]{1,0:T(8,128)(2,1)} %collective-permute-done.1.refs_1_.refs_14_.refs_10_), channel_id=1, source_target_pairs={{0,4},{1,5},{2,6},{3,7},{4,0},{5,1},{6,2},{7,3},{8,12},{9,13},{10,... | collective-permute-start | bytes 3538952 | tf_op jit(solution)/shard_map/ppermute | solution.py:47
  186.8 25.2 %collective-permute-start.18 = (bf16[64,3072]{1,0:T(8,128)(2,1)}, bf16[64,3072]{1,0:T(8,128)(2,1)}, u32[]{:S(2)}, u32[]{:S(2)}) collective-permute-start(bf16[64,3072]{1,0:T(8,128)(2,1)} %fusion.9), channel_id=1, source_target_pairs={{0,2},{1,3},{2,0},{3,1},{4,6},{5,7},{6,4},{7,5},{8,10},{9,11},{10,... | collective-permute-start | bytes 1179656 | tf_op jit(solution)/shard_map/ppermute | solution.py:47
  214.2 10.5 %collective-permute-start.19 = (bf16[64,3072]{1,0:T(8,128)(2,1)S(1)}, bf16[64,3072]{1,0:T(8,128)(2,1)S(1)}, u32[]{:S(2)}, u32[]{:S(2)}) collective-permute-start(bf16[64,3072]{1,0:T(8,128)(2,1)S(1)} %multiply_convert_fusion.3.refs_7_), channel_id=1, source_target_pairs={{0,8},{1,9},{2,0},{3,1},{4,12},{5,13},{6,4},{7,5},{8,16},{9,17},{1... | collective-permute-start | bytes 1179656 | tf_op jit(solution)/shard_map/ppermute | solution.py:47
  215.0 10.5 %collective-permute-start.24 = (bf16[64,3072]{1,0:T(8,128)(2,1)S(1)}, bf16[64,3072]{1,0:T(8,128)(2,1)S(1)}, u32[]{:S(2)}, u32[]{:S(2)}) collective-permute-start(bf16[64,3072]{1,0:T(8,128)(2,1)S(1)} %multiply_convert_fusion.3.refs_7_), channel_id=1, source_target_pairs={{0,2},{1,3},{2,10},{3,11},{4,6},{5,7},{6,14},{7,15},{8,0},{9,1},{1... | collective-permute-start | bytes 1179656 | tf_op jit(solution)/shard_map/ppermute | solution.py:47
  216.5 33.0 %collective-permute-start.28 = (bf16[384,1536]{1,0:T(8,128)(2,1)}, bf16[384,1536]{1,0:T(8,128)(2,1)}, u32[]{:S(2)}, u32[]{:S(2)}) collective-permute-start(bf16[384,1536]{1,0:T(8,128)(2,1)} %collective-permute-done.14.refs_0_.refs_16_.refs_12_), channel_id=1, source_target_pairs={{0,4},{1,5},{2,6},{3,7},{4,0},{5,1},{6,2},{7,3},{8,12},{9,13},{10,... | collective-permute-start | bytes 3538952 | tf_op jit(solution)/shard_map/ppermute | solution.py:47
  224.8 9.7 %collective-permute-start.20 = (bf16[64,3072]{1,0:T(8,128)(2,1)S(1)}, bf16[64,3072]{1,0:T(8,128)(2,1)S(1)}, u32[]{:S(2)}, u32[]{:S(2)}) collective-permute-start(bf16[64,3072]{1,0:T(8,128)(2,1)S(1)} %collective-permute-done.19.refs_6_), channel_id=1, source_target_pairs={{0,8},{1,9},{2,0},{3,1},{4,12},{5,13},{6,4},{7,5},{8,16},{9,17},{1... | collective-permute-start | bytes 1179656 | tf_op jit(solution)/shard_map/ppermute | solution.py:47
  225.5 9.7 %collective-permute-start.26 = (bf16[64,3072]{1,0:T(8,128)(2,1)S(1)}, bf16[64,3072]{1,0:T(8,128)(2,1)S(1)}, u32[]{:S(2)}, u32[]{:S(2)}) collective-permute-start(bf16[64,3072]{1,0:T(8,128)(2,1)S(1)} %collective-permute-done.24.refs_8_), channel_id=1, source_target_pairs={{0,2},{1,3},{2,10},{3,11},{4,6},{5,7},{6,14},{7,15},{8,0},{9,1},{1... | collective-permute-start | bytes 1179656 | tf_op jit(solution)/shard_map/ppermute | solution.py:47
  235.1 10.5 %collective-permute-start.34 = (bf16[64,3072]{1,0:T(8,128)(2,1)S(1)}, bf16[64,3072]{1,0:T(8,128)(2,1)S(1)}, u32[]{:S(2)}, u32[]{:S(2)}) collective-permute-start(bf16[64,3072]{1,0:T(8,128)(2,1)S(1)} %collective-permute-done.26.refs_9_), channel_id=1, source_target_pairs={{0,2},{1,3},{2,10},{3,11},{4,6},{5,7},{6,14},{7,15},{8,0},{9,1},{1... | collective-permute-start | bytes 1179656 | tf_op jit(solution)/shard_map/ppermute | solution.py:47
  255.2 17.8 %collective-permute-start.33 = (bf16[64,3072]{1,0:T(8,128)(2,1)}, bf16[64,3072]{1,0:T(8,128)(2,1)}, u32[]{:S(2)}, u32[]{:S(2)}) collective-permute-start(bf16[64,3072]{1,0:T(8,128)(2,1)} %copy-done.36), channel_id=1, source_target_pairs={{0,1},{1,0},{2,3},{3,2},{4,5},{5,4},{6,7},{7,6},{8,9},{9,8},{10,11... | collective-permute-start | bytes 1179656 | tf_op jit(solution)/shard_map/ppermute | solution.py:47
  255.8 17.3 %collective-permute-start.35 = (bf16[64,3072]{1,0:T(8,128)(2,1)}, bf16[64,3072]{1,0:T(8,128)(2,1)}, u32[]{:S(2)}, u32[]{:S(2)}) collective-permute-start(bf16[64,3072]{1,0:T(8,128)(2,1)} %copy-done.37), channel_id=1, source_target_pairs={{0,1},{1,0},{2,3},{3,2},{4,5},{5,4},{6,7},{7,6},{8,9},{9,8},{10,11... | collective-permute-start | bytes 1179656 | tf_op jit(solution)/shard_map/ppermute | solution.py:47
  256.5 16.5 %collective-permute-start.38 = (bf16[64,3072]{1,0:T(8,128)(2,1)S(1)}, bf16[64,3072]{1,0:T(8,128)(2,1)}, u32[]{:S(2)}, u32[]{:S(2)}) collective-permute-start(bf16[64,3072]{1,0:T(8,128)(2,1)S(1)} %constant_dynamic-update-slice_fusion.refs_5_), channel_id=1, source_target_pairs={{0,1},{1,0},{2,3},{3,2},{4,5},{5,4},{6,7},{7,6},{8,9},{9,8},{10,11... | collective-permute-start | bytes 1179656 | tf_op jit(solution)/shard_map/ppermute | solution.py:47
  285.8 30.3 %collective-permute-start.46 = (bf16[64,3072]{1,0:T(8,128)(2,1)}, bf16[64,3072]{1,0:T(8,128)(2,1)S(1)}, u32[]{:S(2)}, u32[]{:S(2)}) collective-permute-start(bf16[64,3072]{1,0:T(8,128)(2,1)} %get-tuple-element.65.refs_14_), channel_id=1, source_target_pairs={{0,1},{1,0},{2,3},{3,2},{4,5},{5,4},{6,7},{7,6},{8,9},{9,8},{10,11... | collective-permute-start | bytes 1179656 | tf_op jit(solution)/shard_map/ppermute | solution.py:47
  286.2 20.4 %collective-permute-start.31 = (bf16[64,3072]{1,0:T(8,128)(2,1)}, bf16[64,3072]{1,0:T(8,128)(2,1)S(1)}, u32[]{:S(2)}, u32[]{:S(2)}) collective-permute-start(bf16[64,3072]{1,0:T(8,128)(2,1)} %get-tuple-element.64), channel_id=1, source_target_pairs={{0,1},{1,0},{2,3},{3,2},{4,5},{5,4},{6,7},{7,6},{8,9},{9,8},{10,11... | collective-permute-start | bytes 1179656 | tf_op jit(solution)/shard_map/ppermute | solution.py:47
  286.3 38.9 %collective-permute-start.30 = (bf16[64,3072]{1,0:T(8,128)(2,1)}, bf16[64,3072]{1,0:T(8,128)(2,1)S(1)}, u32[]{:S(2)}, u32[]{:S(2)}) collective-permute-start(bf16[64,3072]{1,0:T(8,128)(2,1)} %get-tuple-element.62), channel_id=1, source_target_pairs={{0,1},{1,0},{2,3},{3,2},{4,5},{5,4},{6,7},{7,6},{8,9},{9,8},{10,11... | collective-permute-start | bytes 1179656 | tf_op jit(solution)/shard_map/ppermute | solution.py:47
  286.7 40.1 %collective-permute-start.45 = (bf16[64,3072]{1,0:T(8,128)(2,1)S(1)}, bf16[64,3072]{1,0:T(8,128)(2,1)S(1)}, u32[]{:S(2)}, u32[]{:S(2)}) collective-permute-start(bf16[64,3072]{1,0:T(8,128)(2,1)S(1)} %copy-done.64), channel_id=1, source_target_pairs={{0,1},{1,0},{2,3},{3,2},{4,5},{5,4},{6,7},{7,6},{8,9},{9,8},{10,11... | collective-permute-start | bytes 1179656 | tf_op jit(solution)/shard_map/ppermute | solution.py:47
  305.4 9.4 %collective-permute-start.42 = (bf16[64,3072]{1,0:T(8,128)(2,1)S(1)}, bf16[64,3072]{1,0:T(8,128)(2,1)S(1)}, u32[]{:S(2)}, u32[]{:S(2)}) collective-permute-start(bf16[64,3072]{1,0:T(8,128)(2,1)S(1)} %pad_maximum_fusion.5), channel_id=1, source_target_pairs={{0,8},{1,9},{2,0},{3,1},{4,12},{5,13},{6,4},{7,5},{8,16},{9,17},{1... | collective-permute-start | bytes 1179656 | tf_op jit(solution)/shard_map/ppermute | solution.py:47
  306.5 32.1 %collective-permute-start.29 = (bf16[64,3072]{1,0:T(8,128)(2,1)}, bf16[64,3072]{1,0:T(8,128)(2,1)}, u32[]{:S(2)}, u32[]{:S(2)}) collective-permute-start(bf16[64,3072]{1,0:T(8,128)(2,1)} %get-tuple-element.60), channel_id=1, source_target_pairs={{0,1},{1,0},{2,3},{3,2},{4,5},{5,4},{6,7},{7,6},{8,9},{9,8},{10,11... | collective-permute-start | bytes 1179656 | tf_op jit(solution)/shard_map/ppermute | solution.py:47
  316.1 9.1 %collective-permute-start.43 = (bf16[64,3072]{1,0:T(8,128)(2,1)S(1)}, bf16[64,3072]{1,0:T(8,128)(2,1)S(1)}, u32[]{:S(2)}, u32[]{:S(2)}) collective-permute-start(bf16[64,3072]{1,0:T(8,128)(2,1)S(1)} %add_convert_fusion.8), channel_id=1, source_target_pairs={{0,8},{1,9},{2,0},{3,1},{4,12},{5,13},{6,4},{7,5},{8,16},{9,17},{1... | collective-permute-start | bytes 1179656 | tf_op jit(solution)/shard_map/ppermute | solution.py:47
  326.1 12.5 %collective-permute-start.44 = (bf16[64,3072]{1,0:T(8,128)(2,1)}, bf16[64,3072]{1,0:T(8,128)(2,1)}, u32[]{:S(2)}, u32[]{:S(2)}) collective-permute-start(bf16[64,3072]{1,0:T(8,128)(2,1)} %add_convert_fusion.7), channel_id=1, source_target_pairs={{0,8},{1,9},{2,0},{3,1},{4,12},{5,13},{6,4},{7,5},{8,16},{9,17},{1... | collective-permute-start | bytes 1179656 | tf_op jit(solution)/shard_map/ppermute | solution.py:47
  391.5 11.6 %collective-permute-start.63 = (bf16[64,3072]{1,0:T(8,128)(2,1)S(1)}, bf16[64,3072]{1,0:T(8,128)(2,1)}, u32[]{:S(2)}, u32[]{:S(2)}) collective-permute-start(bf16[64,3072]{1,0:T(8,128)(2,1)S(1)} %fusion.10), channel_id=1, source_target_pairs={{0,2},{1,3},{2,0},{3,1},{4,6},{5,7},{6,4},{7,5},{8,10},{9,11},{10,... | collective-permute-start | bytes 1179656 | tf_op jit(solution)/shard_map/ppermute | solution.py:47
  405.2 10.6 %collective-permute-start.64 = (bf16[64,3072]{1,0:T(8,128)(2,1)S(1)}, bf16[64,3072]{1,0:T(8,128)(2,1)S(1)}, u32[]{:S(2)}, u32[]{:S(2)}) collective-permute-start(bf16[64,3072]{1,0:T(8,128)(2,1)S(1)} %multiply_convert_fusion.1.refs_7_), channel_id=1, source_target_pairs={{0,8},{1,9},{2,0},{3,1},{4,12},{5,13},{6,4},{7,5},{8,16},{9,17},{1... | collective-permute-start | bytes 1179656 | tf_op jit(solution)/shard_map/ppermute | solution.py:47
  405.3 11.0 %collective-permute-start.69 = (bf16[64,3072]{1,0:T(8,128)(2,1)S(1)}, bf16[64,3072]{1,0:T(8,128)(2,1)S(1)}, u32[]{:S(2)}, u32[]{:S(2)}) collective-permute-start(bf16[64,3072]{1,0:T(8,128)(2,1)S(1)} %multiply_convert_fusion.1.refs_7_), channel_id=1, source_target_pairs={{0,2},{1,3},{2,10},{3,11},{4,6},{5,7},{6,14},{7,15},{8,0},{9,1},{1... | collective-permute-start | bytes 1179656 | tf_op jit(solution)/shard_map/ppermute | solution.py:47
  415.9 9.7 %collective-permute-start.65 = (bf16[64,3072]{1,0:T(8,128)(2,1)S(1)}, bf16[64,3072]{1,0:T(8,128)(2,1)S(1)}, u32[]{:S(2)}, u32[]{:S(2)}) collective-permute-start(bf16[64,3072]{1,0:T(8,128)(2,1)S(1)} %collective-permute-done.64.refs_6_), channel_id=1, source_target_pairs={{0,8},{1,9},{2,0},{3,1},{4,12},{5,13},{6,4},{7,5},{8,16},{9,17},{1... | collective-permute-start | bytes 1179656 | tf_op jit(solution)/shard_map/ppermute | solution.py:47
  416.3 9.8 %collective-permute-start.71 = (bf16[64,3072]{1,0:T(8,128)(2,1)S(1)}, bf16[64,3072]{1,0:T(8,128)(2,1)S(1)}, u32[]{:S(2)}, u32[]{:S(2)}) collective-permute-start(bf16[64,3072]{1,0:T(8,128)(2,1)S(1)} %collective-permute-done.69.refs_8_), channel_id=1, source_target_pairs={{0,2},{1,3},{2,10},{3,11},{4,6},{5,7},{6,14},{7,15},{8,0},{9,1},{1... | collective-permute-start | bytes 1179656 | tf_op jit(solution)/shard_map/ppermute | solution.py:47
  425.5 9.2 %collective-permute-start.76 = (bf16[64,3072]{1,0:T(8,128)(2,1)S(1)}, bf16[64,3072]{1,0:T(8,128)(2,1)S(1)}, u32[]{:S(2)}, u32[]{:S(2)}) collective-permute-start(bf16[64,3072]{1,0:T(8,128)(2,1)S(1)} %collective-permute-done.65.refs_5_), channel_id=1, source_target_pairs={{0,8},{1,9},{2,0},{3,1},{4,12},{5,13},{6,4},{7,5},{8,16},{9,17},{1... | collective-permute-start | bytes 1179656 | tf_op jit(solution)/shard_map/ppermute | solution.py:47
  426.1 9.3 %collective-permute-start.78 = (bf16[64,3072]{1,0:T(8,128)(2,1)S(1)}, bf16[64,3072]{1,0:T(8,128)(2,1)S(1)}, u32[]{:S(2)}, u32[]{:S(2)}) collective-permute-start(bf16[64,3072]{1,0:T(8,128)(2,1)S(1)} %collective-permute-done.71.refs_9_), channel_id=1, source_target_pairs={{0,2},{1,3},{2,10},{3,11},{4,6},{5,7},{6,14},{7,15},{8,0},{9,1},{1... | collective-permute-start | bytes 1179656 | tf_op jit(solution)/shard_map/ppermute | solution.py:47
  442.9 17.2 %collective-permute-start.77 = (bf16[64,3072]{1,0:T(8,128)(2,1)S(1)}, bf16[64,3072]{1,0:T(8,128)(2,1)S(1)}, u32[]{:S(2)}, u32[]{:S(2)}) collective-permute-start(bf16[64,3072]{1,0:T(8,128)(2,1)S(1)} %collective-permute-done.76.refs_3_), channel_id=1, source_target_pairs={{0,1},{1,0},{2,3},{3,2},{4,5},{5,4},{6,7},{7,6},{8,9},{9,8},{10,11... | collective-permute-start | bytes 1179656 | tf_op jit(solution)/shard_map/ppermute | solution.py:47
  443.5 16.7 %collective-permute-start.79 = (bf16[64,3072]{1,0:T(8,128)(2,1)S(1)}, bf16[64,3072]{1,0:T(8,128)(2,1)}, u32[]{:S(2)}, u32[]{:S(2)}) collective-permute-start(bf16[64,3072]{1,0:T(8,128)(2,1)S(1)} %collective-permute-done.78.refs_4_), channel_id=1, source_target_pairs={{0,1},{1,0},{2,3},{3,2},{4,5},{5,4},{6,7},{7,6},{8,9},{9,8},{10,11... | collective-permute-start | bytes 1179656 | tf_op jit(solution)/shard_map/ppermute | solution.py:47
  443.6 16.6 %collective-permute-start.82 = (bf16[64,3072]{1,0:T(8,128)(2,1)}, bf16[64,3072]{1,0:T(8,128)(2,1)}, u32[]{:S(2)}, u32[]{:S(2)}) collective-permute-start(bf16[64,3072]{1,0:T(8,128)(2,1)} %constant_dynamic-update-slice_fusion.2.refs_5_), channel_id=1, source_target_pairs={{0,1},{1,0},{2,3},{3,2},{4,5},{5,4},{6,7},{7,6},{8,9},{9,8},{10,11... | collective-permute-start | bytes 1179656 | tf_op jit(solution)/shard_map/ppermute | solution.py:47
  474.0 31.1 %collective-permute-start.90 = (bf16[64,3072]{1,0:T(8,128)(2,1)}, bf16[64,3072]{1,0:T(8,128)(2,1)S(1)}, u32[]{:S(2)}, u32[]{:S(2)}) collective-permute-start(bf16[64,3072]{1,0:T(8,128)(2,1)} %get-tuple-element.81.refs_14_), channel_id=1, source_target_pairs={{0,1},{1,0},{2,3},{3,2},{4,5},{5,4},{6,7},{7,6},{8,9},{9,8},{10,11... | collective-permute-start | bytes 1179656 | tf_op jit(solution)/shard_map/ppermute | solution.py:47
  474.1 21.6 %collective-permute-start.75 = (bf16[64,3072]{1,0:T(8,128)(2,1)}, bf16[64,3072]{1,0:T(8,128)(2,1)S(1)}, u32[]{:S(2)}, u32[]{:S(2)}) collective-permute-start(bf16[64,3072]{1,0:T(8,128)(2,1)} %get-tuple-element.80), channel_id=1, source_target_pairs={{0,1},{1,0},{2,3},{3,2},{4,5},{5,4},{6,7},{7,6},{8,9},{9,8},{10,11... | collective-permute-start | bytes 1179656 | tf_op jit(solution)/shard_map/ppermute | solution.py:47
  474.5 39.7 %collective-permute-start.74 = (bf16[64,3072]{1,0:T(8,128)(2,1)S(1)}, bf16[64,3072]{1,0:T(8,128)(2,1)S(1)}, u32[]{:S(2)}, u32[]{:S(2)}) collective-permute-start(bf16[64,3072]{1,0:T(8,128)(2,1)S(1)} %copy-done.65), channel_id=1, source_target_pairs={{0,1},{1,0},{2,3},{3,2},{4,5},{5,4},{6,7},{7,6},{8,9},{9,8},{10,11... | collective-permute-start | bytes 1179656 | tf_op jit(solution)/shard_map/ppermute | solution.py:47
  474.6 40.6 %collective-permute-start.89 = (bf16[64,3072]{1,0:T(8,128)(2,1)S(1)}, bf16[64,3072]{1,0:T(8,128)(2,1)S(1)}, u32[]{:S(2)}, u32[]{:S(2)}) collective-permute-start(bf16[64,3072]{1,0:T(8,128)(2,1)S(1)} %copy-done.63), channel_id=1, source_target_pairs={{0,1},{1,0},{2,3},{3,2},{4,5},{5,4},{6,7},{7,6},{8,9},{9,8},{10,11... | collective-permute-start | bytes 1179656 | tf_op jit(solution)/shard_map/ppermute | solution.py:47
  493.9 9.8 %collective-permute-start.86 = (bf16[64,3072]{1,0:T(8,128)(2,1)S(1)}, bf16[64,3072]{1,0:T(8,128)(2,1)S(1)}, u32[]{:S(2)}, u32[]{:S(2)}) collective-permute-start(bf16[64,3072]{1,0:T(8,128)(2,1)S(1)} %pad_maximum_fusion.7), channel_id=1, source_target_pairs={{0,8},{1,9},{2,0},{3,1},{4,12},{5,13},{6,4},{7,5},{8,16},{9,17},{1... | collective-permute-start | bytes 1179656 | tf_op jit(solution)/shard_map/ppermute | solution.py:47
  495.7 27.7 %collective-permute-start.73 = (bf16[64,3072]{1,0:T(8,128)(2,1)S(1)}, bf16[64,3072]{1,0:T(8,128)(2,1)S(1)}, u32[]{:S(2)}, u32[]{:S(2)}) collective-permute-start(bf16[64,3072]{1,0:T(8,128)(2,1)S(1)} %copy-done.62), channel_id=1, source_target_pairs={{0,1},{1,0},{2,3},{3,2},{4,5},{5,4},{6,7},{7,6},{8,9},{9,8},{10,11... | collective-permute-start | bytes 1179656 | tf_op jit(solution)/shard_map/ppermute | solution.py:47
  505.1 9.1 %collective-permute-start.87 = (bf16[64,3072]{1,0:T(8,128)(2,1)S(1)}, bf16[64,3072]{1,0:T(8,128)(2,1)S(1)}, u32[]{:S(2)}, u32[]{:S(2)}) collective-permute-start(bf16[64,3072]{1,0:T(8,128)(2,1)S(1)} %add_convert_fusion.3), channel_id=1, source_target_pairs={{0,8},{1,9},{2,0},{3,1},{4,12},{5,13},{6,4},{7,5},{8,16},{9,17},{1... | collective-permute-start | bytes 1179656 | tf_op jit(solution)/shard_map/ppermute | solution.py:47
  512.9 9.1 %collective-permute-start.94 = (bf16[64,3072]{1,0:T(8,128)(2,1)S(1)}, bf16[64,3072]{1,0:T(8,128)(2,1)S(1)}, u32[]{:S(2)}, u32[]{:S(2)}) collective-permute-start(bf16[64,3072]{1,0:T(8,128)(2,1)S(1)} %add_convert_fusion.1), channel_id=1, source_target_pairs={{0,2},{1,3},{2,10},{3,11},{4,6},{5,7},{6,14},{7,15},{8,0},{9,1},{1... | collective-permute-start | bytes 1179656 | tf_op jit(solution)/shard_map/ppermute | solution.py:47
  514.4 9.1 %collective-permute-start.88 = (bf16[64,3072]{1,0:T(8,128)(2,1)S(1)}, bf16[64,3072]{1,0:T(8,128)(2,1)S(1)}, u32[]{:S(2)}, u32[]{:S(2)}) collective-permute-start(bf16[64,3072]{1,0:T(8,128)(2,1)S(1)} %add_convert_fusion.2), channel_id=1, source_target_pairs={{0,8},{1,9},{2,0},{3,1},{4,12},{5,13},{6,4},{7,5},{8,16},{9,17},{1... | collective-permute-start | bytes 1179656 | tf_op jit(solution)/shard_map/ppermute | solution.py:47
  (138 other events, 1278.5 us)

commit v4 on v3

--- a/solution.py
+++ b/solution.py
@@ -14,6 +14,7 @@
 BLOCKS = 2
 STRIP = 256
 CHUNK = 1024
+MLP_ROWS = 320
 HEADS_A_STEP = 2
 BF16, F32 = jnp.bfloat16, jnp.float32
 
@@ -140,14 +141,16 @@
     for j in range(1, half):
         ahead, back = grid.ring_step(ahead, 1), grid.ring_step(back, -1)
         pieces[-j], pieces[j] = ahead, back
+    swapped = {j: grid.core_swap(pieces[j]) for j in range(-half // 2, half // 2 + 1) if abs(j) < half - 2}
+    zero = after(grid.s, list(swapped.values())) - grid.s
     pieces[half] = jnp.concatenate(
         [
-            grid.ring_step(ahead[:cut], 1),
-            grid.ring_step(back[cut:], -1),
+            grid.ring_step(lax.dynamic_slice_in_dim(ahead, zero, cut), 1),
+            grid.ring_step(lax.dynamic_slice_in_dim(back, zero + cut, cut), -1),
         ],
         axis=0,
     )
-    return pieces
+    return pieces, swapped
 
 
 def reduce_ring(grid, terms):
@@ -457,9 +460,9 @@
     )(index.reshape(1).astype(jnp.int32), current, gram, size, eq, aq, ak, av, ek_one, ek_two, ev_one, ev_two, cross_one, cross_two)
 
 
-def mlp_kernel(count, parts, gates, per_tile, places, *refs):
+def mlp_kernel(count, parts, per_tile, places, *refs):
     pieces, refs = refs[:count], refs[count:]
-    parts, refs = refs[:parts], refs[parts + gates :]
+    parts, refs = refs[:parts], refs[parts:]
     outs, (up, down, up_sem, down_sem) = refs[:count], refs[count:]
     width, chunk = up.shape
     ups, downs = [], []
@@ -495,17 +498,17 @@
             outs[i][...] = terms[n * sub : (n + 1) * sub]
 
 
-def mlp(pieces, weights, gates=()):
+def mlp(pieces, weights):
     places, parts = weights
     count, (sub, width) = len(pieces), pieces[0].shape
     chunk = parts[0].shape[1] if parts[0].shape[0] == width else parts[0].shape[1] // 2
     vmem = pl.BlockSpec(memory_space=pltpu.VMEM)
     anywhere = pl.BlockSpec(memory_space=pl.ANY)
     return pl.pallas_call(
-        functools.partial(mlp_kernel, count, len(parts), len(gates), max(1, 320 // sub)),
+        functools.partial(mlp_kernel, count, len(parts), max(1, MLP_ROWS // sub)),
         in_specs=[pl.BlockSpec(memory_space=pltpu.SMEM)]
         + [vmem] * count
-        + [anywhere] * (len(parts) + len(gates)),
+        + [anywhere] * len(parts),
         out_specs=[vmem] * count,
         out_shape=[jax.ShapeDtypeStruct((sub, width), BF16)] * count,
         scratch_shapes=[
@@ -521,7 +524,7 @@
             transcendentals=0,
         ),
         name="mlp",
-    )(places, *pieces, *parts, *gates)
+    )(places, *pieces, *parts)
 
 
 def per_device(
@@ -557,8 +560,9 @@
         over_seq=over_seq,
         gates=arrivals[:early] + [own_swap, two[0]],
     )
-    early_swaps = [weights.swap(j) for j in range(1, early + 1)]
-    turn = after(grid.s, arrivals[early:] + early_swaps[:1])
+    turn = grid.s
+    for j in range(1, early + 1):
+        weights.swap(j)
     next_row = grid.seq_shift(latent[:1], -1)
     latent_next = lax.dynamic_slice_in_dim(
         jnp.concatenate([latent, next_row]), grid.h * sub + 1, sub
@@ -582,7 +586,8 @@
         stream_in = jnp.dot(own_rows, w_in, preferred_element_type=F32) + embedding
         zero = 0
         if step_index == 0:
-            zero = after(grid.s, early_swaps[1:]) - grid.s
+            swaps = [weights.swapped[j] for j in range(1, early + 1)]
+            zero = after(grid.s, arrivals[early:] + swaps[:1]) - grid.s
             for j in range(early + 1, grid.outer):
                 weights.swap(j)
         stream_attn = stream_in + reduce_head(
@@ -590,20 +595,16 @@
             jnp.dot(attended, w_attn_out, preferred_element_type=F32).astype(BF16),
             zero,
         )
-        pieces = gather_ring(grid, layer_norm(stream_attn, gain_mlp).astype(BF16))
+        pieces, swapped = gather_ring(grid, layer_norm(stream_attn, gain_mlp).astype(BF16))
         if step_index == 0:
             parts = weights.parts()
-        half = max(pieces)
-        terms, gates = {}, ()
-        for part in (
-            [k for k in sorted(pieces) if abs(k) <= half // 2],
-            [k for k in sorted(pieces) if abs(k) > half // 2],
-        ):
-            others = [grid.core_swap(pieces[k]) for k in part]
-            made = mlp(others + [pieces[k] for k in part], parts, gates)
-            gates = (made[0],)
-            for k, other, mine in zip(part, made, made[len(part) :]):
-                terms[k] = mine.astype(F32) + grid.core_swap(other).astype(F32)
+        order = sorted(pieces)
+        others = [swapped.get(k) for k in order]
+        others = [grid.core_swap(pieces[k]) if o is None else o for k, o in zip(order, others)]
+        made = mlp(others + [pieces[k] for k in order], parts)
+        terms = {}
+        for k, other, mine in zip(order, made, made[len(order) :]):
+            terms[k] = mine.astype(F32) + grid.core_swap(other).astype(F32)
         stream_mlp = stream_attn + reduce_ring(grid, terms)
         final = layer_norm(stream_mlp, gain_final).astype(BF16)
         params = jnp.dot(final, w_final, preferred_element_type=F32)

time: 553 us -> 542 us (0.980)
  Pallas kernels: 141 us -> 126 us
  starting transfers between devices: 92.2 us -> 103 us
    pallas_call x4 -> x2, Pallas kernels: 55 us -> 39.6 us  [mlp(): pl.pallas_call(functools.partial(mlp_kernel, count, len(parts), max(1, ML...]
    ppermute x101, starting transfers between devices: 92.2 us -> 103 us  [move(): return lax.ppermute(value, ('seq', 'head'), route)]
    unnamed x172 -> x144, local copies, waits for them, and re-layouts: 15.2 us -> 9.55 us
  transfers between devices with their start and end apart: 101 -> 101, of which waited for: 45 -> 45; matrix products, arithmetic and copies ran while one was open for 9% -> 9% of each run, Pallas kernels for 16% -> 10%
where the time goes in v4:
time: 542 us; the launch traced here: 537 us
  waiting for transfers between devices  220 us (41%)
  Pallas kernels  126 us (23%)
  starting transfers between devices  103 us (19%)
  local copies, waits for them, and re-layouts  32.1 us (6%)
  other arithmetic  26.8 us (5%)
  between operations  15.4 us (3%)
  matrix products  14.5 us (3%)
    ppermute x101, waiting for transfers between devices, move(): return lax.ppermute(value, ('seq', 'head'), route)  220 us
    ppermute x101, starting transfers between devices, move(): return lax.ppermute(value, ('seq', 'head'), route)  103 us
    pallas_call x2, Pallas kernels, embed_products(): pl.pallas_call(functools.partial(embed_kernel, count, with_query), grid_s...  48.8 us
    pallas_call x2, Pallas kernels, mlp(): pl.pallas_call(functools.partial(mlp_kernel, count, len(parts), max(1, ML...  39.6 us
    pallas_call x2, Pallas kernels, attend(): pl.pallas_call(functools.partial(attend_kernel, width, HEAD_DIM ** (-0.5)...  24.8 us
  transfers between devices with their start and end apart: 101, of which 45 were waited for; matrix products, arithmetic and copies ran while one was open for 9% of the time, Pallas kernels for 10%

profile of v4, /device:TPU:0, one launch (start us, length us, event | category | flops | bytes accessed | tf_op | source)
XLA Modules:
  0.0 536.6 jit_solution(15041104271037296525)
XLA Ops:
  0.9 6.0 %collective-permute-start.3 = (bf16[64,128]{1,0:T(8,128)(2,1)S(1)}, bf16[64,128]{1,0:T(8,128)(2,1)S(1)}, u32[]{:S(2)}, u32[]{:S(2)}) collective-permute-start(bf16[64,128]{1,0:T(8,128)(2,1)S(1)} %dynamic-slice_convert_fusion.2.refs_0_), channel_id=1, source_target_pairs={{0,28},{1,29},{2,30},{3,31},{4,0},{5,1},{6,2},{7,3},{8,4},{9,5},{1... | collective-permute-start | bytes 49160 | tf_op jit(solution)/shard_map/ppermute | solution.py:48
  7.3 3.0 collective-permute-start.6
  10.4 2.3 multiply_cosine_fusion
  17.7 2.3 multiply_subtract_fusion.size_ref
  20.0 2.7 constant_dynamic-slice_fusion.6
  40.5 22.3 %embed_products.2 = (bf16[1024,768]{1,0:T(8,128)(2,1)}, bf16[1024,768]{1,0:T(8,128)(2,1)}, f32[1024,128]{1,0:T(8,128)}, bf16[128,768]{1,0:T(8,128)(2,1)}, bf16[128,768]{1,0:T(8,128)(2,1)}) custom-call(s32[4]{0:T(128)} %pad_add_fusion.1.ids_ref, bf16[128,3072]{1,0:T(8,128)(2,1)} %refs_0_.3, f32[1,3072]{1,0:T(1,128)} %bitcast.114, ...), custom_call_target="tpu_custom_call" | custom-call | flops 38654705664 | bytes 14155776 | tf_op jit(solution)/shard_map/embed_products/pallas_call | solution.py:341
  67.4 26.5 %embed_products.3 = (bf16[1024,768]{1,0:T(8,128)(2,1)}, bf16[1024,768]{1,0:T(8,128)(2,1)}, f32[1024,128]{1,0:T(8,128)}, bf16[256,768]{1,0:T(8,128)(2,1)}, bf16[128,768]{1,0:T(8,128)(2,1)}) custom-call(s32[4]{0:T(128)} %pad_add_fusion.2.ids_ref, bf16[128,3072]{1,0:T(8,128)(2,1)} %refs_0_.3, f32[1,3072]{1,0:T(1,128)} %bitcast.115, ...), custom_call_target="tpu_custom_call" | custom-call | flops 38654705664 | bytes 14155776 | tf_op jit(solution)/shard_map/embed_products/pallas_call | solution.py:341
  104.7 3.6 collective-permute-done.10.refs_1_
  114.6 12.5 %attend.2 = bf16[256,768]{1,0:T(8,128)(2,1)} custom-call(s32[1]{0:T(128)} %bitcast.36.value_ref.index_ref, bf16[2048,128]{1,0:T(8,128)(2,1)} %place.6.cur_ref, bf16[128,256]{1,0:T(8,128)(2,1)} %pad_maximum_fusion.9.gram_ref, f32[2048,1]{1,0:T(8,128)} %multiply_subtract_fusion.size_ref, bf16[256,768]{1,0:T(8,128)(2,1)} %get-tuple-element.51.eq_ref, ...), custom_call_target="tpu_custom_call" | custom-call | flops 6442450944 | bytes 6291456 | tf_op jit(solution)/shard_map/attend/pallas_call | solution.py:439
  127.1 3.9 convolution_convert_fusion.1
  145.0 19.5 %collective-permute-done.15.refs_0_.refs_22_ = bf16[384,1536]{1,0:T(8,128)(2,1)} collective-permute-done((bf16[384,1536]{1,0:T(8,128)(2,1)}, bf16[384,1536]{1,0:T(8,128)(2,1)}, u32[]{:S(2)}, u32[]{:S(2)}) %collective-permute-start.15) | collective-permute-done | bytes 1179680 | tf_op jit(solution)/shard_map/ppermute | solution.py:48
  164.5 3.8 collective-permute-done.16.refs_1_.refs_19_
  171.7 20.4 %collective-permute-start.18 = (bf16[64,3072]{1,0:T(8,128)(2,1)S(1)}, bf16[64,3072]{1,0:T(8,128)(2,1)S(1)}, u32[]{:S(2)}, u32[]{:S(2)}) collective-permute-start(bf16[64,3072]{1,0:T(8,128)(2,1)S(1)} %multiply_convert_fusion.3.refs_11_), channel_id=1, source_target_pairs={{0,8},{1,9},{2,0},{3,1},{4,12},{5,13},{6,4},{7,5},{8,16},{9,17},{1... | collective-permute-start | bytes 1179656 | tf_op jit(solution)/shard_map/ppermute | solution.py:48
  192.1 8.4 %collective-permute-done.18.refs_10_ = bf16[64,3072]{1,0:T(8,128)(2,1)S(1)} collective-permute-done((bf16[64,3072]{1,0:T(8,128)(2,1)S(1)}, bf16[64,3072]{1,0:T(8,128)(2,1)S(1)}, u32[]{:S(2)}, u32[]{:S(2)}) %collective-permute-start.18) | collective-permute-done | bytes 393248 | tf_op jit(solution)/shard_map/ppermute | solution.py:48
  200.6 2.5 collective-permute-start.19
  203.7 7.9 %collective-permute-done.19.refs_9_ = bf16[64,3072]{1,0:T(8,128)(2,1)} collective-permute-done((bf16[64,3072]{1,0:T(8,128)(2,1)S(1)}, bf16[64,3072]{1,0:T(8,128)(2,1)}, u32[]{:S(2)}, u32[]{:S(2)}) %collective-permute-start.19) | collective-permute-done | bytes 393248 | tf_op jit(solution)/shard_map/ppermute | solution.py:48
  217.8 3.9 collective-permute-done.20.refs_8_
  224.7 5.3 collective-permute-done.31
  232.4 4.5 collective-permute-done.32
  237.6 6.0 %collective-permute-done.34.refs_21_ = bf16[384,1536]{1,0:T(8,128)(2,1)} collective-permute-done((bf16[384,1536]{1,0:T(8,128)(2,1)}, bf16[384,1536]{1,0:T(8,128)(2,1)}, u32[]{:S(2)}, u32[]{:S(2)}) %collective-permute-start.34) | collective-permute-done | bytes 1179680 | tf_op jit(solution)/shard_map/ppermute | solution.py:48
  243.6 22.4 %collective-permute-done.35.refs_23_ = bf16[384,1536]{1,0:T(8,128)(2,1)} collective-permute-done((bf16[384,1536]{1,0:T(8,128)(2,1)}, bf16[384,1536]{1,0:T(8,128)(2,1)}, u32[]{:S(2)}, u32[]{:S(2)}) %collective-permute-start.35) | collective-permute-done | bytes 1179680 | tf_op jit(solution)/shard_map/ppermute | solution.py:48
  268.1 19.8 %mlp.2 = (bf16[64,3072]{1,0:T(8,128)(2,1)}, bf16[64,3072]{1,0:T(8,128)(2,1)}, bf16[64,3072]{1,0:T(8,128)(2,1)}, bf16[64,3072]{1,0:T(8,128)(2,1)}, bf16[64,3072]{...) custom-call(s32[8]{0:T(128)} %stack.316.places, ...), custom_call_target="tpu_custom_call" | custom-call | flops 19327352832 | bytes 9437184 | tf_op jit(solution)/shard_map/mlp/pallas_call | solution.py:507
  293.8 5.4 collective-permute-done.48
  300.3 5.0 collective-permute-done.41
  306.9 7.8 %collective-permute-done.49 = bf16[64,3072]{1,0:T(8,128)(2,1)S(1)} collective-permute-done((bf16[64,3072]{1,0:T(8,128)(2,1)S(1)}, bf16[64,3072]{1,0:T(8,128)(2,1)S(1)}, u32[]{:S(2)}, u32[]{:S(2)}) %collective-permute-start.49) | collective-permute-done | bytes 393248 | tf_op jit(solution)/shard_map/ppermute | solution.py:48
  317.4 6.4 %collective-permute-done.42 = bf16[64,3072]{1,0:T(8,128)(2,1)S(1)} collective-permute-done((bf16[64,3072]{1,0:T(8,128)(2,1)S(1)}, bf16[64,3072]{1,0:T(8,128)(2,1)S(1)}, u32[]{:S(2)}, u32[]{:S(2)}) %collective-permute-start.42) | collective-permute-done | bytes 393248 | tf_op jit(solution)/shard_map/ppermute | solution.py:48
  326.9 5.6 %collective-permute-done.43 = bf16[64,3072]{1,0:T(8,128)(2,1)S(1)} collective-permute-done((bf16[64,3072]{1,0:T(8,128)(2,1)S(1)}, bf16[64,3072]{1,0:T(8,128)(2,1)S(1)}, u32[]{:S(2)}, u32[]{:S(2)}) %collective-permute-start.43) | collective-permute-done | bytes 393248 | tf_op jit(solution)/shard_map/ppermute | solution.py:48
  337.3 4.3 collective-permute-done.44
  348.2 2.5 collective-permute-start.55
  356.2 2.5 collective-permute-done.58.refs_7_
  362.4 3.6 collective-permute-done.59.refs_1_
  368.6 2.1 place.8.cur_ref
  370.8 12.3 %attend.3 = bf16[256,768]{1,0:T(8,128)(2,1)} custom-call(s32[1]{0:T(128)} %bitcast.36.value_ref.index_ref, bf16[2048,128]{1,0:T(8,128)(2,1)} %place.8.cur_ref, bf16[128,256]{1,0:T(8,128)(2,1)} %pad_maximum_fusion.9.gram_ref, f32[2048,1]{1,0:T(8,128)} %multiply_subtract_fusion.size_ref, bf16[256,768]{1,0:T(8,128)(2,1)} %get-tuple-element.51.eq_ref, ...), custom_call_target="tpu_custom_call" | custom-call | flops 6442450944 | bytes 6291456 | tf_op jit(solution)/shard_map/attend/pallas_call | solution.py:439
  383.1 3.9 convolution_convert_fusion
  392.6 9.9 %collective-permute-done.63 = bf16[64,3072]{1,0:T(8,128)(2,1)} collective-permute-done((bf16[64,3072]{1,0:T(8,128)(2,1)S(1)}, bf16[64,3072]{1,0:T(8,128)(2,1)}, u32[]{:S(2)}, u32[]{:S(2)}) %collective-permute-start.63) | collective-permute-done | bytes 393248 | tf_op jit(solution)/shard_map/ppermute | solution.py:48
  406.8 8.5 %collective-permute-done.64.refs_10_ = bf16[64,3072]{1,0:T(8,128)(2,1)S(1)} collective-permute-done((bf16[64,3072]{1,0:T(8,128)(2,1)S(1)}, bf16[64,3072]{1,0:T(8,128)(2,1)S(1)}, u32[]{:S(2)}, u32[]{:S(2)}) %collective-permute-start.64) | collective-permute-done | bytes 393248 | tf_op jit(solution)/shard_map/ppermute | solution.py:48
  417.9 7.2 %collective-permute-done.65.refs_9_ = bf16[64,3072]{1,0:T(8,128)(2,1)} collective-permute-done((bf16[64,3072]{1,0:T(8,128)(2,1)S(1)}, bf16[64,3072]{1,0:T(8,128)(2,1)}, u32[]{:S(2)}, u32[]{:S(2)}) %collective-permute-start.65) | collective-permute-done | bytes 393248 | tf_op jit(solution)/shard_map/ppermute | solution.py:48
  429.9 4.3 collective-permute-done.66.refs_8_
  438.5 2.4 collective-permute-done.77
  445.7 19.8 %mlp.3 = (bf16[64,3072]{1,0:T(8,128)(2,1)}, bf16[64,3072]{1,0:T(8,128)(2,1)}, bf16[64,3072]{1,0:T(8,128)(2,1)}, bf16[64,3072]{1,0:T(8,128)(2,1)}, bf16[64,3072]{...) custom-call(s32[8]{0:T(128)} %stack.316.places, ...), custom_call_target="tpu_custom_call" | custom-call | flops 19327352832 | bytes 9437184 | tf_op jit(solution)/shard_map/mlp/pallas_call | solution.py:507
  471.0 5.7 %collective-permute-done.92 = bf16[32,3072]{1,0:T(8,128)(2,1)S(1)} collective-permute-done((bf16[32,3072]{1,0:T(8,128)(2,1)S(1)}, bf16[32,3072]{1,0:T(8,128)(2,1)S(1)}, u32[]{:S(2)}, u32[]{:S(2)}) %collective-permute-start.92) | collective-permute-done | bytes 196640 | tf_op jit(solution)/shard_map/ppermute | solution.py:48
  477.1 5.7 %collective-permute-done.85 = bf16[32,3072]{1,0:T(8,128)(2,1)S(1)} collective-permute-done((bf16[32,3072]{1,0:T(8,128)(2,1)S(1)}, bf16[32,3072]{1,0:T(8,128)(2,1)S(1)}, u32[]{:S(2)}, u32[]{:S(2)}) %collective-permute-start.85) | collective-permute-done | bytes 196640 | tf_op jit(solution)/shard_map/ppermute | solution.py:48
  484.1 8.1 %collective-permute-done.93 = bf16[64,3072]{1,0:T(8,128)(2,1)S(1)} collective-permute-done((bf16[64,3072]{1,0:T(8,128)(2,1)S(1)}, bf16[64,3072]{1,0:T(8,128)(2,1)S(1)}, u32[]{:S(2)}, u32[]{:S(2)}) %collective-permute-start.93) | collective-permute-done | bytes 393248 | tf_op jit(solution)/shard_map/ppermute | solution.py:48
  494.5 6.8 %collective-permute-done.86 = bf16[64,3072]{1,0:T(8,128)(2,1)S(1)} collective-permute-done((bf16[64,3072]{1,0:T(8,128)(2,1)S(1)}, bf16[64,3072]{1,0:T(8,128)(2,1)S(1)}, u32[]{:S(2)}, u32[]{:S(2)}) %collective-permute-start.86) | collective-permute-done | bytes 393248 | tf_op jit(solution)/shard_map/ppermute | solution.py:48
  503.8 7.2 %collective-permute-done.87 = bf16[64,3072]{1,0:T(8,128)(2,1)S(1)} collective-permute-done((bf16[64,3072]{1,0:T(8,128)(2,1)S(1)}, bf16[64,3072]{1,0:T(8,128)(2,1)S(1)}, u32[]{:S(2)}, u32[]{:S(2)}) %collective-permute-start.87) | collective-permute-done | bytes 393248 | tf_op jit(solution)/shard_map/ppermute | solution.py:48
  511.4 7.5 %collective-permute-done.88 = bf16[64,3072]{1,0:T(8,128)(2,1)S(1)} collective-permute-done((bf16[64,3072]{1,0:T(8,128)(2,1)S(1)}, bf16[64,3072]{1,0:T(8,128)(2,1)S(1)}, u32[]{:S(2)}, u32[]{:S(2)}) %collective-permute-start.88) | collective-permute-done | bytes 393248 | tf_op jit(solution)/shard_map/ppermute | solution.py:48
  523.3 4.5 collective-permute-done.96
  530.6 2.5 collective-permute-done.98.refs_1_
  (422 shorter events, 149.9 us)
Async XLA Ops:
  0.9 26.3 %collective-permute-start.3 = (bf16[64,128]{1,0:T(8,128)(2,1)S(1)}, bf16[64,128]{1,0:T(8,128)(2,1)S(1)}, u32[]{:S(2)}, u32[]{:S(2)}) collective-permute-start(bf16[64,128]{1,0:T(8,128)(2,1)S(1)} %dynamic-slice_convert_fusion.2.refs_0_), channel_id=1, source_target_pairs={{0,28},{1,29},{2,30},{3,31},{4,0},{5,1},{6,2},{7,3},{8,4},{9,5},{1... | collective-permute-start | bytes 49160 | tf_op jit(solution)/shard_map/ppermute | solution.py:48
  6.9 22.1 %collective-permute-start.4 = (bf16[64,128]{1,0:T(8,128)(2,1)S(1)}, bf16[64,128]{1,0:T(8,128)(2,1)S(1)}, u32[]{:S(2)}, u32[]{:S(2)}) collective-permute-start(bf16[64,128]{1,0:T(8,128)(2,1)S(1)} %dynamic-slice_convert_fusion.2.refs_0_), channel_id=1, source_target_pairs={{0,24},{1,25},{2,26},{3,27},{4,28},{5,29},{6,30},{7,31},{8,0},{9,1... | collective-permute-start | bytes 49160 | tf_op jit(solution)/shard_map/ppermute | solution.py:48
  7.3 23.3 %collective-permute-start.5 = (bf16[64,128]{1,0:T(8,128)(2,1)S(1)}, bf16[64,128]{1,0:T(8,128)(2,1)S(1)}, u32[]{:S(2)}, u32[]{:S(2)}) collective-permute-start(bf16[64,128]{1,0:T(8,128)(2,1)S(1)} %dynamic-slice_convert_fusion.2.refs_0_), channel_id=1, source_target_pairs={{0,20},{1,21},{2,22},{3,23},{4,24},{5,25},{6,26},{7,27},{8,28},{9,... | collective-permute-start | bytes 49160 | tf_op jit(solution)/shard_map/ppermute | solution.py:48
  7.3 25.4 %collective-permute-start.6 = (bf16[64,128]{1,0:T(8,128)(2,1)S(1)}, bf16[64,128]{1,0:T(8,128)(2,1)S(1)}, u32[]{:S(2)}, u32[]{:S(2)}) collective-permute-start(bf16[64,128]{1,0:T(8,128)(2,1)S(1)} %dynamic-slice_convert_fusion.2.refs_0_), channel_id=1, source_target_pairs={{0,16},{1,17},{2,18},{3,19},{4,20},{5,21},{6,22},{7,23},{8,24},{9,... | collective-permute-start | bytes 49160 | tf_op jit(solution)/shard_map/ppermute | solution.py:48
  10.3 23.3 %collective-permute-start.7 = (bf16[64,128]{1,0:T(8,128)(2,1)S(1)}, bf16[64,128]{1,0:T(8,128)(2,1)S(1)}, u32[]{:S(2)}, u32[]{:S(2)}) collective-permute-start(bf16[64,128]{1,0:T(8,128)(2,1)S(1)} %dynamic-slice_convert_fusion.2.refs_0_), channel_id=1, source_target_pairs={{0,12},{1,13},{2,14},{3,15},{4,16},{5,17},{6,18},{7,19},{8,20},{9,... | collective-permute-start | bytes 49160 | tf_op jit(solution)/shard_map/ppermute | solution.py:48
  30.7 63.2 %collective-permute-start = (bf16[384,1536]{1,0:T(8,128)(2,1)}, bf16[384,1536]{1,0:T(8,128)(2,1)}, u32[]{:S(2)}, u32[]{:S(2)}) collective-permute-start(bf16[384,1536]{1,0:T(8,128)(2,1)} %pad_maximum_fusion), channel_id=1, source_target_pairs={{0,8},{1,9},{2,10},{3,11},{4,12},{5,13},{6,14},{7,15},{8,0},{9,1},... | collective-permute-start | bytes 3538952 | tf_op jit(solution)/shard_map/ppermute | solution.py:48
  32.7 61.2 %collective-permute-start.1 = (bf16[384,1536]{1,0:T(8,128)(2,1)}, bf16[384,1536]{1,0:T(8,128)(2,1)}, u32[]{:S(2)}, u32[]{:S(2)}) collective-permute-start(bf16[384,1536]{1,0:T(8,128)(2,1)} %pad_maximum_fusion.1), channel_id=1, source_target_pairs={{0,16},{1,17},{2,18},{3,19},{4,20},{5,21},{6,22},{7,23},{8,24},{9,... | collective-permute-start | bytes 3538952 | tf_op jit(solution)/shard_map/ppermute | solution.py:48
  33.7 60.2 %collective-permute-start.2 = (bf16[384,1536]{1,0:T(8,128)(2,1)}, bf16[384,1536]{1,0:T(8,128)(2,1)}, u32[]{:S(2)}, u32[]{:S(2)}) collective-permute-start(bf16[384,1536]{1,0:T(8,128)(2,1)} %pad_maximum_fusion.2.refs_16_), channel_id=1, source_target_pairs={{0,4},{1,5},{2,6},{3,7},{4,0},{5,1},{6,2},{7,3},{8,12},{9,13},{10,... | collective-permute-start | bytes 3538952 | tf_op jit(solution)/shard_map/ppermute | solution.py:48
  133.9 30.6 %collective-permute-start.15 = (bf16[384,1536]{1,0:T(8,128)(2,1)}, bf16[384,1536]{1,0:T(8,128)(2,1)}, u32[]{:S(2)}, u32[]{:S(2)}) collective-permute-start(bf16[384,1536]{1,0:T(8,128)(2,1)} %pad_maximum_fusion.3), channel_id=1, source_target_pairs={{0,24},{1,25},{2,26},{3,27},{4,28},{5,29},{6,30},{7,31},{8,16},{9,... | collective-permute-start | bytes 3538952 | tf_op jit(solution)/shard_map/ppermute | solution.py:48
  139.8 28.5 %collective-permute-start.16 = (bf16[384,1536]{1,0:T(8,128)(2,1)}, bf16[384,1536]{1,0:T(8,128)(2,1)}, u32[]{:S(2)}, u32[]{:S(2)}) collective-permute-start(bf16[384,1536]{1,0:T(8,128)(2,1)} %collective-permute-done.refs_0_.refs_18_), channel_id=1, source_target_pairs={{0,4},{1,5},{2,6},{3,7},{4,0},{5,1},{6,2},{7,3},{8,12},{9,13},{10,... | collective-permute-start | bytes 3538952 | tf_op jit(solution)/shard_map/ppermute | solution.py:48
  142.4 27.1 %collective-permute-start.17 = (bf16[64,3072]{1,0:T(8,128)(2,1)}, bf16[64,3072]{1,0:T(8,128)(2,1)}, u32[]{:S(2)}, u32[]{:S(2)}) collective-permute-start(bf16[64,3072]{1,0:T(8,128)(2,1)} %fusion.9), channel_id=1, source_target_pairs={{0,2},{1,3},{2,0},{3,1},{4,6},{5,7},{6,4},{7,5},{8,10},{9,11},{10,... | collective-permute-start | bytes 1179656 | tf_op jit(solution)/shard_map/ppermute | solution.py:48
  171.7 28.8 %collective-permute-start.18 = (bf16[64,3072]{1,0:T(8,128)(2,1)S(1)}, bf16[64,3072]{1,0:T(8,128)(2,1)S(1)}, u32[]{:S(2)}, u32[]{:S(2)}) collective-permute-start(bf16[64,3072]{1,0:T(8,128)(2,1)S(1)} %multiply_convert_fusion.3.refs_11_), channel_id=1, source_target_pairs={{0,8},{1,9},{2,0},{3,1},{4,12},{5,13},{6,4},{7,5},{8,16},{9,17},{1... | collective-permute-start | bytes 1179656 | tf_op jit(solution)/shard_map/ppermute | solution.py:48
  192.1 10.9 %collective-permute-start.25 = (bf16[64,3072]{1,0:T(8,128)(2,1)S(1)}, bf16[64,3072]{1,0:T(8,128)(2,1)S(1)}, u32[]{:S(2)}, u32[]{:S(2)}) collective-permute-start(bf16[64,3072]{1,0:T(8,128)(2,1)S(1)} %multiply_convert_fusion.3.refs_11_), channel_id=1, source_target_pairs={{0,2},{1,3},{2,10},{3,11},{4,6},{5,7},{6,14},{7,15},{8,0},{9,1},{1... | collective-permute-start | bytes 1179656 | tf_op jit(solution)/shard_map/ppermute | solution.py:48
  200.6 11.0 %collective-permute-start.19 = (bf16[64,3072]{1,0:T(8,128)(2,1)S(1)}, bf16[64,3072]{1,0:T(8,128)(2,1)}, u32[]{:S(2)}, u32[]{:S(2)}) collective-permute-start(bf16[64,3072]{1,0:T(8,128)(2,1)S(1)} %collective-permute-done.18.refs_10_), channel_id=1, source_target_pairs={{0,8},{1,9},{2,0},{3,1},{4,12},{5,13},{6,4},{7,5},{8,16},{9,17},{1... | collective-permute-start | bytes 1179656 | tf_op jit(solution)/shard_map/ppermute | solution.py:48
  203.1 10.2 %collective-permute-start.27 = (bf16[64,3072]{1,0:T(8,128)(2,1)S(1)}, bf16[64,3072]{1,0:T(8,128)(2,1)}, u32[]{:S(2)}, u32[]{:S(2)}) collective-permute-start(bf16[64,3072]{1,0:T(8,128)(2,1)S(1)} %collective-permute-done.25.refs_12_), channel_id=1, source_target_pairs={{0,2},{1,3},{2,10},{3,11},{4,6},{5,7},{6,14},{7,15},{8,0},{9,1},{1... | collective-permute-start | bytes 1179656 | tf_op jit(solution)/shard_map/ppermute | solution.py:48
  203.1 10.6 %collective-permute-start.24 = (bf16[64,3072]{1,0:T(8,128)(2,1)S(1)}, bf16[64,3072]{1,0:T(8,128)(2,1)S(1)}, u32[]{:S(2)}, u32[]{:S(2)}) collective-permute-start(bf16[64,3072]{1,0:T(8,128)(2,1)S(1)} %multiply_convert_fusion.3.refs_11_), channel_id=1, source_target_pairs={{0,1},{1,0},{2,3},{3,2},{4,5},{5,4},{6,7},{7,6},{8,9},{9,8},{10,11... | collective-permute-start | bytes 1179656 | tf_op jit(solution)/shard_map/ppermute | solution.py:48
  203.2 11.3 %collective-permute-start.23 = (bf16[64,3072]{1,0:T(8,128)(2,1)S(1)}, bf16[64,3072]{1,0:T(8,128)(2,1)}, u32[]{:S(2)}, u32[]{:S(2)}) collective-permute-start(bf16[64,3072]{1,0:T(8,128)(2,1)S(1)} %collective-permute-done.18.refs_10_), channel_id=1, source_target_pairs={{0,1},{1,0},{2,3},{3,2},{4,5},{5,4},{6,7},{7,6},{8,9},{9,8},{10,11... | collective-permute-start | bytes 1179656 | tf_op jit(solution)/shard_map/ppermute | solution.py:48
  203.7 12.9 %collective-permute-start.26 = (bf16[64,3072]{1,0:T(8,128)(2,1)S(1)}, bf16[64,3072]{1,0:T(8,128)(2,1)}, u32[]{:S(2)}, u32[]{:S(2)}) collective-permute-start(bf16[64,3072]{1,0:T(8,128)(2,1)S(1)} %collective-permute-done.25.refs_12_), channel_id=1, source_target_pairs={{0,1},{1,0},{2,3},{3,2},{4,5},{5,4},{6,7},{7,6},{8,9},{9,8},{10,11... | collective-permute-start | bytes 1179656 | tf_op jit(solution)/shard_map/ppermute | solution.py:48
  211.6 10.1 %collective-permute-start.20 = (bf16[64,3072]{1,0:T(8,128)(2,1)}, bf16[64,3072]{1,0:T(8,128)(2,1)}, u32[]{:S(2)}, u32[]{:S(2)}) collective-permute-start(bf16[64,3072]{1,0:T(8,128)(2,1)} %collective-permute-done.19.refs_9_), channel_id=1, source_target_pairs={{0,8},{1,9},{2,0},{3,1},{4,12},{5,13},{6,4},{7,5},{8,16},{9,17},{1... | collective-permute-start | bytes 1179656 | tf_op jit(solution)/shard_map/ppermute | solution.py:48
  214.4 29.2 %collective-permute-start.34 = (bf16[384,1536]{1,0:T(8,128)(2,1)}, bf16[384,1536]{1,0:T(8,128)(2,1)}, u32[]{:S(2)}, u32[]{:S(2)}) collective-permute-start(bf16[384,1536]{1,0:T(8,128)(2,1)} %collective-permute-done.1.refs_1_.refs_20_), channel_id=1, source_target_pairs={{0,4},{1,5},{2,6},{3,7},{4,0},{5,1},{6,2},{7,3},{8,12},{9,13},{10,... | collective-permute-start | bytes 3538952 | tf_op jit(solution)/shard_map/ppermute | solution.py:48
  214.4 51.6 %collective-permute-start.35 = (bf16[384,1536]{1,0:T(8,128)(2,1)}, bf16[384,1536]{1,0:T(8,128)(2,1)}, u32[]{:S(2)}, u32[]{:S(2)}) collective-permute-start(bf16[384,1536]{1,0:T(8,128)(2,1)} %collective-permute-done.15.refs_0_.refs_22_), channel_id=1, source_target_pairs={{0,4},{1,5},{2,6},{3,7},{4,0},{5,1},{6,2},{7,3},{8,12},{9,13},{10,... | collective-permute-start | bytes 3538952 | tf_op jit(solution)/shard_map/ppermute | solution.py:48
  217.7 49.0 %collective-permute-start.22 = (bf16[64,3072]{1,0:T(8,128)(2,1)}, bf16[64,3072]{1,0:T(8,128)(2,1)}, u32[]{:S(2)}, u32[]{:S(2)}) collective-permute-start(bf16[64,3072]{1,0:T(8,128)(2,1)} %collective-permute-done.19.refs_9_), channel_id=1, source_target_pairs={{0,1},{1,0},{2,3},{3,2},{4,5},{5,4},{6,7},{7,6},{8,9},{9,8},{10,11... | collective-permute-start | bytes 1179656 | tf_op jit(solution)/shard_map/ppermute | solution.py:48
  221.7 45.0 %collective-permute-start.28 = (bf16[64,3072]{1,0:T(8,128)(2,1)}, bf16[64,3072]{1,0:T(8,128)(2,1)}, u32[]{:S(2)}, u32[]{:S(2)}) collective-permute-start(bf16[64,3072]{1,0:T(8,128)(2,1)} %collective-permute-done.27.refs_13_), channel_id=1, source_target_pairs={{0,1},{1,0},{2,3},{3,2},{4,5},{5,4},{6,7},{7,6},{8,9},{9,8},{10,11... | collective-permute-start | bytes 1179656 | tf_op jit(solution)/shard_map/ppermute | solution.py:48
  236.9 29.8 %collective-permute-start.21 = (bf16[64,3072]{1,0:T(8,128)(2,1)}, bf16[64,3072]{1,0:T(8,128)(2,1)}, u32[]{:S(2)}, u32[]{:S(2)}) collective-permute-start(bf16[64,3072]{1,0:T(8,128)(2,1)} %collective-permute-done.20.refs_8_), channel_id=1, source_target_pairs={{0,1},{1,0},{2,3},{3,2},{4,5},{5,4},{6,7},{7,6},{8,9},{9,8},{10,11... | collective-permute-start | bytes 1179656 | tf_op jit(solution)/shard_map/ppermute | solution.py:48
  243.6 23.1 %collective-permute-start.30 = (bf16[64,3072]{1,0:T(8,128)(2,1)}, bf16[64,3072]{1,0:T(8,128)(2,1)}, u32[]{:S(2)}, u32[]{:S(2)}) collective-permute-start(bf16[64,3072]{1,0:T(8,128)(2,1)} %collective-permute-done.29.refs_14_), channel_id=1, source_target_pairs={{0,1},{1,0},{2,3},{3,2},{4,5},{5,4},{6,7},{7,6},{8,9},{9,8},{10,11... | collective-permute-start | bytes 1179656 | tf_op jit(solution)/shard_map/ppermute | solution.py:48
  288.6 18.3 %collective-permute-start.46 = (bf16[64,3072]{1,0:T(8,128)(2,1)}, bf16[64,3072]{1,0:T(8,128)(2,1)S(1)}, u32[]{:S(2)}, u32[]{:S(2)}) collective-permute-start(bf16[64,3072]{1,0:T(8,128)(2,1)} %get-tuple-element.72), channel_id=1, source_target_pairs={{0,1},{1,0},{2,3},{3,2},{4,5},{5,4},{6,7},{7,6},{8,9},{9,8},{10,11... | collective-permute-start | bytes 1179656 | tf_op jit(solution)/shard_map/ppermute | solution.py:48
  288.7 36.3 %collective-permute-start.45 = (bf16[64,3072]{1,0:T(8,128)(2,1)}, bf16[64,3072]{1,0:T(8,128)(2,1)S(1)}, u32[]{:S(2)}, u32[]{:S(2)}) collective-permute-start(bf16[64,3072]{1,0:T(8,128)(2,1)} %get-tuple-element.70), channel_id=1, source_target_pairs={{0,1},{1,0},{2,3},{3,2},{4,5},{5,4},{6,7},{7,6},{8,9},{9,8},{10,11... | collective-permute-start | bytes 1179656 | tf_op jit(solution)/shard_map/ppermute | solution.py:48
  290.0 25.9 %collective-permute-start.38 = (bf16[64,3072]{1,0:T(8,128)(2,1)}, bf16[64,3072]{1,0:T(8,128)(2,1)S(1)}, u32[]{:S(2)}, u32[]{:S(2)}) collective-permute-start(bf16[64,3072]{1,0:T(8,128)(2,1)} %get-tuple-element.64), channel_id=1, source_target_pairs={{0,1},{1,0},{2,3},{3,2},{4,5},{5,4},{6,7},{7,6},{8,9},{9,8},{10,11... | collective-permute-start | bytes 1179656 | tf_op jit(solution)/shard_map/ppermute | solution.py:48
  291.3 35.7 %collective-permute-start.37 = (bf16[64,3072]{1,0:T(8,128)(2,1)S(1)}, bf16[64,3072]{1,0:T(8,128)(2,1)S(1)}, u32[]{:S(2)}, u32[]{:S(2)}) collective-permute-start(bf16[64,3072]{1,0:T(8,128)(2,1)S(1)} %copy-done.68), channel_id=1, source_target_pairs={{0,1},{1,0},{2,3},{3,2},{4,5},{5,4},{6,7},{7,6},{8,9},{9,8},{10,11... | collective-permute-start | bytes 1179656 | tf_op jit(solution)/shard_map/ppermute | solution.py:48
  306.8 30.4 %collective-permute-start.36 = (bf16[64,3072]{1,0:T(8,128)(2,1)}, bf16[64,3072]{1,0:T(8,128)(2,1)}, u32[]{:S(2)}, u32[]{:S(2)}) collective-permute-start(bf16[64,3072]{1,0:T(8,128)(2,1)} %get-tuple-element.60), channel_id=1, source_target_pairs={{0,1},{1,0},{2,3},{3,2},{4,5},{5,4},{6,7},{7,6},{8,9},{9,8},{10,11... | collective-permute-start | bytes 1179656 | tf_op jit(solution)/shard_map/ppermute | solution.py:48
  325.9 11.3 %collective-permute-start.51 = (bf16[64,3072]{1,0:T(8,128)(2,1)}, bf16[64,3072]{1,0:T(8,128)(2,1)}, u32[]{:S(2)}, u32[]{:S(2)}) collective-permute-start(bf16[64,3072]{1,0:T(8,128)(2,1)} %add_convert_fusion.5), channel_id=1, source_target_pairs={{0,2},{1,3},{2,10},{3,11},{4,6},{5,7},{6,14},{7,15},{8,0},{9,1},{1... | collective-permute-start | bytes 1179656 | tf_op jit(solution)/shard_map/ppermute | solution.py:48
  391.0 11.6 %collective-permute-start.63 = (bf16[64,3072]{1,0:T(8,128)(2,1)S(1)}, bf16[64,3072]{1,0:T(8,128)(2,1)}, u32[]{:S(2)}, u32[]{:S(2)}) collective-permute-start(bf16[64,3072]{1,0:T(8,128)(2,1)S(1)} %fusion.10), channel_id=1, source_target_pairs={{0,2},{1,3},{2,0},{3,1},{4,6},{5,7},{6,4},{7,5},{8,10},{9,11},{10,... | collective-permute-start | bytes 1179656 | tf_op jit(solution)/shard_map/ppermute | solution.py:48
  404.8 10.6 %collective-permute-start.64 = (bf16[64,3072]{1,0:T(8,128)(2,1)S(1)}, bf16[64,3072]{1,0:T(8,128)(2,1)S(1)}, u32[]{:S(2)}, u32[]{:S(2)}) collective-permute-start(bf16[64,3072]{1,0:T(8,128)(2,1)S(1)} %multiply_convert_fusion.1.refs_11_), channel_id=1, source_target_pairs={{0,8},{1,9},{2,0},{3,1},{4,12},{5,13},{6,4},{7,5},{8,16},{9,17},{1... | collective-permute-start | bytes 1179656 | tf_op jit(solution)/shard_map/ppermute | solution.py:48
  404.8 10.9 %collective-permute-start.71 = (bf16[64,3072]{1,0:T(8,128)(2,1)S(1)}, bf16[64,3072]{1,0:T(8,128)(2,1)S(1)}, u32[]{:S(2)}, u32[]{:S(2)}) collective-permute-start(bf16[64,3072]{1,0:T(8,128)(2,1)S(1)} %multiply_convert_fusion.1.refs_11_), channel_id=1, source_target_pairs={{0,2},{1,3},{2,10},{3,11},{4,6},{5,7},{6,14},{7,15},{8,0},{9,1},{1... | collective-permute-start | bytes 1179656 | tf_op jit(solution)/shard_map/ppermute | solution.py:48
  415.4 9.8 %collective-permute-start.65 = (bf16[64,3072]{1,0:T(8,128)(2,1)S(1)}, bf16[64,3072]{1,0:T(8,128)(2,1)}, u32[]{:S(2)}, u32[]{:S(2)}) collective-permute-start(bf16[64,3072]{1,0:T(8,128)(2,1)S(1)} %collective-permute-done.64.refs_10_), channel_id=1, source_target_pairs={{0,8},{1,9},{2,0},{3,1},{4,12},{5,13},{6,4},{7,5},{8,16},{9,17},{1... | collective-permute-start | bytes 1179656 | tf_op jit(solution)/shard_map/ppermute | solution.py:48
  415.7 10.1 %collective-permute-start.73 = (bf16[64,3072]{1,0:T(8,128)(2,1)S(1)}, bf16[64,3072]{1,0:T(8,128)(2,1)}, u32[]{:S(2)}, u32[]{:S(2)}) collective-permute-start(bf16[64,3072]{1,0:T(8,128)(2,1)S(1)} %collective-permute-done.71.refs_12_), channel_id=1, source_target_pairs={{0,2},{1,3},{2,10},{3,11},{4,6},{5,7},{6,14},{7,15},{8,0},{9,1},{1... | collective-permute-start | bytes 1179656 | tf_op jit(solution)/shard_map/ppermute | solution.py:48
  417.4 9.8 %collective-permute-start.70 = (bf16[64,3072]{1,0:T(8,128)(2,1)S(1)}, bf16[64,3072]{1,0:T(8,128)(2,1)S(1)}, u32[]{:S(2)}, u32[]{:S(2)}) collective-permute-start(bf16[64,3072]{1,0:T(8,128)(2,1)S(1)} %multiply_convert_fusion.1.refs_11_), channel_id=1, source_target_pairs={{0,1},{1,0},{2,3},{3,2},{4,5},{5,4},{6,7},{7,6},{8,9},{9,8},{10,11... | collective-permute-start | bytes 1179656 | tf_op jit(solution)/shard_map/ppermute | solution.py:48
  417.4 9.8 %collective-permute-start.69 = (bf16[64,3072]{1,0:T(8,128)(2,1)S(1)}, bf16[64,3072]{1,0:T(8,128)(2,1)S(1)}, u32[]{:S(2)}, u32[]{:S(2)}) collective-permute-start(bf16[64,3072]{1,0:T(8,128)(2,1)S(1)} %collective-permute-done.64.refs_10_), channel_id=1, source_target_pairs={{0,1},{1,0},{2,3},{3,2},{4,5},{5,4},{6,7},{7,6},{8,9},{9,8},{10,11... | collective-permute-start | bytes 1179656 | tf_op jit(solution)/shard_map/ppermute | solution.py:48
  425.8 10.4 %collective-permute-start.75 = (bf16[64,3072]{1,0:T(8,128)(2,1)}, bf16[64,3072]{1,0:T(8,128)(2,1)}, u32[]{:S(2)}, u32[]{:S(2)}) collective-permute-start(bf16[64,3072]{1,0:T(8,128)(2,1)} %collective-permute-done.73.refs_13_), channel_id=1, source_target_pairs={{0,2},{1,3},{2,10},{3,11},{4,6},{5,7},{6,14},{7,15},{8,0},{9,1},{1... | collective-permute-start | bytes 1179656 | tf_op jit(solution)/shard_map/ppermute | solution.py:48
  429.3 13.9 %collective-permute-start.68 = (bf16[64,3072]{1,0:T(8,128)(2,1)}, bf16[64,3072]{1,0:T(8,128)(2,1)}, u32[]{:S(2)}, u32[]{:S(2)}) collective-permute-start(bf16[64,3072]{1,0:T(8,128)(2,1)} %collective-permute-done.65.refs_9_), channel_id=1, source_target_pairs={{0,1},{1,0},{2,3},{3,2},{4,5},{5,4},{6,7},{7,6},{8,9},{9,8},{10,11... | collective-permute-start | bytes 1179656 | tf_op jit(solution)/shard_map/ppermute | solution.py:48
  429.4 13.8 %collective-permute-start.74 = (bf16[64,3072]{1,0:T(8,128)(2,1)}, bf16[64,3072]{1,0:T(8,128)(2,1)}, u32[]{:S(2)}, u32[]{:S(2)}) collective-permute-start(bf16[64,3072]{1,0:T(8,128)(2,1)} %collective-permute-done.73.refs_13_), channel_id=1, source_target_pairs={{0,1},{1,0},{2,3},{3,2},{4,5},{5,4},{6,7},{7,6},{8,9},{9,8},{10,11... | collective-permute-start | bytes 1179656 | tf_op jit(solution)/shard_map/ppermute | solution.py:48
  466.1 17.9 %collective-permute-start.90 = (bf16[64,3072]{1,0:T(8,128)(2,1)}, bf16[64,3072]{1,0:T(8,128)(2,1)S(1)}, u32[]{:S(2)}, u32[]{:S(2)}) collective-permute-start(bf16[64,3072]{1,0:T(8,128)(2,1)} %get-tuple-element.88), channel_id=1, source_target_pairs={{0,1},{1,0},{2,3},{3,2},{4,5},{5,4},{6,7},{7,6},{8,9},{9,8},{10,11... | collective-permute-start | bytes 1179656 | tf_op jit(solution)/shard_map/ppermute | solution.py:48
  466.2 35.6 %collective-permute-start.89 = (bf16[64,3072]{1,0:T(8,128)(2,1)}, bf16[64,3072]{1,0:T(8,128)(2,1)S(1)}, u32[]{:S(2)}, u32[]{:S(2)}) collective-permute-start(bf16[64,3072]{1,0:T(8,128)(2,1)} %get-tuple-element.86), channel_id=1, source_target_pairs={{0,1},{1,0},{2,3},{3,2},{4,5},{5,4},{6,7},{7,6},{8,9},{9,8},{10,11... | collective-permute-start | bytes 1179656 | tf_op jit(solution)/shard_map/ppermute | solution.py:48
  467.5 25.2 %collective-permute-start.82 = (bf16[64,3072]{1,0:T(8,128)(2,1)}, bf16[64,3072]{1,0:T(8,128)(2,1)S(1)}, u32[]{:S(2)}, u32[]{:S(2)}) collective-permute-start(bf16[64,3072]{1,0:T(8,128)(2,1)} %get-tuple-element.80), channel_id=1, source_target_pairs={{0,1},{1,0},{2,3},{3,2},{4,5},{5,4},{6,7},{7,6},{8,9},{9,8},{10,11... | collective-permute-start | bytes 1179656 | tf_op jit(solution)/shard_map/ppermute | solution.py:48
  468.8 35.0 %collective-permute-start.81 = (bf16[64,3072]{1,0:T(8,128)(2,1)S(1)}, bf16[64,3072]{1,0:T(8,128)(2,1)S(1)}, u32[]{:S(2)}, u32[]{:S(2)}) collective-permute-start(bf16[64,3072]{1,0:T(8,128)(2,1)S(1)} %copy-done.66), channel_id=1, source_target_pairs={{0,1},{1,0},{2,3},{3,2},{4,5},{5,4},{6,7},{7,6},{8,9},{9,8},{10,11... | collective-permute-start | bytes 1179656 | tf_op jit(solution)/shard_map/ppermute | solution.py:48
  484.0 27.4 %collective-permute-start.80 = (bf16[64,3072]{1,0:T(8,128)(2,1)S(1)}, bf16[64,3072]{1,0:T(8,128)(2,1)S(1)}, u32[]{:S(2)}, u32[]{:S(2)}) collective-permute-start(bf16[64,3072]{1,0:T(8,128)(2,1)S(1)} %copy-done.65), channel_id=1, source_target_pairs={{0,1},{1,0},{2,3},{3,2},{4,5},{5,4},{6,7},{7,6},{8,9},{9,8},{10,11... | collective-permute-start | bytes 1179656 | tf_op jit(solution)/shard_map/ppermute | solution.py:48
  501.4 9.5 %collective-permute-start.87 = (bf16[64,3072]{1,0:T(8,128)(2,1)S(1)}, bf16[64,3072]{1,0:T(8,128)(2,1)S(1)}, u32[]{:S(2)}, u32[]{:S(2)}) collective-permute-start(bf16[64,3072]{1,0:T(8,128)(2,1)S(1)} %add_convert_fusion.3), channel_id=1, source_target_pairs={{0,8},{1,9},{2,0},{3,1},{4,12},{5,13},{6,4},{7,5},{8,16},{9,17},{1... | collective-permute-start | bytes 1179656 | tf_op jit(solution)/shard_map/ppermute | solution.py:48
  502.0 9.5 %collective-permute-start.95 = (bf16[64,3072]{1,0:T(8,128)(2,1)S(1)}, bf16[64,3072]{1,0:T(8,128)(2,1)S(1)}, u32[]{:S(2)}, u32[]{:S(2)}) collective-permute-start(bf16[64,3072]{1,0:T(8,128)(2,1)S(1)} %add_convert_fusion), channel_id=1, source_target_pairs={{0,2},{1,3},{2,10},{3,11},{4,6},{5,7},{6,14},{7,15},{8,0},{9,1},{1... | collective-permute-start | bytes 1179656 | tf_op jit(solution)/shard_map/ppermute | solution.py:48
  (124 other events, 1112.2 us)

commit v5 on v4

--- a/solution.py
+++ b/solution.py
@@ -133,7 +133,7 @@
     return place(lines, dests, sub, first)
 
 
-def gather_ring(grid, own):
+def gather_ring(grid, own, gates):
     size = len(grid.ring)
     half, cut = size // 2, own.shape[0] // 2
     pieces = {0: own}
@@ -142,7 +142,7 @@
         ahead, back = grid.ring_step(ahead, 1), grid.ring_step(back, -1)
         pieces[-j], pieces[j] = ahead, back
     swapped = {j: grid.core_swap(pieces[j]) for j in range(-half // 2, half // 2 + 1) if abs(j) < half - 2}
-    zero = after(grid.s, list(swapped.values())) - grid.s
+    zero = after(grid.s, list(swapped.values()) + gates) - grid.s
     pieces[half] = jnp.concatenate(
         [
             grid.ring_step(lax.dynamic_slice_in_dim(ahead, zero, cut), 1),
@@ -560,9 +560,8 @@
         over_seq=over_seq,
         gates=arrivals[:early] + [own_swap, two[0]],
     )
-    turn = grid.s
-    for j in range(1, early + 1):
-        weights.swap(j)
+    early_swaps = [weights.swap(j) for j in range(1, early + 1)]
+    turn = after(grid.s, early_swaps[:1])
     next_row = grid.seq_shift(latent[:1], -1)
     latent_next = lax.dynamic_slice_in_dim(
         jnp.concatenate([latent, next_row]), grid.h * sub + 1, sub
@@ -586,16 +585,18 @@
         stream_in = jnp.dot(own_rows, w_in, preferred_element_type=F32) + embedding
         zero = 0
         if step_index == 0:
-            swaps = [weights.swapped[j] for j in range(1, early + 1)]
-            zero = after(grid.s, arrivals[early:] + swaps[:1]) - grid.s
-            for j in range(early + 1, grid.outer):
-                weights.swap(j)
+            zero = after(grid.s, arrivals[early:] + early_swaps[1:]) - grid.s
+            late_swaps = [weights.swap(j) for j in range(early + 1, grid.outer)]
         stream_attn = stream_in + reduce_head(
             grid,
             jnp.dot(attended, w_attn_out, preferred_element_type=F32).astype(BF16),
             zero,
         )
-        pieces, swapped = gather_ring(grid, layer_norm(stream_attn, gain_mlp).astype(BF16))
+        pieces, swapped = gather_ring(
+            grid,
+            layer_norm(stream_attn, gain_mlp).astype(BF16),
+            late_swaps if step_index == 0 else [],
+        )
         if step_index == 0:
             parts = weights.parts()
         order = sorted(pieces)

time: 542 us -> 530 us (0.978)
  waiting for transfers between devices: 220 us -> 207 us
    ppermute x101, waiting for transfers between devices: 220 us -> 207 us  [move(): return lax.ppermute(value, ('seq', 'head'), route)]
  transfers between devices with their start and end apart: 101 -> 101, of which waited for: 45 -> 44; matrix products, arithmetic and copies ran while one was open for 9% -> 10% of each run, Pallas kernels for 10% -> 11%
where the time goes in v5:
time: 530 us; the launch traced here: 525 us
  waiting for transfers between devices  207 us (39%)
  Pallas kernels  127 us (24%)
  starting transfers between devices  102 us (19%)
  local copies, waits for them, and re-layouts  32.9 us (6%)
  other arithmetic  26.7 us (5%)
  between operations  15.2 us (3%)
  matrix products  14.5 us (3%)
    ppermute x101, waiting for transfers between devices, move(): return lax.ppermute(value, ('seq', 'head'), route)  207 us
    ppermute x101, starting transfers between devices, move(): return lax.ppermute(value, ('seq', 'head'), route)  102 us
    pallas_call x2, Pallas kernels, embed_products(): pl.pallas_call(functools.partial(embed_kernel, count, with_query), grid_s...  48.9 us
    pallas_call x2, Pallas kernels, mlp(): pl.pallas_call(functools.partial(mlp_kernel, count, len(parts), max(1, ML...  39.7 us
    pallas_call x2, Pallas kernels, attend(): pl.pallas_call(functools.partial(attend_kernel, width, HEAD_DIM ** (-0.5)...  25.5 us
  transfers between devices with their start and end apart: 101, of which 44 were waited for; matrix products, arithmetic and copies ran while one was open for 10% of the time, Pallas kernels for 11%

profile of v5, /device:TPU:0, one launch (start us, length us, event | category | flops | bytes accessed | tf_op | source)
XLA Modules:
  0.0 525.1 jit_solution(15687269946737719866)
XLA Ops:
  0.9 6.0 %collective-permute-start.3 = (bf16[64,128]{1,0:T(8,128)(2,1)S(1)}, bf16[64,128]{1,0:T(8,128)(2,1)S(1)}, u32[]{:S(2)}, u32[]{:S(2)}) collective-permute-start(bf16[64,128]{1,0:T(8,128)(2,1)S(1)} %dynamic-slice_convert_fusion.2.refs_0_), channel_id=1, source_target_pairs={{0,28},{1,29},{2,30},{3,31},{4,0},{5,1},{6,2},{7,3},{8,4},{9,5},{1... | collective-permute-start | bytes 49160 | tf_op jit(solution)/shard_map/ppermute | solution.py:48
  7.3 3.0 collective-permute-start.6
  10.4 2.4 multiply_cosine_fusion
  17.8 2.3 multiply_subtract_fusion.size_ref
  20.0 2.7 constant_dynamic-slice_fusion.6
  40.4 22.4 %embed_products.2 = (bf16[1024,768]{1,0:T(8,128)(2,1)}, bf16[1024,768]{1,0:T(8,128)(2,1)}, f32[1024,128]{1,0:T(8,128)}, bf16[128,768]{1,0:T(8,128)(2,1)}, bf16[128,768]{1,0:T(8,128)(2,1)}) custom-call(s32[4]{0:T(128)} %pad_add_fusion.1.ids_ref, bf16[128,3072]{1,0:T(8,128)(2,1)} %refs_0_.3, f32[1,3072]{1,0:T(1,128)} %bitcast.114, ...), custom_call_target="tpu_custom_call" | custom-call | flops 38654705664 | bytes 14155776 | tf_op jit(solution)/shard_map/embed_products/pallas_call | solution.py:341
  67.1 15.1 %collective-permute-done.refs_0_.refs_18_ = bf16[384,1536]{1,0:T(8,128)(2,1)} collective-permute-done((bf16[384,1536]{1,0:T(8,128)(2,1)}, bf16[384,1536]{1,0:T(8,128)(2,1)}, u32[]{:S(2)}, u32[]{:S(2)}) %collective-permute-start) | collective-permute-done | bytes 1179680 | tf_op jit(solution)/shard_map/ppermute | solution.py:48
  83.7 26.5 %embed_products.3 = (bf16[1024,768]{1,0:T(8,128)(2,1)}, bf16[1024,768]{1,0:T(8,128)(2,1)}, f32[1024,128]{1,0:T(8,128)}, bf16[256,768]{1,0:T(8,128)(2,1)}, bf16[128,768]{1,0:T(8,128)(2,1)}) custom-call(s32[4]{0:T(128)} %pad_add_fusion.2.ids_ref, bf16[128,3072]{1,0:T(8,128)(2,1)} %refs_0_.3, f32[1,3072]{1,0:T(1,128)} %bitcast.115, ...), custom_call_target="tpu_custom_call" | custom-call | flops 38654705664 | bytes 14155776 | tf_op jit(solution)/shard_map/embed_products/pallas_call | solution.py:341
  121.1 3.7 collective-permute-done.10.refs_1_
  131.6 13.1 %attend.2 = bf16[256,768]{1,0:T(8,128)(2,1)} custom-call(s32[1]{0:T(128)} %after.10.index_ref, bf16[2048,128]{1,0:T(8,128)(2,1)} %place.6.cur_ref, bf16[128,256]{1,0:T(8,128)(2,1)} %pad_maximum_fusion.9.gram_ref, f32[2048,1]{1,0:T(8,128)} %multiply_subtract_fusion.size_ref, bf16[256,768]{1,0:T(8,128)(2,1)} %get-tuple-element.51.eq_ref, ...), custom_call_target="tpu_custom_call" | custom-call | flops 6442450944 | bytes 6291456 | tf_op jit(solution)/shard_map/attend/pallas_call | solution.py:439
  144.7 3.9 convolution_convert_fusion.1
  151.5 2.6 collective-permute-start.16
  163.8 18.4 %collective-permute-done.16.refs_0_.refs_22_ = bf16[384,1536]{1,0:T(8,128)(2,1)} collective-permute-done((bf16[384,1536]{1,0:T(8,128)(2,1)}, bf16[384,1536]{1,0:T(8,128)(2,1)}, u32[]{:S(2)}, u32[]{:S(2)}) %collective-permute-start.16) | collective-permute-done | bytes 1179680 | tf_op jit(solution)/shard_map/ppermute | solution.py:48
  182.6 5.2 collective-permute-done.17.refs_1_.refs_21_
  191.2 17.7 %collective-permute-start.19 = (bf16[64,3072]{1,0:T(8,128)(2,1)S(1)}, bf16[64,3072]{1,0:T(8,128)(2,1)S(1)}, u32[]{:S(2)}, u32[]{:S(2)}) collective-permute-start(bf16[64,3072]{1,0:T(8,128)(2,1)S(1)} %multiply_convert_fusion.3.refs_11_), channel_id=1, source_target_pairs={{0,8},{1,9},{2,0},{3,1},{4,12},{5,13},{6,4},{7,5},{8,16},{9,17},{1... | collective-permute-start | bytes 1179656 | tf_op jit(solution)/shard_map/ppermute | solution.py:48
  209.0 8.0 %collective-permute-done.19.refs_10_ = bf16[64,3072]{1,0:T(8,128)(2,1)S(1)} collective-permute-done((bf16[64,3072]{1,0:T(8,128)(2,1)S(1)}, bf16[64,3072]{1,0:T(8,128)(2,1)S(1)}, u32[]{:S(2)}, u32[]{:S(2)}) %collective-permute-start.19) | collective-permute-done | bytes 393248 | tf_op jit(solution)/shard_map/ppermute | solution.py:48
  217.0 2.5 collective-permute-start.20
  220.1 7.3 %collective-permute-done.20.refs_9_ = bf16[64,3072]{1,0:T(8,128)(2,1)} collective-permute-done((bf16[64,3072]{1,0:T(8,128)(2,1)S(1)}, bf16[64,3072]{1,0:T(8,128)(2,1)}, u32[]{:S(2)}, u32[]{:S(2)}) %collective-permute-start.20) | collective-permute-done | bytes 393248 | tf_op jit(solution)/shard_map/ppermute | solution.py:48
  227.4 5.5 %collective-permute-start.21 = (bf16[64,3072]{1,0:T(8,128)(2,1)}, bf16[64,3072]{1,0:T(8,128)(2,1)}, u32[]{:S(2)}, u32[]{:S(2)}) collective-permute-start(bf16[64,3072]{1,0:T(8,128)(2,1)} %collective-permute-done.20.refs_9_), channel_id=1, source_target_pairs={{0,8},{1,9},{2,0},{3,1},{4,12},{5,13},{6,4},{7,5},{8,16},{9,17},{1... | collective-permute-start | bytes 1179656 | tf_op jit(solution)/shard_map/ppermute | solution.py:48
  236.3 6.1 %collective-permute-done.21.refs_8_ = bf16[64,3072]{1,0:T(8,128)(2,1)} collective-permute-done((bf16[64,3072]{1,0:T(8,128)(2,1)}, bf16[64,3072]{1,0:T(8,128)(2,1)}, u32[]{:S(2)}, u32[]{:S(2)}) %collective-permute-start.21) | collective-permute-done | bytes 393248 | tf_op jit(solution)/shard_map/ppermute | solution.py:48
  243.3 2.5 collective-permute-start.33
  247.2 3.4 collective-permute-done.33
  256.1 19.9 %mlp.2 = (bf16[64,3072]{1,0:T(8,128)(2,1)}, bf16[64,3072]{1,0:T(8,128)(2,1)}, bf16[64,3072]{1,0:T(8,128)(2,1)}, bf16[64,3072]{1,0:T(8,128)(2,1)}, bf16[64,3072]{...) custom-call(s32[8]{0:T(128)} %stack.316.places, ...), custom_call_target="tpu_custom_call" | custom-call | flops 19327352832 | bytes 9437184 | tf_op jit(solution)/shard_map/mlp/pallas_call | solution.py:507
  280.7 6.5 %collective-permute-done.48 = bf16[32,3072]{1,0:T(8,128)(2,1)S(1)} collective-permute-done((bf16[32,3072]{1,0:T(8,128)(2,1)S(1)}, bf16[32,3072]{1,0:T(8,128)(2,1)S(1)}, u32[]{:S(2)}, u32[]{:S(2)}) %collective-permute-start.48) | collective-permute-done | bytes 196640 | tf_op jit(solution)/shard_map/ppermute | solution.py:48
  289.0 4.3 collective-permute-done.41
  293.8 8.9 %collective-permute-done.49 = bf16[64,3072]{1,0:T(8,128)(2,1)S(1)} collective-permute-done((bf16[64,3072]{1,0:T(8,128)(2,1)S(1)}, bf16[64,3072]{1,0:T(8,128)(2,1)S(1)}, u32[]{:S(2)}, u32[]{:S(2)}) %collective-permute-start.49) | collective-permute-done | bytes 393248 | tf_op jit(solution)/shard_map/ppermute | solution.py:48
  305.4 6.4 %collective-permute-done.42 = bf16[64,3072]{1,0:T(8,128)(2,1)S(1)} collective-permute-done((bf16[64,3072]{1,0:T(8,128)(2,1)S(1)}, bf16[64,3072]{1,0:T(8,128)(2,1)S(1)}, u32[]{:S(2)}, u32[]{:S(2)}) %collective-permute-start.42) | collective-permute-done | bytes 393248 | tf_op jit(solution)/shard_map/ppermute | solution.py:48
  315.0 5.5 %collective-permute-done.43 = bf16[64,3072]{1,0:T(8,128)(2,1)S(1)} collective-permute-done((bf16[64,3072]{1,0:T(8,128)(2,1)S(1)}, bf16[64,3072]{1,0:T(8,128)(2,1)S(1)}, u32[]{:S(2)}, u32[]{:S(2)}) %collective-permute-start.43) | collective-permute-done | bytes 393248 | tf_op jit(solution)/shard_map/ppermute | solution.py:48
  326.5 3.0 collective-permute-done.44
  332.2 2.2 collective-permute-start.52
  344.7 2.8 collective-permute-done.58.refs_7_
  350.1 4.7 collective-permute-done.59.refs_1_
  359.6 12.3 %attend.3 = bf16[256,768]{1,0:T(8,128)(2,1)} custom-call(s32[1]{0:T(128)} %bitcast.36.value_ref.index_ref, bf16[2048,128]{1,0:T(8,128)(2,1)} %place.8.cur_ref, bf16[128,256]{1,0:T(8,128)(2,1)} %pad_maximum_fusion.9.gram_ref, f32[2048,1]{1,0:T(8,128)} %multiply_subtract_fusion.size_ref, bf16[256,768]{1,0:T(8,128)(2,1)} %get-tuple-element.51.eq_ref, ...), custom_call_target="tpu_custom_call" | custom-call | flops 6442450944 | bytes 6291456 | tf_op jit(solution)/shard_map/attend/pallas_call | solution.py:439
  371.9 3.9 convolution_convert_fusion
  380.3 11.0 %collective-permute-done.63 = bf16[64,3072]{1,0:T(8,128)(2,1)} collective-permute-done((bf16[64,3072]{1,0:T(8,128)(2,1)S(1)}, bf16[64,3072]{1,0:T(8,128)(2,1)}, u32[]{:S(2)}, u32[]{:S(2)}) %collective-permute-start.63) | collective-permute-done | bytes 393248 | tf_op jit(solution)/shard_map/ppermute | solution.py:48
  395.6 8.5 %collective-permute-done.64.refs_10_ = bf16[64,3072]{1,0:T(8,128)(2,1)S(1)} collective-permute-done((bf16[64,3072]{1,0:T(8,128)(2,1)S(1)}, bf16[64,3072]{1,0:T(8,128)(2,1)S(1)}, u32[]{:S(2)}, u32[]{:S(2)}) %collective-permute-start.64) | collective-permute-done | bytes 393248 | tf_op jit(solution)/shard_map/ppermute | solution.py:48
  406.7 7.2 %collective-permute-done.65.refs_9_ = bf16[64,3072]{1,0:T(8,128)(2,1)} collective-permute-done((bf16[64,3072]{1,0:T(8,128)(2,1)S(1)}, bf16[64,3072]{1,0:T(8,128)(2,1)}, u32[]{:S(2)}, u32[]{:S(2)}) %collective-permute-start.65) | collective-permute-done | bytes 393248 | tf_op jit(solution)/shard_map/ppermute | solution.py:48
  418.6 4.4 collective-permute-done.66.refs_8_
  427.2 2.4 collective-permute-done.77
  434.4 19.9 %mlp.3 = (bf16[64,3072]{1,0:T(8,128)(2,1)}, bf16[64,3072]{1,0:T(8,128)(2,1)}, bf16[64,3072]{1,0:T(8,128)(2,1)}, bf16[64,3072]{1,0:T(8,128)(2,1)}, bf16[64,3072]{...) custom-call(s32[8]{0:T(128)} %stack.316.places, ...), custom_call_target="tpu_custom_call" | custom-call | flops 19327352832 | bytes 9437184 | tf_op jit(solution)/shard_map/mlp/pallas_call | solution.py:507
  459.7 5.7 %collective-permute-done.92 = bf16[32,3072]{1,0:T(8,128)(2,1)S(1)} collective-permute-done((bf16[32,3072]{1,0:T(8,128)(2,1)S(1)}, bf16[32,3072]{1,0:T(8,128)(2,1)S(1)}, u32[]{:S(2)}, u32[]{:S(2)}) %collective-permute-start.92) | collective-permute-done | bytes 196640 | tf_op jit(solution)/shard_map/ppermute | solution.py:48
  465.8 5.8 %collective-permute-done.85 = bf16[32,3072]{1,0:T(8,128)(2,1)S(1)} collective-permute-done((bf16[32,3072]{1,0:T(8,128)(2,1)S(1)}, bf16[32,3072]{1,0:T(8,128)(2,1)S(1)}, u32[]{:S(2)}, u32[]{:S(2)}) %collective-permute-start.85) | collective-permute-done | bytes 196640 | tf_op jit(solution)/shard_map/ppermute | solution.py:48
  472.8 8.1 %collective-permute-done.93 = bf16[64,3072]{1,0:T(8,128)(2,1)S(1)} collective-permute-done((bf16[64,3072]{1,0:T(8,128)(2,1)S(1)}, bf16[64,3072]{1,0:T(8,128)(2,1)S(1)}, u32[]{:S(2)}, u32[]{:S(2)}) %collective-permute-start.93) | collective-permute-done | bytes 393248 | tf_op jit(solution)/shard_map/ppermute | solution.py:48
  483.2 6.8 %collective-permute-done.86 = bf16[64,3072]{1,0:T(8,128)(2,1)S(1)} collective-permute-done((bf16[64,3072]{1,0:T(8,128)(2,1)S(1)}, bf16[64,3072]{1,0:T(8,128)(2,1)S(1)}, u32[]{:S(2)}, u32[]{:S(2)}) %collective-permute-start.86) | collective-permute-done | bytes 393248 | tf_op jit(solution)/shard_map/ppermute | solution.py:48
  492.5 7.2 %collective-permute-done.87 = bf16[64,3072]{1,0:T(8,128)(2,1)S(1)} collective-permute-done((bf16[64,3072]{1,0:T(8,128)(2,1)S(1)}, bf16[64,3072]{1,0:T(8,128)(2,1)S(1)}, u32[]{:S(2)}, u32[]{:S(2)}) %collective-permute-start.87) | collective-permute-done | bytes 393248 | tf_op jit(solution)/shard_map/ppermute | solution.py:48
  500.2 7.5 %collective-permute-done.88 = bf16[64,3072]{1,0:T(8,128)(2,1)S(1)} collective-permute-done((bf16[64,3072]{1,0:T(8,128)(2,1)S(1)}, bf16[64,3072]{1,0:T(8,128)(2,1)S(1)}, u32[]{:S(2)}, u32[]{:S(2)}) %collective-permute-start.88) | collective-permute-done | bytes 393248 | tf_op jit(solution)/shard_map/ppermute | solution.py:48
  511.3 5.3 %collective-permute-done.96 = f32[1,128]{1,0:T(1,128)S(1)} collective-permute-done((f32[1,128]{1,0:T(1,128)S(1)}, f32[1,128]{1,0:T(1,128)S(1)}, u32[]{:S(2)}, u32[]{:S(2)}) %collective-permute-start.96) | collective-permute-done | bytes 544 | tf_op jit(solution)/shard_map/ppermute | solution.py:48
  519.3 2.3 collective-permute-done.98.refs_1_
  (425 shorter events, 147.2 us)
Async XLA Ops:
  0.9 26.2 %collective-permute-start.3 = (bf16[64,128]{1,0:T(8,128)(2,1)S(1)}, bf16[64,128]{1,0:T(8,128)(2,1)S(1)}, u32[]{:S(2)}, u32[]{:S(2)}) collective-permute-start(bf16[64,128]{1,0:T(8,128)(2,1)S(1)} %dynamic-slice_convert_fusion.2.refs_0_), channel_id=1, source_target_pairs={{0,28},{1,29},{2,30},{3,31},{4,0},{5,1},{6,2},{7,3},{8,4},{9,5},{1... | collective-permute-start | bytes 49160 | tf_op jit(solution)/shard_map/ppermute | solution.py:48
  6.9 22.1 %collective-permute-start.4 = (bf16[64,128]{1,0:T(8,128)(2,1)S(1)}, bf16[64,128]{1,0:T(8,128)(2,1)S(1)}, u32[]{:S(2)}, u32[]{:S(2)}) collective-permute-start(bf16[64,128]{1,0:T(8,128)(2,1)S(1)} %dynamic-slice_convert_fusion.2.refs_0_), channel_id=1, source_target_pairs={{0,24},{1,25},{2,26},{3,27},{4,28},{5,29},{6,30},{7,31},{8,0},{9,1... | collective-permute-start | bytes 49160 | tf_op jit(solution)/shard_map/ppermute | solution.py:48
  7.3 23.3 %collective-permute-start.5 = (bf16[64,128]{1,0:T(8,128)(2,1)S(1)}, bf16[64,128]{1,0:T(8,128)(2,1)S(1)}, u32[]{:S(2)}, u32[]{:S(2)}) collective-permute-start(bf16[64,128]{1,0:T(8,128)(2,1)S(1)} %dynamic-slice_convert_fusion.2.refs_0_), channel_id=1, source_target_pairs={{0,20},{1,21},{2,22},{3,23},{4,24},{5,25},{6,26},{7,27},{8,28},{9,... | collective-permute-start | bytes 49160 | tf_op jit(solution)/shard_map/ppermute | solution.py:48
  7.3 25.4 %collective-permute-start.6 = (bf16[64,128]{1,0:T(8,128)(2,1)S(1)}, bf16[64,128]{1,0:T(8,128)(2,1)S(1)}, u32[]{:S(2)}, u32[]{:S(2)}) collective-permute-start(bf16[64,128]{1,0:T(8,128)(2,1)S(1)} %dynamic-slice_convert_fusion.2.refs_0_), channel_id=1, source_target_pairs={{0,16},{1,17},{2,18},{3,19},{4,20},{5,21},{6,22},{7,23},{8,24},{9,... | collective-permute-start | bytes 49160 | tf_op jit(solution)/shard_map/ppermute | solution.py:48
  10.3 23.3 %collective-permute-start.7 = (bf16[64,128]{1,0:T(8,128)(2,1)S(1)}, bf16[64,128]{1,0:T(8,128)(2,1)S(1)}, u32[]{:S(2)}, u32[]{:S(2)}) collective-permute-start(bf16[64,128]{1,0:T(8,128)(2,1)S(1)} %dynamic-slice_convert_fusion.2.refs_0_), channel_id=1, source_target_pairs={{0,12},{1,13},{2,14},{3,15},{4,16},{5,17},{6,18},{7,19},{8,20},{9,... | collective-permute-start | bytes 49160 | tf_op jit(solution)/shard_map/ppermute | solution.py:48
  30.6 51.6 %collective-permute-start = (bf16[384,1536]{1,0:T(8,128)(2,1)}, bf16[384,1536]{1,0:T(8,128)(2,1)}, u32[]{:S(2)}, u32[]{:S(2)}) collective-permute-start(bf16[384,1536]{1,0:T(8,128)(2,1)} %pad_maximum_fusion), channel_id=1, source_target_pairs={{0,8},{1,9},{2,10},{3,11},{4,12},{5,13},{6,14},{7,15},{8,0},{9,1},... | collective-permute-start | bytes 3538952 | tf_op jit(solution)/shard_map/ppermute | solution.py:48
  32.7 77.6 %collective-permute-start.1 = (bf16[384,1536]{1,0:T(8,128)(2,1)}, bf16[384,1536]{1,0:T(8,128)(2,1)}, u32[]{:S(2)}, u32[]{:S(2)}) collective-permute-start(bf16[384,1536]{1,0:T(8,128)(2,1)} %pad_maximum_fusion.1), channel_id=1, source_target_pairs={{0,16},{1,17},{2,18},{3,19},{4,20},{5,21},{6,22},{7,23},{8,24},{9,... | collective-permute-start | bytes 3538952 | tf_op jit(solution)/shard_map/ppermute | solution.py:48
  33.6 76.6 %collective-permute-start.2 = (bf16[384,1536]{1,0:T(8,128)(2,1)}, bf16[384,1536]{1,0:T(8,128)(2,1)}, u32[]{:S(2)}, u32[]{:S(2)}) collective-permute-start(bf16[384,1536]{1,0:T(8,128)(2,1)} %pad_maximum_fusion.2.refs_16_), channel_id=1, source_target_pairs={{0,4},{1,5},{2,6},{3,7},{4,0},{5,1},{6,2},{7,3},{8,12},{9,13},{10,... | collective-permute-start | bytes 3538952 | tf_op jit(solution)/shard_map/ppermute | solution.py:48
  82.2 48.9 %collective-permute-start.14 = (bf16[384,1536]{1,0:T(8,128)(2,1)}, bf16[384,1536]{1,0:T(8,128)(2,1)}, u32[]{:S(2)}, u32[]{:S(2)}) collective-permute-start(bf16[384,1536]{1,0:T(8,128)(2,1)} %collective-permute-done.refs_0_.refs_18_), channel_id=1, source_target_pairs={{0,4},{1,5},{2,6},{3,7},{4,0},{5,1},{6,2},{7,3},{8,12},{9,13},{10,... | collective-permute-start | bytes 3538952 | tf_op jit(solution)/shard_map/ppermute | solution.py:48
  151.5 30.6 %collective-permute-start.16 = (bf16[384,1536]{1,0:T(8,128)(2,1)}, bf16[384,1536]{1,0:T(8,128)(2,1)}, u32[]{:S(2)}, u32[]{:S(2)}) collective-permute-start(bf16[384,1536]{1,0:T(8,128)(2,1)} %pad_maximum_fusion.3), channel_id=1, source_target_pairs={{0,24},{1,25},{2,26},{3,27},{4,28},{5,29},{6,30},{7,31},{8,16},{9,... | collective-permute-start | bytes 3538952 | tf_op jit(solution)/shard_map/ppermute | solution.py:48
  158.6 29.2 %collective-permute-start.17 = (bf16[384,1536]{1,0:T(8,128)(2,1)}, bf16[384,1536]{1,0:T(8,128)(2,1)}, u32[]{:S(2)}, u32[]{:S(2)}) collective-permute-start(bf16[384,1536]{1,0:T(8,128)(2,1)} %collective-permute-done.1.refs_1_.refs_20_), channel_id=1, source_target_pairs={{0,4},{1,5},{2,6},{3,7},{4,0},{5,1},{6,2},{7,3},{8,12},{9,13},{10,... | collective-permute-start | bytes 3538952 | tf_op jit(solution)/shard_map/ppermute | solution.py:48
  161.3 27.7 %collective-permute-start.18 = (bf16[64,3072]{1,0:T(8,128)(2,1)}, bf16[64,3072]{1,0:T(8,128)(2,1)}, u32[]{:S(2)}, u32[]{:S(2)}) collective-permute-start(bf16[64,3072]{1,0:T(8,128)(2,1)} %fusion.9), channel_id=1, source_target_pairs={{0,2},{1,3},{2,0},{3,1},{4,6},{5,7},{6,4},{7,5},{8,10},{9,11},{10,... | collective-permute-start | bytes 1179656 | tf_op jit(solution)/shard_map/ppermute | solution.py:48
  182.1 37.9 %collective-permute-start.32 = (bf16[384,1536]{1,0:T(8,128)(2,1)}, bf16[384,1536]{1,0:T(8,128)(2,1)}, u32[]{:S(2)}, u32[]{:S(2)}) collective-permute-start(bf16[384,1536]{1,0:T(8,128)(2,1)} %collective-permute-done.16.refs_0_.refs_22_), channel_id=1, source_target_pairs={{0,4},{1,5},{2,6},{3,7},{4,0},{5,1},{6,2},{7,3},{8,12},{9,13},{10,... | collective-permute-start | bytes 3538952 | tf_op jit(solution)/shard_map/ppermute | solution.py:48
  191.2 25.7 %collective-permute-start.19 = (bf16[64,3072]{1,0:T(8,128)(2,1)S(1)}, bf16[64,3072]{1,0:T(8,128)(2,1)S(1)}, u32[]{:S(2)}, u32[]{:S(2)}) collective-permute-start(bf16[64,3072]{1,0:T(8,128)(2,1)S(1)} %multiply_convert_fusion.3.refs_11_), channel_id=1, source_target_pairs={{0,8},{1,9},{2,0},{3,1},{4,12},{5,13},{6,4},{7,5},{8,16},{9,17},{1... | collective-permute-start | bytes 1179656 | tf_op jit(solution)/shard_map/ppermute | solution.py:48
  209.0 10.5 %collective-permute-start.26 = (bf16[64,3072]{1,0:T(8,128)(2,1)S(1)}, bf16[64,3072]{1,0:T(8,128)(2,1)S(1)}, u32[]{:S(2)}, u32[]{:S(2)}) collective-permute-start(bf16[64,3072]{1,0:T(8,128)(2,1)S(1)} %multiply_convert_fusion.3.refs_11_), channel_id=1, source_target_pairs={{0,2},{1,3},{2,10},{3,11},{4,6},{5,7},{6,14},{7,15},{8,0},{9,1},{1... | collective-permute-start | bytes 1179656 | tf_op jit(solution)/shard_map/ppermute | solution.py:48
  217.0 10.5 %collective-permute-start.20 = (bf16[64,3072]{1,0:T(8,128)(2,1)S(1)}, bf16[64,3072]{1,0:T(8,128)(2,1)}, u32[]{:S(2)}, u32[]{:S(2)}) collective-permute-start(bf16[64,3072]{1,0:T(8,128)(2,1)S(1)} %collective-permute-done.19.refs_10_), channel_id=1, source_target_pairs={{0,8},{1,9},{2,0},{3,1},{4,12},{5,13},{6,4},{7,5},{8,16},{9,17},{1... | collective-permute-start | bytes 1179656 | tf_op jit(solution)/shard_map/ppermute | solution.py:48
  219.5 13.5 %collective-permute-start.28 = (bf16[64,3072]{1,0:T(8,128)(2,1)S(1)}, bf16[64,3072]{1,0:T(8,128)(2,1)}, u32[]{:S(2)}, u32[]{:S(2)}) collective-permute-start(bf16[64,3072]{1,0:T(8,128)(2,1)S(1)} %collective-permute-done.26.refs_12_), channel_id=1, source_target_pairs={{0,2},{1,3},{2,10},{3,11},{4,6},{5,7},{6,14},{7,15},{8,0},{9,1},{1... | collective-permute-start | bytes 1179656 | tf_op jit(solution)/shard_map/ppermute | solution.py:48
  219.5 13.5 %collective-permute-start.25 = (bf16[64,3072]{1,0:T(8,128)(2,1)S(1)}, bf16[64,3072]{1,0:T(8,128)(2,1)S(1)}, u32[]{:S(2)}, u32[]{:S(2)}) collective-permute-start(bf16[64,3072]{1,0:T(8,128)(2,1)S(1)} %multiply_convert_fusion.3.refs_11_), channel_id=1, source_target_pairs={{0,1},{1,0},{2,3},{3,2},{4,5},{5,4},{6,7},{7,6},{8,9},{9,8},{10,11... | collective-permute-start | bytes 1179656 | tf_op jit(solution)/shard_map/ppermute | solution.py:48
  219.6 14.2 %collective-permute-start.24 = (bf16[64,3072]{1,0:T(8,128)(2,1)S(1)}, bf16[64,3072]{1,0:T(8,128)(2,1)S(1)}, u32[]{:S(2)}, u32[]{:S(2)}) collective-permute-start(bf16[64,3072]{1,0:T(8,128)(2,1)S(1)} %collective-permute-done.19.refs_10_), channel_id=1, source_target_pairs={{0,1},{1,0},{2,3},{3,2},{4,5},{5,4},{6,7},{7,6},{8,9},{9,8},{10,11... | collective-permute-start | bytes 1179656 | tf_op jit(solution)/shard_map/ppermute | solution.py:48
  220.1 14.4 %collective-permute-start.27 = (bf16[64,3072]{1,0:T(8,128)(2,1)S(1)}, bf16[64,3072]{1,0:T(8,128)(2,1)}, u32[]{:S(2)}, u32[]{:S(2)}) collective-permute-start(bf16[64,3072]{1,0:T(8,128)(2,1)S(1)} %collective-permute-done.26.refs_12_), channel_id=1, source_target_pairs={{0,1},{1,0},{2,3},{3,2},{4,5},{5,4},{6,7},{7,6},{8,9},{9,8},{10,11... | collective-permute-start | bytes 1179656 | tf_op jit(solution)/shard_map/ppermute | solution.py:48
  227.4 14.9 %collective-permute-start.21 = (bf16[64,3072]{1,0:T(8,128)(2,1)}, bf16[64,3072]{1,0:T(8,128)(2,1)}, u32[]{:S(2)}, u32[]{:S(2)}) collective-permute-start(bf16[64,3072]{1,0:T(8,128)(2,1)} %collective-permute-done.20.refs_9_), channel_id=1, source_target_pairs={{0,8},{1,9},{2,0},{3,1},{4,12},{5,13},{6,4},{7,5},{8,16},{9,17},{1... | collective-permute-start | bytes 1179656 | tf_op jit(solution)/shard_map/ppermute | solution.py:48
  233.0 12.9 %collective-permute-start.30 = (bf16[64,3072]{1,0:T(8,128)(2,1)}, bf16[64,3072]{1,0:T(8,128)(2,1)}, u32[]{:S(2)}, u32[]{:S(2)}) collective-permute-start(bf16[64,3072]{1,0:T(8,128)(2,1)} %collective-permute-done.28.refs_13_), channel_id=1, source_target_pairs={{0,2},{1,3},{2,10},{3,11},{4,6},{5,7},{6,14},{7,15},{8,0},{9,1},{1... | collective-permute-start | bytes 1179656 | tf_op jit(solution)/shard_map/ppermute | solution.py:48
  235.7 19.0 %collective-permute-start.23 = (bf16[64,3072]{1,0:T(8,128)(2,1)}, bf16[64,3072]{1,0:T(8,128)(2,1)}, u32[]{:S(2)}, u32[]{:S(2)}) collective-permute-start(bf16[64,3072]{1,0:T(8,128)(2,1)} %collective-permute-done.20.refs_9_), channel_id=1, source_target_pairs={{0,1},{1,0},{2,3},{3,2},{4,5},{5,4},{6,7},{7,6},{8,9},{9,8},{10,11... | collective-permute-start | bytes 1179656 | tf_op jit(solution)/shard_map/ppermute | solution.py:48
  236.0 18.7 %collective-permute-start.29 = (bf16[64,3072]{1,0:T(8,128)(2,1)}, bf16[64,3072]{1,0:T(8,128)(2,1)}, u32[]{:S(2)}, u32[]{:S(2)}) collective-permute-start(bf16[64,3072]{1,0:T(8,128)(2,1)} %collective-permute-done.28.refs_13_), channel_id=1, source_target_pairs={{0,1},{1,0},{2,3},{3,2},{4,5},{5,4},{6,7},{7,6},{8,9},{9,8},{10,11... | collective-permute-start | bytes 1179656 | tf_op jit(solution)/shard_map/ppermute | solution.py:48
  276.6 17.1 %collective-permute-start.46 = (bf16[64,3072]{1,0:T(8,128)(2,1)}, bf16[64,3072]{1,0:T(8,128)(2,1)S(1)}, u32[]{:S(2)}, u32[]{:S(2)}) collective-permute-start(bf16[64,3072]{1,0:T(8,128)(2,1)} %get-tuple-element.72), channel_id=1, source_target_pairs={{0,1},{1,0},{2,3},{3,2},{4,5},{5,4},{6,7},{7,6},{8,9},{9,8},{10,11... | collective-permute-start | bytes 1179656 | tf_op jit(solution)/shard_map/ppermute | solution.py:48
  276.7 37.0 %collective-permute-start.45 = (bf16[64,3072]{1,0:T(8,128)(2,1)}, bf16[64,3072]{1,0:T(8,128)(2,1)S(1)}, u32[]{:S(2)}, u32[]{:S(2)}) collective-permute-start(bf16[64,3072]{1,0:T(8,128)(2,1)} %get-tuple-element.70), channel_id=1, source_target_pairs={{0,1},{1,0},{2,3},{3,2},{4,5},{5,4},{6,7},{7,6},{8,9},{9,8},{10,11... | collective-permute-start | bytes 1179656 | tf_op jit(solution)/shard_map/ppermute | solution.py:48
  278.0 26.6 %collective-permute-start.38 = (bf16[64,3072]{1,0:T(8,128)(2,1)}, bf16[64,3072]{1,0:T(8,128)(2,1)S(1)}, u32[]{:S(2)}, u32[]{:S(2)}) collective-permute-start(bf16[64,3072]{1,0:T(8,128)(2,1)} %get-tuple-element.64), channel_id=1, source_target_pairs={{0,1},{1,0},{2,3},{3,2},{4,5},{5,4},{6,7},{7,6},{8,9},{9,8},{10,11... | collective-permute-start | bytes 1179656 | tf_op jit(solution)/shard_map/ppermute | solution.py:48
  279.3 35.7 %collective-permute-start.37 = (bf16[64,3072]{1,0:T(8,128)(2,1)S(1)}, bf16[64,3072]{1,0:T(8,128)(2,1)S(1)}, u32[]{:S(2)}, u32[]{:S(2)}) collective-permute-start(bf16[64,3072]{1,0:T(8,128)(2,1)S(1)} %copy-done.69), channel_id=1, source_target_pairs={{0,1},{1,0},{2,3},{3,2},{4,5},{5,4},{6,7},{7,6},{8,9},{9,8},{10,11... | collective-permute-start | bytes 1179656 | tf_op jit(solution)/shard_map/ppermute | solution.py:48
  293.7 32.8 %collective-permute-start.36 = (bf16[64,3072]{1,0:T(8,128)(2,1)}, bf16[64,3072]{1,0:T(8,128)(2,1)}, u32[]{:S(2)}, u32[]{:S(2)}) collective-permute-start(bf16[64,3072]{1,0:T(8,128)(2,1)} %get-tuple-element.60), channel_id=1, source_target_pairs={{0,1},{1,0},{2,3},{3,2},{4,5},{5,4},{6,7},{7,6},{8,9},{9,8},{10,11... | collective-permute-start | bytes 1179656 | tf_op jit(solution)/shard_map/ppermute | solution.py:48
  314.7 11.8 %collective-permute-start.51 = (bf16[64,3072]{1,0:T(8,128)(2,1)}, bf16[64,3072]{1,0:T(8,128)(2,1)}, u32[]{:S(2)}, u32[]{:S(2)}) collective-permute-start(bf16[64,3072]{1,0:T(8,128)(2,1)} %add_convert_fusion.5), channel_id=1, source_target_pairs={{0,2},{1,3},{2,10},{3,11},{4,6},{5,7},{6,14},{7,15},{8,0},{9,1},{1... | collective-permute-start | bytes 1179656 | tf_op jit(solution)/shard_map/ppermute | solution.py:48
  379.7 11.6 %collective-permute-start.63 = (bf16[64,3072]{1,0:T(8,128)(2,1)S(1)}, bf16[64,3072]{1,0:T(8,128)(2,1)}, u32[]{:S(2)}, u32[]{:S(2)}) collective-permute-start(bf16[64,3072]{1,0:T(8,128)(2,1)S(1)} %fusion.10), channel_id=1, source_target_pairs={{0,2},{1,3},{2,0},{3,1},{4,6},{5,7},{6,4},{7,5},{8,10},{9,11},{10,... | collective-permute-start | bytes 1179656 | tf_op jit(solution)/shard_map/ppermute | solution.py:48
  393.5 10.6 %collective-permute-start.64 = (bf16[64,3072]{1,0:T(8,128)(2,1)S(1)}, bf16[64,3072]{1,0:T(8,128)(2,1)S(1)}, u32[]{:S(2)}, u32[]{:S(2)}) collective-permute-start(bf16[64,3072]{1,0:T(8,128)(2,1)S(1)} %multiply_convert_fusion.1.refs_11_), channel_id=1, source_target_pairs={{0,8},{1,9},{2,0},{3,1},{4,12},{5,13},{6,4},{7,5},{8,16},{9,17},{1... | collective-permute-start | bytes 1179656 | tf_op jit(solution)/shard_map/ppermute | solution.py:48
  393.5 10.9 %collective-permute-start.71 = (bf16[64,3072]{1,0:T(8,128)(2,1)S(1)}, bf16[64,3072]{1,0:T(8,128)(2,1)S(1)}, u32[]{:S(2)}, u32[]{:S(2)}) collective-permute-start(bf16[64,3072]{1,0:T(8,128)(2,1)S(1)} %multiply_convert_fusion.1.refs_11_), channel_id=1, source_target_pairs={{0,2},{1,3},{2,10},{3,11},{4,6},{5,7},{6,14},{7,15},{8,0},{9,1},{1... | collective-permute-start | bytes 1179656 | tf_op jit(solution)/shard_map/ppermute | solution.py:48
  404.1 9.8 %collective-permute-start.65 = (bf16[64,3072]{1,0:T(8,128)(2,1)S(1)}, bf16[64,3072]{1,0:T(8,128)(2,1)}, u32[]{:S(2)}, u32[]{:S(2)}) collective-permute-start(bf16[64,3072]{1,0:T(8,128)(2,1)S(1)} %collective-permute-done.64.refs_10_), channel_id=1, source_target_pairs={{0,8},{1,9},{2,0},{3,1},{4,12},{5,13},{6,4},{7,5},{8,16},{9,17},{1... | collective-permute-start | bytes 1179656 | tf_op jit(solution)/shard_map/ppermute | solution.py:48
  404.4 10.1 %collective-permute-start.73 = (bf16[64,3072]{1,0:T(8,128)(2,1)S(1)}, bf16[64,3072]{1,0:T(8,128)(2,1)}, u32[]{:S(2)}, u32[]{:S(2)}) collective-permute-start(bf16[64,3072]{1,0:T(8,128)(2,1)S(1)} %collective-permute-done.71.refs_12_), channel_id=1, source_target_pairs={{0,2},{1,3},{2,10},{3,11},{4,6},{5,7},{6,14},{7,15},{8,0},{9,1},{1... | collective-permute-start | bytes 1179656 | tf_op jit(solution)/shard_map/ppermute | solution.py:48
  406.1 9.8 %collective-permute-start.70 = (bf16[64,3072]{1,0:T(8,128)(2,1)S(1)}, bf16[64,3072]{1,0:T(8,128)(2,1)S(1)}, u32[]{:S(2)}, u32[]{:S(2)}) collective-permute-start(bf16[64,3072]{1,0:T(8,128)(2,1)S(1)} %multiply_convert_fusion.1.refs_11_), channel_id=1, source_target_pairs={{0,1},{1,0},{2,3},{3,2},{4,5},{5,4},{6,7},{7,6},{8,9},{9,8},{10,11... | collective-permute-start | bytes 1179656 | tf_op jit(solution)/shard_map/ppermute | solution.py:48
  406.1 9.8 %collective-permute-start.69 = (bf16[64,3072]{1,0:T(8,128)(2,1)S(1)}, bf16[64,3072]{1,0:T(8,128)(2,1)S(1)}, u32[]{:S(2)}, u32[]{:S(2)}) collective-permute-start(bf16[64,3072]{1,0:T(8,128)(2,1)S(1)} %collective-permute-done.64.refs_10_), channel_id=1, source_target_pairs={{0,1},{1,0},{2,3},{3,2},{4,5},{5,4},{6,7},{7,6},{8,9},{9,8},{10,11... | collective-permute-start | bytes 1179656 | tf_op jit(solution)/shard_map/ppermute | solution.py:48
  414.5 10.4 %collective-permute-start.75 = (bf16[64,3072]{1,0:T(8,128)(2,1)}, bf16[64,3072]{1,0:T(8,128)(2,1)}, u32[]{:S(2)}, u32[]{:S(2)}) collective-permute-start(bf16[64,3072]{1,0:T(8,128)(2,1)} %collective-permute-done.73.refs_13_), channel_id=1, source_target_pairs={{0,2},{1,3},{2,10},{3,11},{4,6},{5,7},{6,14},{7,15},{8,0},{9,1},{1... | collective-permute-start | bytes 1179656 | tf_op jit(solution)/shard_map/ppermute | solution.py:48
  418.0 13.9 %collective-permute-start.68 = (bf16[64,3072]{1,0:T(8,128)(2,1)}, bf16[64,3072]{1,0:T(8,128)(2,1)}, u32[]{:S(2)}, u32[]{:S(2)}) collective-permute-start(bf16[64,3072]{1,0:T(8,128)(2,1)} %collective-permute-done.65.refs_9_), channel_id=1, source_target_pairs={{0,1},{1,0},{2,3},{3,2},{4,5},{5,4},{6,7},{7,6},{8,9},{9,8},{10,11... | collective-permute-start | bytes 1179656 | tf_op jit(solution)/shard_map/ppermute | solution.py:48
  418.1 13.8 %collective-permute-start.74 = (bf16[64,3072]{1,0:T(8,128)(2,1)}, bf16[64,3072]{1,0:T(8,128)(2,1)}, u32[]{:S(2)}, u32[]{:S(2)}) collective-permute-start(bf16[64,3072]{1,0:T(8,128)(2,1)} %collective-permute-done.73.refs_13_), channel_id=1, source_target_pairs={{0,1},{1,0},{2,3},{3,2},{4,5},{5,4},{6,7},{7,6},{8,9},{9,8},{10,11... | collective-permute-start | bytes 1179656 | tf_op jit(solution)/shard_map/ppermute | solution.py:48
  454.8 17.9 %collective-permute-start.90 = (bf16[64,3072]{1,0:T(8,128)(2,1)}, bf16[64,3072]{1,0:T(8,128)(2,1)S(1)}, u32[]{:S(2)}, u32[]{:S(2)}) collective-permute-start(bf16[64,3072]{1,0:T(8,128)(2,1)} %get-tuple-element.88), channel_id=1, source_target_pairs={{0,1},{1,0},{2,3},{3,2},{4,5},{5,4},{6,7},{7,6},{8,9},{9,8},{10,11... | collective-permute-start | bytes 1179656 | tf_op jit(solution)/shard_map/ppermute | solution.py:48
  455.0 35.6 %collective-permute-start.89 = (bf16[64,3072]{1,0:T(8,128)(2,1)}, bf16[64,3072]{1,0:T(8,128)(2,1)S(1)}, u32[]{:S(2)}, u32[]{:S(2)}) collective-permute-start(bf16[64,3072]{1,0:T(8,128)(2,1)} %get-tuple-element.86), channel_id=1, source_target_pairs={{0,1},{1,0},{2,3},{3,2},{4,5},{5,4},{6,7},{7,6},{8,9},{9,8},{10,11... | collective-permute-start | bytes 1179656 | tf_op jit(solution)/shard_map/ppermute | solution.py:48
  456.2 25.2 %collective-permute-start.82 = (bf16[64,3072]{1,0:T(8,128)(2,1)}, bf16[64,3072]{1,0:T(8,128)(2,1)S(1)}, u32[]{:S(2)}, u32[]{:S(2)}) collective-permute-start(bf16[64,3072]{1,0:T(8,128)(2,1)} %get-tuple-element.80), channel_id=1, source_target_pairs={{0,1},{1,0},{2,3},{3,2},{4,5},{5,4},{6,7},{7,6},{8,9},{9,8},{10,11... | collective-permute-start | bytes 1179656 | tf_op jit(solution)/shard_map/ppermute | solution.py:48
  457.5 35.0 %collective-permute-start.81 = (bf16[64,3072]{1,0:T(8,128)(2,1)S(1)}, bf16[64,3072]{1,0:T(8,128)(2,1)S(1)}, u32[]{:S(2)}, u32[]{:S(2)}) collective-permute-start(bf16[64,3072]{1,0:T(8,128)(2,1)S(1)} %copy-done.67), channel_id=1, source_target_pairs={{0,1},{1,0},{2,3},{3,2},{4,5},{5,4},{6,7},{7,6},{8,9},{9,8},{10,11... | collective-permute-start | bytes 1179656 | tf_op jit(solution)/shard_map/ppermute | solution.py:48
  471.6 9.4 %collective-permute-start.93 = (bf16[64,3072]{1,0:T(8,128)(2,1)S(1)}, bf16[64,3072]{1,0:T(8,128)(2,1)S(1)}, u32[]{:S(2)}, u32[]{:S(2)}) collective-permute-start(bf16[64,3072]{1,0:T(8,128)(2,1)S(1)} %pad_maximum_fusion.8), channel_id=1, source_target_pairs={{0,2},{1,3},{2,10},{3,11},{4,6},{5,7},{6,14},{7,15},{8,0},{9,1},{1... | collective-permute-start | bytes 1179656 | tf_op jit(solution)/shard_map/ppermute | solution.py:48
  472.8 27.4 %collective-permute-start.80 = (bf16[64,3072]{1,0:T(8,128)(2,1)S(1)}, bf16[64,3072]{1,0:T(8,128)(2,1)S(1)}, u32[]{:S(2)}, u32[]{:S(2)}) collective-permute-start(bf16[64,3072]{1,0:T(8,128)(2,1)S(1)} %copy-done.66), channel_id=1, source_target_pairs={{0,1},{1,0},{2,3},{3,2},{4,5},{5,4},{6,7},{7,6},{8,9},{9,8},{10,11... | collective-permute-start | bytes 1179656 | tf_op jit(solution)/shard_map/ppermute | solution.py:48
  490.2 9.5 %collective-permute-start.87 = (bf16[64,3072]{1,0:T(8,128)(2,1)S(1)}, bf16[64,3072]{1,0:T(8,128)(2,1)S(1)}, u32[]{:S(2)}, u32[]{:S(2)}) collective-permute-start(bf16[64,3072]{1,0:T(8,128)(2,1)S(1)} %add_convert_fusion.3), channel_id=1, source_target_pairs={{0,8},{1,9},{2,0},{3,1},{4,12},{5,13},{6,4},{7,5},{8,16},{9,17},{1... | collective-permute-start | bytes 1179656 | tf_op jit(solution)/shard_map/ppermute | solution.py:48
  490.7 9.5 %collective-permute-start.95 = (bf16[64,3072]{1,0:T(8,128)(2,1)S(1)}, bf16[64,3072]{1,0:T(8,128)(2,1)S(1)}, u32[]{:S(2)}, u32[]{:S(2)}) collective-permute-start(bf16[64,3072]{1,0:T(8,128)(2,1)S(1)} %add_convert_fusion), channel_id=1, source_target_pairs={{0,2},{1,3},{2,10},{3,11},{4,6},{5,7},{6,14},{7,15},{8,0},{9,1},{1... | collective-permute-start | bytes 1179656 | tf_op jit(solution)/shard_map/ppermute | solution.py:48
  (125 other events, 1099.8 us)
